TPU v7x, 32 devices: a whole 2x2x4 slice. The times are simulated.
32 devices in a mesh: fsdp: 16 (over z, x, core), tensor: 2 (over y).
Axes of the slice: x: 2, y: 2, z: 4, core: 2. Of those that a mesh axis runs over, the one named last changes fastest.
Arguments:
- tokens: bfloat16 [2, 3072, 1536], P(None, 'fsdp'), may hold values from -6 to 6
- norm1_gain: bfloat16 [1536], P('fsdp'), may hold values from 0.5 to 1.5
- query_weight: bfloat16 [1536, 1536], P('fsdp', 'tensor'), may hold values from -0.15625 to 0.15625
- query_bias: bfloat16 [12, 128], P('tensor'), may hold values from -3 to 3
- key_weight: bfloat16 [1536, 256], P('fsdp', 'tensor'), may hold values from -0.15625 to 0.15625
- key_bias: bfloat16 [2, 128], P('tensor'), may hold values from -3 to 3
- value_weight: bfloat16 [1536, 256], P('fsdp', 'tensor'), may hold values from -0.15625 to 0.15625
- value_bias: bfloat16 [2, 128], P('tensor'), may hold values from -3 to 3
- output_weight: bfloat16 [1536, 1536], P('tensor', 'fsdp'), may hold values from -0.625 to 0.625
- norm2_gain: bfloat16 [1536], P('fsdp'), may hold values from 0.5 to 1.5
- gate_weight: bfloat16 [1536, 8960], P('fsdp', 'tensor'), may hold values from -0.15625 to 0.15625
- up_weight: bfloat16 [1536, 8960], P('fsdp', 'tensor'), may hold values from -0.15625 to 0.15625
- down_weight: bfloat16 [8960, 1536], P('tensor', 'fsdp'), may hold values from -0.0625 to 0.0625
- cotangent: bfloat16 [2, 3072, 1536], P(None, 'fsdp'), may hold values from -6 to 6
- segments: int32 [2, 3072], replicated, may hold values from 0 to 107, as said below
- positions: int32 [2, 3072], replicated, may hold values from 0 to 799, as said below
Outputs:
- output: bfloat16 [2, 3072, 1536], P(None, 'fsdp')
- input_grad: float32 [2, 3072, 1536], P(None, 'fsdp')
- norm1_gain_grad: float32 [1536], P('fsdp')
- query_weight_grad: float32 [1536, 1536], P('fsdp', 'tensor')
- query_bias_grad: float32 [12, 128], P('tensor')
- key_weight_grad: float32 [1536, 256], P('fsdp', 'tensor')
- key_bias_grad: float32 [2, 128], P('tensor')
- value_weight_grad: float32 [1536, 256], P('fsdp', 'tensor')
- value_bias_grad: float32 [2, 128], P('tensor')
- output_weight_grad: float32 [1536, 1536], P('tensor', 'fsdp')
- norm2_gain_grad: float32 [1536], P('fsdp')
- gate_weight_grad: float32 [1536, 8960], P('fsdp', 'tensor')
- up_weight_grad: float32 [1536, 8960], P('fsdp', 'tensor')
- down_weight_grad: float32 [8960, 1536], P('tensor', 'fsdp')
Inputs may be any that keep to these rules, and one draw needn't show every extreme that they name: `segments`: along each micro-batch the numbers never fall; each number marks one document of consecutive tokens inside one sequence of 1024 tokens (sequences start at multiples of 1024); a document has at most 800 tokens, and some document has exactly 800; the documents of sequence j have numbers from j * (18) to (j + 1) * 18 - 1, the last document of each sequence the highest of these. `positions`: the position of each token within its document, counted from 0.
All inputs are finite; a program needn't handle non-finite values.
Results may differ from a plain program's by a relative error of at most 0.02.
Values may be sent and summed in bfloat16 or wider, within the bound.
A program may use at most 160 MiB of HBM per device.

v0:
```python
import math

import jax
import jax.numpy as jnp
from jax import lax
from jax.sharding import PartitionSpec as P

BACK = 5


EPSILON = 1e-06
THETA = 1000000.0
NEGATIVE = -1e30


def shifted(value, axis, steps):
    count = lax.axis_size(axis)
    first, last = (max(0, -steps), min(count, count - steps))
    return lax.ppermute(value, axis, [(source, source + steps) for source in range(first, last)])


def matmul(left_side, right_side):
    return jnp.dot(left_side, right_side, preferred_element_type=jnp.float32)


def contract_rows(left_side, right_side):
    return lax.dot_general(
        left_side, right_side, (((0,), (0,)), ((), ())), preferred_element_type=jnp.float32
    )


def times_transpose(left_side, right_side):
    return lax.dot_general(
        left_side, right_side, (((1,), (1,)), ((), ())), preferred_element_type=jnp.float32
    )


def rotation(places, width):
    half_width = width // 2
    frequency = THETA ** (-(jnp.arange(half_width, dtype=jnp.float32) * 2.0) / width)
    angles = places.astype(jnp.float32)[:, None] * frequency[None, :]
    cosine = jnp.concatenate([jnp.cos(angles), jnp.cos(angles)], axis=-1)[:, None, :]
    sine_table = jnp.concatenate([jnp.sin(angles), jnp.sin(angles)], axis=-1)[:, None, :]
    return (cosine, sine_table)


def rotate(values, cosine, sine_table):
    half_width = values.shape[-1] // 2
    turned = jnp.concatenate([-values[..., half_width:], values[..., :half_width]], axis=-1)
    return values * cosine + turned * sine_table


def rotate_back(gradient, cosine, sine_table):
    half_width = gradient.shape[-1] // 2
    moved_part = gradient * sine_table
    return gradient * cosine + jnp.concatenate(
        [moved_part[..., half_width:], -moved_part[..., :half_width]], axis=-1
    )


def root_mean_square_parts(values):
    scale_row = lax.rsqrt(jnp.mean(values * values, axis=-1, keepdims=True) + EPSILON)
    return (values * scale_row, scale_row)


def norm_back(grad_normed, normalized, scale_row, gain):
    scaled = grad_normed * gain
    return scale_row * (scaled - normalized * jnp.mean(scaled * normalized, axis=-1, keepdims=True))


def tensor_total(partial_sum):
    return lax.psum(partial_sum, "tensor")


def fetch_weights(shards):
    (
        first_norm_gain,
        second_norm_gain,
        w_query,
        w_key,
        w_value,
        w_gate,
        w_up,
        b_query,
        b_key,
        b_value,
        w_out,
        w_down,
    ) = shards
    row_parts = (
        lax.all_gather(first_norm_gain, "fsdp", axis=0, tiled=True),
        lax.all_gather(second_norm_gain, "fsdp", axis=0, tiled=True),
        lax.all_gather(w_query, "fsdp", axis=0, tiled=True),
        lax.all_gather(w_key, "fsdp", axis=0, tiled=True),
        lax.all_gather(w_value, "fsdp", axis=0, tiled=True),
        lax.all_gather(w_gate, "fsdp", axis=0, tiled=True),
        lax.all_gather(w_up, "fsdp", axis=0, tiled=True),
    )
    col_parts = (
        lax.all_gather(w_out, "fsdp", axis=1, tiled=True),
        lax.all_gather(w_down, "fsdp", axis=1, tiled=True),
    )
    return tuple(row_parts) + (b_query, b_key, b_value) + tuple(col_parts)


def visible(seg_row, pos_row, row_start, count_rows):
    pad_rows = BACK * count_rows
    seg_padded = jnp.concatenate([jnp.full((pad_rows,), -1, jnp.int32), seg_row])
    pos_padded = jnp.concatenate([jnp.zeros((pad_rows,), jnp.int32), pos_row])
    key_seg = lax.dynamic_slice_in_dim(seg_padded, row_start, pad_rows + count_rows)
    key_pos = lax.dynamic_slice_in_dim(pos_padded, row_start, pad_rows + count_rows)
    query_seg = lax.dynamic_slice_in_dim(seg_row, row_start, count_rows)
    query_pos = lax.dynamic_slice_in_dim(pos_row, row_start, count_rows)
    return (query_seg[:, None] == key_seg[None, :]) & (key_pos[None, :] <= query_pos[:, None])


def score_table(grouped, key_rows, allowed):
    raw_scores = jnp.einsum("tkgd,skd->kgts", grouped, key_rows, preferred_element_type=jnp.float32)
    raw_scores = raw_scores * (1.0 / math.sqrt(grouped.shape[-1]))
    return jnp.where(allowed, raw_scores, NEGATIVE)


def forward_part(inputs, seg_row, pos_row, weights, row_start):
    (
        first_norm_gain,
        second_norm_gain,
        w_query,
        w_key,
        w_value,
        w_gate,
        w_up,
        b_query,
        b_key,
        b_value,
        w_out,
        w_down,
    ) = weights
    count_rows = inputs.shape[0]
    head_size = b_query.shape[1]
    input_as_float = inputs.astype(jnp.float32)
    first_unit_rows, first_inverse_scale = root_mean_square_parts(input_as_float)
    first_normed_rows = (first_unit_rows * first_norm_gain.astype(jnp.float32)).astype(jnp.bfloat16)
    query_raw = matmul(first_normed_rows, w_query) + b_query.astype(jnp.float32).reshape(-1)
    key_raw = matmul(first_normed_rows, w_key) + b_key.astype(jnp.float32).reshape(-1)
    value_raw = matmul(first_normed_rows, w_value) + b_value.astype(jnp.float32).reshape(-1)
    query_places = lax.dynamic_slice_in_dim(pos_row, row_start, count_rows)
    cosine, sine_table = rotation(query_places, head_size)
    query_rows = rotate(query_raw.reshape(count_rows, -1, head_size), cosine, sine_table).astype(
        jnp.bfloat16
    )
    key_now = rotate(key_raw.reshape(count_rows, -1, head_size), cosine, sine_table).astype(
        jnp.bfloat16
    )
    value_now = value_raw.reshape(count_rows, -1, head_size).astype(jnp.bfloat16)
    key_list = []
    value_list = []
    for blocks_back in range(BACK, 0, -1):
        far_key, far_value = shifted((key_now, value_now), "fsdp", blocks_back)
        key_list.append(far_key)
        value_list.append(far_value)
    key_rows = jnp.concatenate(key_list + [key_now], axis=0)
    value_rows = jnp.concatenate(value_list + [value_now], axis=0)
    allowed = visible(seg_row, pos_row, row_start, count_rows)
    grouped = query_rows.reshape(count_rows, key_now.shape[1], -1, head_size)
    scores = score_table(grouped, key_rows, allowed)
    row_max = jnp.max(scores, axis=-1, keepdims=True)
    log_total = row_max + jnp.log(jnp.sum(jnp.exp(scores - row_max), axis=-1, keepdims=True))
    probs_low = jnp.exp(scores - log_total).astype(jnp.bfloat16)
    mixed_heads = jnp.einsum(
        "kgts,skd->tkgd", probs_low, value_rows, preferred_element_type=jnp.float32
    )
    heads_out = mixed_heads.reshape(count_rows, -1).astype(jnp.bfloat16)
    residual_state = input_as_float + tensor_total(matmul(heads_out, w_out))
    second_unit_rows, second_inverse_scale = root_mean_square_parts(residual_state)
    second_normed_rows = (second_unit_rows * second_norm_gain.astype(jnp.float32)).astype(
        jnp.bfloat16
    )
    gate_value = matmul(second_normed_rows, w_gate)
    up_part = matmul(second_normed_rows, w_up)
    hidden = (jax.nn.silu(gate_value) * up_part).astype(jnp.bfloat16)
    output_rows = (residual_state + tensor_total(matmul(hidden, w_down))).astype(jnp.bfloat16)
    saved_state = (
        first_unit_rows,
        first_inverse_scale,
        first_normed_rows,
        grouped,
        key_rows,
        value_rows,
        allowed,
        log_total,
        heads_out,
        second_unit_rows,
        second_inverse_scale,
        second_normed_rows,
        gate_value,
        up_part,
        hidden,
        cosine,
        sine_table,
    )
    return (output_rows, saved_state)


def backward_part(grad_rows, saved_state, weights):
    (
        first_norm_gain,
        second_norm_gain,
        w_query,
        w_key,
        w_value,
        w_gate,
        w_up,
        b_query,
        b_key,
        b_value,
        w_out,
        w_down,
    ) = weights
    (
        first_unit_rows,
        first_inverse_scale,
        first_normed_rows,
        grouped,
        key_rows,
        value_rows,
        allowed,
        log_total,
        heads_out,
        second_unit_rows,
        second_inverse_scale,
        second_normed_rows,
        gate_value,
        up_part,
        hidden,
        cosine,
        sine_table,
    ) = saved_state
    count_rows = grad_rows.shape[0]
    head_size = grouped.shape[-1]
    grad_float = grad_rows.astype(jnp.float32)
    grad_mlp = grad_float.astype(jnp.bfloat16)
    grad_w_down = contract_rows(hidden, grad_mlp)
    grad_hidden = times_transpose(grad_mlp, w_down)
    sigmoid_gate = jax.nn.sigmoid(gate_value)
    silu_gate = gate_value * sigmoid_gate
    grad_gate = (
        grad_hidden * up_part * sigmoid_gate * (1.0 + gate_value * (1.0 - sigmoid_gate))
    ).astype(jnp.bfloat16)
    grad_up = (grad_hidden * silu_gate).astype(jnp.bfloat16)
    grad_w_gate = contract_rows(second_normed_rows, grad_gate)
    grad_w_up = contract_rows(second_normed_rows, grad_up)
    second_normed_gradient = tensor_total(
        times_transpose(grad_gate, w_gate) + times_transpose(grad_up, w_up)
    )
    second_gain_gradient = jnp.sum(second_normed_gradient * second_unit_rows, axis=0)
    grad_state = grad_float + norm_back(
        second_normed_gradient,
        second_unit_rows,
        second_inverse_scale,
        second_norm_gain.astype(jnp.float32),
    )
    grad_branch = grad_state.astype(jnp.bfloat16)
    grad_w_out = contract_rows(heads_out, grad_branch)
    grad_heads = times_transpose(grad_branch, w_out).astype(jnp.bfloat16).reshape(grouped.shape)
    scores = score_table(grouped, key_rows, allowed)
    probs = jnp.exp(scores - log_total)
    grad_probs = jnp.einsum(
        "tkgd,skd->kgts", grad_heads, value_rows, preferred_element_type=jnp.float32
    )
    row_inner = jnp.sum(probs * grad_probs, axis=-1, keepdims=True)
    grad_scores = (probs * (grad_probs - row_inner)).astype(jnp.bfloat16)
    inverse_root = 1.0 / math.sqrt(head_size)
    grad_query = (
        jnp.einsum("kgts,skd->tkgd", grad_scores, key_rows, preferred_element_type=jnp.float32)
        * inverse_root
    )
    grad_keys = (
        jnp.einsum("kgts,tkgd->skd", grad_scores, grouped, preferred_element_type=jnp.float32)
        * inverse_root
    )
    grad_values = jnp.einsum(
        "kgts,tkgd->skd", probs.astype(jnp.bfloat16), grad_heads, preferred_element_type=jnp.float32
    )
    key_total = grad_keys[BACK * count_rows :]
    value_total = grad_values[BACK * count_rows :]
    for blocks_back in range(1, BACK + 1):
        first_row = (BACK - blocks_back) * count_rows
        got_key, got_value = (
            shifted(
                grad_keys[first_row : first_row + count_rows].astype(jnp.bfloat16),
                "fsdp",
                -blocks_back,
            ).astype(jnp.float32),
            shifted(
                grad_values[first_row : first_row + count_rows].astype(jnp.bfloat16),
                "fsdp",
                -blocks_back,
            ).astype(jnp.float32),
        )
        key_total = key_total + got_key
        value_total = value_total + got_value
    grad_query_raw = (
        rotate_back(grad_query.reshape(count_rows, -1, head_size), cosine, sine_table)
        .reshape(count_rows, -1)
        .astype(jnp.bfloat16)
    )
    grad_key_raw = (
        rotate_back(key_total, cosine, sine_table).reshape(count_rows, -1).astype(jnp.bfloat16)
    )
    grad_value_raw = value_total.reshape(count_rows, -1).astype(jnp.bfloat16)
    grad_w_query = contract_rows(first_normed_rows, grad_query_raw)
    grad_w_key = contract_rows(first_normed_rows, grad_key_raw)
    grad_w_value = contract_rows(first_normed_rows, grad_value_raw)
    grad_b_query = jnp.sum(grad_query_raw.astype(jnp.float32), axis=0).reshape(-1, head_size)
    grad_b_key = jnp.sum(grad_key_raw.astype(jnp.float32), axis=0).reshape(-1, head_size)
    grad_b_value = jnp.sum(grad_value_raw.astype(jnp.float32), axis=0).reshape(-1, head_size)
    first_normed_gradient = tensor_total(
        times_transpose(grad_query_raw, w_query)
        + times_transpose(grad_key_raw, w_key)
        + times_transpose(grad_value_raw, w_value)
    )
    first_gain_gradient = jnp.sum(first_normed_gradient * first_unit_rows, axis=0)
    input_rows = grad_state + norm_back(
        first_normed_gradient,
        first_unit_rows,
        first_inverse_scale,
        first_norm_gain.astype(jnp.float32),
    )
    gradients = (
        first_gain_gradient,
        second_gain_gradient,
        grad_w_query,
        grad_w_key,
        grad_w_value,
        grad_w_gate,
        grad_w_up,
        grad_b_query,
        grad_b_key,
        grad_b_value,
        grad_w_out,
        grad_w_down,
    )
    return (input_rows, gradients)


def body(
    tokens,
    norm1_gain,
    query_weight,
    query_bias,
    key_weight,
    key_bias,
    value_weight,
    value_bias,
    output_weight,
    norm2_gain,
    gate_weight,
    up_weight,
    down_weight,
    cotangent,
    segments,
    positions,
):
    shards = (
        norm1_gain,
        norm2_gain,
        query_weight,
        key_weight,
        value_weight,
        gate_weight,
        up_weight,
        query_bias,
        key_bias,
        value_bias,
        output_weight,
        down_weight,
    )
    batches = tokens.shape[0]
    count_rows = tokens.shape[1]
    row_start = lax.axis_index("fsdp") * count_rows
    output_list = []
    saved_list = []
    weights = shards
    for batch_index in range(batches):
        weights = fetch_weights(shards)
        output_rows, saved_state = forward_part(
            tokens[batch_index], segments[batch_index], positions[batch_index], weights, row_start
        )
        output_list.append(output_rows)
        saved_list.append(saved_state)
    input_list = [None] * batches
    totals = None
    for batch_index in range(batches - 1, -1, -1):
        weights = fetch_weights(shards)
        input_rows, gradients = backward_part(
            cotangent[batch_index], saved_list[batch_index], weights
        )
        input_list[batch_index] = input_rows
        if batch_index == batches - 1:
            totals = gradients
        else:
            totals = jax.tree.map(jnp.add, totals, gradients)
    sum_gain_one, sum_gain_two, sum_w_query, sum_w_key, sum_w_value, sum_w_gate, sum_w_up = (
        lax.psum_scatter(totals[0], "fsdp", scatter_dimension=0, tiled=True),
        lax.psum_scatter(totals[1], "fsdp", scatter_dimension=0, tiled=True),
        lax.psum_scatter(totals[2], "fsdp", scatter_dimension=0, tiled=True),
        lax.psum_scatter(totals[3], "fsdp", scatter_dimension=0, tiled=True),
        lax.psum_scatter(totals[4], "fsdp", scatter_dimension=0, tiled=True),
        lax.psum_scatter(totals[5], "fsdp", scatter_dimension=0, tiled=True),
        lax.psum_scatter(totals[6], "fsdp", scatter_dimension=0, tiled=True),
    )
    sum_w_out, sum_w_down = (
        lax.psum_scatter(totals[10], "fsdp", scatter_dimension=1, tiled=True),
        lax.psum_scatter(totals[11], "fsdp", scatter_dimension=1, tiled=True),
    )
    sum_b_query, sum_b_key, sum_b_value = lax.psum((totals[7], totals[8], totals[9]), "fsdp")
    return (
        jnp.stack(output_list),
        jnp.stack(input_list),
        sum_gain_one,
        sum_w_query,
        sum_b_query,
        sum_w_key,
        sum_b_key,
        sum_w_value,
        sum_b_value,
        sum_w_out,
        sum_gain_two,
        sum_w_gate,
        sum_w_up,
        sum_w_down,
    )


def solution(mesh):
    placed = (
        P(None, "fsdp", None),
        P("fsdp"),
        P("fsdp", "tensor"),
        P("tensor", None),
        P("fsdp", "tensor"),
        P("tensor", None),
        P("fsdp", "tensor"),
        P("tensor", None),
        P("tensor", "fsdp"),
        P("fsdp"),
        P("fsdp", "tensor"),
        P("fsdp", "tensor"),
        P("tensor", "fsdp"),
        P(None, "fsdp", None),
        P(),
        P(),
    )
    return jax.shard_map(
        body,
        mesh=mesh,
        in_specs=placed,
        out_specs=(
            P(None, "fsdp", None),
            P(None, "fsdp", None),
            P("fsdp"),
            P("fsdp", "tensor"),
            P("tensor", None),
            P("fsdp", "tensor"),
            P("tensor", None),
            P("fsdp", "tensor"),
            P("tensor", None),
            P("tensor", "fsdp"),
            P("fsdp"),
            P("fsdp", "tensor"),
            P("fsdp", "tensor"),
            P("tensor", "fsdp"),
        ),
        check_vma=False,
    )
```

profile of v0, /device:TPU:0, one launch (start us, length us, event | category | flops | bytes accessed | tf_op | source)
XLA Modules:
  0.0 1978.9 jit_solution(3183808392995653961)
XLA Ops:
  11.7 36.5 %all-reduce.12 = (bf16[1536]{0:T(1024)(128)(2,1)S(1)}, bf16[1536]{0:T(1024)(128)(2,1)}) all-reduce(bf16[1536]{0:T(1024)(128)(2,1)S(1)} %dynamic-update-slice, bf16[1536]{0:T(1024)(128)(2,1)S(1)} %dynamic-update-slice.1), channel_id=1, replica_groups=mesh['fsdp'=16,'tensor'=2] {'fsdp'}, use_global_device_ids=true, to_apply=%add.4 | all-reduce | flops 3072 | bytes 12288
  50.7 18.5 all_gather.20
  73.9 4.6 collective-permute-start.17
  78.6 4.7 collective-permute-start.18
  85.3 19.3 all_gather.19
  109.5 3.8 collective-permute-start.12
  113.4 4.5 collective-permute-start.13
  123.4 2.8 collective-permute-start.7
  126.2 2.9 collective-permute-start.8
  137.0 3.0 collective-permute-start.3
  158.8 3.9 fusion.99
  168.1 66.5 %all-reduce.21.cloned.1.call-done = (f32[192,1536]{1,0:T(8,128)}, f32[192,1536]{1,0:T(8,128)}) async-done(((f32[192,1536]{1,0:T(8,128)}, f32[192,1536]{1,0:T(8,128)}), (f32[192,1536]{1,0:T(8,128)}, f32[192,1536]{1,0:T(8,128)})) %all-reduce.21.cloned.1.call-update) | async-done | bytes 2359312 | tf_op jit(solution)/shard_map/psum | solution.py:72
  239.3 105.9 %all-gather.10.cloned.1.call-done = bf16[1536,4480]{1,0:T(8,128)(2,1)} async-done(((bf16[96,4480]{1,0:T(8,128)(2,1)}), bf16[1536,4480]{1,0:T(8,128)(2,1)}) %all-gather.10.cloned.1.call-update) | async-done | bytes 13762576 | tf_op jit(solution)/shard_map/all_gather | solution.py:96
  345.2 9.9 fusion.223
  355.1 98.9 %all-gather.12.cloned.1.call-done = bf16[1536,4480]{1,0:T(8,128)(2,1)} async-done(((bf16[96,4480]{1,0:T(8,128)(2,1)}), bf16[1536,4480]{1,0:T(8,128)(2,1)}) %all-gather.12.cloned.1.call-update) | async-done | bytes 13762576 | tf_op jit(solution)/shard_map/all_gather | solution.py:97
  454.0 10.0 fusion.224
  464.0 6.7 fusion.220
  470.8 4.7 fusion.221
  475.5 87.3 %all-gather.14.cloned.1.call-done = bf16[4480,1536]{0,1:T(8,128)(2,1)} async-done(((bf16[4480,96]{0,1:T(8,128)(2,1)}), bf16[4480,1536]{0,1:T(8,128)(2,1)}) %all-gather.14.cloned.1.call-update) | async-done | bytes 13762576 | tf_op jit(solution)/shard_map/all_gather | solution.py:101
  562.8 12.5 multiply_convert_fusion
  575.3 8.4 fusion.227
  583.8 12.6 multiply_convert_fusion.2
  596.4 7.7 fusion.226
  604.1 10.7 convolution_add_fusion.9
  614.8 10.6 convolution_add_fusion.10
  625.5 12.0 fusion.225
  637.5 10.7 fusion.222
  648.2 44.4 %all-reduce.19.cloned.1.call-done = (f32[192,1536]{1,0:T(8,128)}, f32[192,1536]{1,0:T(8,128)}) async-done(((f32[192,1536]{1,0:T(8,128)}, f32[192,1536]{1,0:T(8,128)}), (f32[192,1536]{1,0:T(8,128)}, f32[192,1536]{1,0:T(8,128)})) %all-reduce.19.cloned.1.call-update) | async-done | bytes 2359312 | tf_op jit(solution)/shard_map/psum | solution.py:72
  692.6 3.8 multiply_reduce_fusion
  696.4 3.4 multiply_add_fusion.1
  744.2 3.4 collective-permute-done.39
  768.0 3.1 convolution_add_fusion.4
  774.3 3.1 convolution_add_fusion.3
  778.5 12.8 fusion.228
  791.3 19.0 convolution_add_fusion.1
  810.4 12.6 fusion.229
  823.0 19.4 convolution_add_fusion
  843.6 13.0 fusion.80
  856.6 19.1 convolution_add_fusion.2
  878.1 14.0 all-reduce.17.cloned.1.call-done
  892.1 3.0 fusion.48
  895.7 61.2 %all-reduce.8 = (f32[1536]{0:T(1024)}, f32[6,128]{1,0:T(8,128)}, f32[1,128]{1,0:T(1,128)}, f32[1,128]{1,0:T(1,128)}, f32[1536]{0:T(1024)}) all-reduce(f32[1536]{0:T(1024)} %add.473, f32[6,128]{1,0:T(8,128)} %add.477, f32[1,128]{1,0:T(1,128)} %add_bitcast_fusion.1, ...), channel_id=2, replica_groups=mesh['fsdp'=16,'tensor'=2] {'fsdp'}, use_global_device_ids=true, to_apply=%region_24.25.clone | all-reduce | flops 4096 | bytes 32768
  967.4 45.3 %reduce-scatter.12.cloned.1.call-done = f32[96,128]{1,0:T(8,128)} async-done(((f32[1536,128]{1,0:T(8,128)}), f32[96,128]{1,0:T(8,128)}) %reduce-scatter.12.cloned.1.call-update) | async-done | bytes 49168 | tf_op jit(solution)/shard_map/reduce_scatter | solution.py:408
  1012.7 79.5 %reduce-scatter.8.cloned.1.call-done = f32[96,768]{1,0:T(8,128)} async-done(((f32[1536,768]{1,0:T(8,128)}), f32[96,768]{1,0:T(8,128)}) %reduce-scatter.8.cloned.1.call-update) | async-done | bytes 294928 | tf_op jit(solution)/shard_map/reduce_scatter | solution.py:406
  1092.3 78.9 %reduce-scatter.14.cloned.1.call-done = f32[768,96]{0,1:T(8,128)} async-done(((f32[768,1536]{0,1:T(8,128)}), f32[768,96]{0,1:T(8,128)}) %reduce-scatter.14.cloned.1.call-update) | async-done | bytes 294928 | tf_op jit(solution)/shard_map/reduce_scatter | solution.py:413
  1171.2 267.3 %reduce-scatter.16.cloned.1.call-done = f32[96,4480]{1,0:T(8,128)} async-done(((f32[1536,4480]{1,0:T(8,128)}), f32[96,4480]{1,0:T(8,128)}) %reduce-scatter.16.cloned.1.call-update) | async-done | bytes 1720336 | tf_op jit(solution)/shard_map/reduce_scatter | solution.py:409
  1438.5 266.5 %reduce-scatter.18.cloned.1.call-done = f32[96,4480]{1,0:T(8,128)} async-done(((f32[1536,4480]{1,0:T(8,128)}), f32[96,4480]{1,0:T(8,128)}) %reduce-scatter.18.cloned.1.call-update) | async-done | bytes 1720336 | tf_op jit(solution)/shard_map/reduce_scatter | solution.py:410
  1705.0 267.1 %reduce-scatter.20.cloned.1.call-done = f32[4480,96]{0,1:T(8,128)} async-done(((f32[4480,1536]{0,1:T(8,128)}), f32[4480,96]{0,1:T(8,128)}) %reduce-scatter.20.cloned.1.call-update) | async-done | bytes 1720336 | tf_op jit(solution)/shard_map/reduce_scatter | solution.py:414
  (468 shorter events, 141.8 us)
Async XLA Ops:
  7.2 135.0 %all-gather.6.cloned.1.call-start = ((), (), s32[]{:S(2)}) async-start(), calls=%async_computation.7 | async-start | bytes 2506752 | tf_op jit(solution)/shard_map/all_gather | solution.py:93
  7.9 150.8 %all-gather.8.cloned.1.call-start = ((), (), s32[]{:S(2)}) async-start(), calls=%async_computation.8 | async-start | bytes 2506752 | tf_op jit(solution)/shard_map/all_gather | solution.py:100
  71.3 35.5 %collective-permute-start.15 = (bf16[192,1,128]{2,0,1:T(8,128)(2,1)S(1)}, bf16[192,1,128]{2,0,1:T(8,128)(2,1)S(1)}, u32[]{:S(2)}, u32[]{:S(2)}) collective-permute-start(bf16[192,1,128]{2,0,1:T(8,128)(2,1)S(1)} %get-tuple-element.112), channel_id=1, source_target_pairs={{0,10},{2,12},{4,14},{6,16},{8,18},{10,20},{12,22},{14,24},{16,26}... | collective-permute-start | bytes 147464 | tf_op jit(solution)/shard_map/ppermute | solution.py:19
  72.6 35.6 %collective-permute-start.16 = (bf16[192,1,128]{2,0,1:T(8,128)(2,1)S(1)}, bf16[192,1,128]{2,0,1:T(8,128)(2,1)S(1)}, u32[]{:S(2)}, u32[]{:S(2)}) collective-permute-start(bf16[192,1,128]{2,0,1:T(8,128)(2,1)S(1)} %get-tuple-element.112), channel_id=1, source_target_pairs={{0,8},{2,10},{4,12},{6,14},{8,16},{10,18},{12,20},{14,22},{16,24},... | collective-permute-start | bytes 147464 | tf_op jit(solution)/shard_map/ppermute | solution.py:19
  73.9 35.6 %collective-permute-start.17 = (bf16[192,1,128]{2,0,1:T(8,128)(2,1)S(1)}, bf16[192,1,128]{2,0,1:T(8,128)(2,1)S(1)}, u32[]{:S(2)}, u32[]{:S(2)}) collective-permute-start(bf16[192,1,128]{2,0,1:T(8,128)(2,1)S(1)} %get-tuple-element.112), channel_id=1, source_target_pairs={{0,6},{2,8},{4,10},{6,12},{8,14},{10,16},{12,18},{14,20},{16,22},{... | collective-permute-start | bytes 147464 | tf_op jit(solution)/shard_map/ppermute | solution.py:19
  78.6 34.8 %collective-permute-start.18 = (bf16[192,1,128]{2,0,1:T(8,128)(2,1)S(1)}, bf16[192,1,128]{2,0,1:T(8,128)(2,1)S(1)}, u32[]{:S(2)}, u32[]{:S(2)}) collective-permute-start(bf16[192,1,128]{2,0,1:T(8,128)(2,1)S(1)} %get-tuple-element.112), channel_id=1, source_target_pairs={{0,4},{2,6},{4,8},{6,10},{8,12},{10,14},{12,16},{14,18},{16,20},{1... | collective-permute-start | bytes 147464 | tf_op jit(solution)/shard_map/ppermute | solution.py:19
  83.2 34.6 %collective-permute-start.19 = (bf16[192,1,128]{2,0,1:T(8,128)(2,1)S(1)}, bf16[192,1,128]{2,0,1:T(8,128)(2,1)S(1)}, u32[]{:S(2)}, u32[]{:S(2)}) collective-permute-start(bf16[192,1,128]{2,0,1:T(8,128)(2,1)S(1)} %get-tuple-element.112), channel_id=1, source_target_pairs={{0,2},{2,4},{4,6},{6,8},{8,10},{10,12},{12,14},{14,16},{16,18},{18... | collective-permute-start | bytes 147464 | tf_op jit(solution)/shard_map/ppermute | solution.py:19
  84.6 150.0 %all-reduce.21.cloned.1.call-start = ((), (), s32[]{:S(2)}) async-start(), calls=%async_computation.21 | async-start | bytes 4718592 | tf_op jit(solution)/shard_map/psum | solution.py:72
  106.9 12.4 collective-permute-start.10
  108.2 13.6 collective-permute-start.11
  109.5 13.9 collective-permute-start.12
  113.4 12.9 collective-permute-start.13
  117.9 11.2 collective-permute-start.14
  119.3 11.2 collective-permute-start.5
  121.8 10.6 collective-permute-start.6
  123.4 11.5 collective-permute-start.7
  126.2 10.7 collective-permute-start.8
  129.1 10.8 collective-permute-start.9
  130.5 11.0 collective-permute-start
  164.6 180.6 %all-gather.10.cloned.1.call-start = ((), (), s32[]{:S(2)}) async-start(), calls=%async_computation.9 | async-start | bytes 14622720 | tf_op jit(solution)/shard_map/all_gather | solution.py:96
  165.2 288.8 %all-gather.12.cloned.1.call-start = ((), (), s32[]{:S(2)}) async-start(), calls=%async_computation.10 | async-start | bytes 14622720 | tf_op jit(solution)/shard_map/all_gather | solution.py:97
  165.8 397.0 %all-gather.14.cloned.1.call-start = ((), (), s32[]{:S(2)}) async-start(), calls=%async_computation.11 | async-start | bytes 14622720 | tf_op jit(solution)/shard_map/all_gather | solution.py:101
  166.3 526.3 %all-reduce.19.cloned.1.call-start = ((), (), s32[]{:S(2)}) async-start(), calls=%async_computation.20 | async-start | bytes 4718592 | tf_op jit(solution)/shard_map/psum | solution.py:72
  625.4 266.6 %all-reduce.17.cloned.1.call-start = ((), (), s32[]{:S(2)}) async-start(), calls=%async_computation.19 | async-start | bytes 9437184 | tf_op jit(solution)/shard_map/psum | solution.py:72
  716.3 11.6 collective-permute-start.34
  717.6 11.7 collective-permute-start.33
  718.9 11.8 collective-permute-start.32
  720.2 11.8 collective-permute-start.31
  721.5 11.8 collective-permute-start.30
  729.3 9.4 collective-permute-start.23
  730.6 9.4 collective-permute-start.22
  731.9 9.4 collective-permute-start.21
  733.3 9.4 collective-permute-start.20
  736.6 11.1 collective-permute-start.39
  738.8 10.2 collective-permute-start.38
  740.1 10.2 collective-permute-start.37
  741.4 10.2 collective-permute-start.36
  742.7 10.2 collective-permute-start.35
  747.6 10.0 collective-permute-start.29
  748.9 9.8 collective-permute-start.28
  750.2 9.4 collective-permute-start.27
  762.5 204.9 %reduce-scatter.10.cloned.1.call-start = ((), (), s32[]{:S(2)}) async-start(), calls=%async_computation.13 | async-start | bytes 835584 | tf_op jit(solution)/shard_map/reduce_scatter | solution.py:407
  765.0 247.7 %reduce-scatter.12.cloned.1.call-start = ((), (), s32[]{:S(2)}) async-start(), calls=%async_computation.14 | async-start | bytes 835584 | tf_op jit(solution)/shard_map/reduce_scatter | solution.py:408
  767.0 325.2 %reduce-scatter.8.cloned.1.call-start = ((), (), s32[]{:S(2)}) async-start(), calls=%async_computation.12 | async-start | bytes 5013504 | tf_op jit(solution)/shard_map/reduce_scatter | solution.py:406
  771.2 400.0 %reduce-scatter.14.cloned.1.call-start = ((), (), s32[]{:S(2)}) async-start(), calls=%async_computation.15 | async-start | bytes 5013504 | tf_op jit(solution)/shard_map/reduce_scatter | solution.py:413
  777.4 661.1 %reduce-scatter.16.cloned.1.call-start = ((), (), s32[]{:S(2)}) async-start(), calls=%async_computation.16 | async-start | bytes 29245440 | tf_op jit(solution)/shard_map/reduce_scatter | solution.py:409
  810.3 894.7 %reduce-scatter.18.cloned.1.call-start = ((), (), s32[]{:S(2)}) async-start(), calls=%async_computation.17 | async-start | bytes 29245440 | tf_op jit(solution)/shard_map/reduce_scatter | solution.py:410
  842.3 1129.7 %reduce-scatter.20.cloned.1.call-start = ((), (), s32[]{:S(2)}) async-start(), calls=%async_computation.18 | async-start | bytes 29245440 | tf_op jit(solution)/shard_map/reduce_scatter | solution.py:414
  (118 other events, 1307.8 us)
Sparse Core Ops, SparseCore 0:
  10.3 45.5 all-gather.5
  84.8 42.7 all-gather.7
  164.7 69.8 all-reduce.20
  237.0 108.1 all-gather.9
  347.6 106.3 all-gather.11
  456.4 106.3 all-gather.13
  625.6 66.9 all-reduce.18
  762.6 129.4 all-reduce.16
  896.6 56.5 reduce-scatter.9
  957.2 55.5 reduce-scatter.11
  1017.7 74.5 reduce-scatter.7
  1096.6 74.5 reduce-scatter.13
  1176.4 262.0 reduce-scatter.15
  1443.0 261.9 reduce-scatter.17
  1710.1 261.9 reduce-scatter.19
where the time goes:
time: 1990 us; the launch traced here: 1980 us
  waiting for transfers between devices  1430 us (72%)
  matrix products  257 us (13%)
  blocking collectives  135 us (7%)
  starting transfers between devices  74.8 us (4%)
  other arithmetic  36.3 us (2%)
  local copies, waits for them, and re-layouts  24.7 us (1%)
    reduce_scatter x1, waiting for transfers between devices, body(): lax.psum_scatter(totals[5], 'fsdp', scatter_dimension=0, tiled=True)  267 us
    reduce_scatter x1, waiting for transfers between devices, body(): lax.psum_scatter(totals[11], 'fsdp', scatter_dimension=1, tiled=True)  267 us
    reduce_scatter x1, waiting for transfers between devices, body(): lax.psum_scatter(totals[6], 'fsdp', scatter_dimension=0, tiled=True)  267 us
    psum x3, waiting for transfers between devices, tensor_total(): return lax.psum(partial_sum, 'tensor')  125 us
    dot_general x14, matrix products, contract_rows(): lax.dot_general(left_side, right_side, (((0,), (0,)), ((), ())), preferre...  109 us
    all_gather x1, waiting for transfers between devices, fetch_weights(): lax.all_gather(w_gate, 'fsdp', axis=0, tiled=True)  106 us
    all_gather x1, waiting for transfers between devices, fetch_weights(): lax.all_gather(w_up, 'fsdp', axis=0, tiled=True)  98.9 us
    unnamed x2, blocking collectives  97.7 us
  transfers between devices with their start and end apart: 55, of which 21 were waited for; matrix products, arithmetic and copies ran while one was open for 11% of the time, Pallas kernels for 0%

commit v1 on v0

v1 whole, which is shorter than its diff:
```python
import math

import jax
import jax.numpy as jnp
from jax import lax
from jax.sharding import Mesh
from jax.sharding import PartitionSpec as P

BACK = 5
LINE = 4
LANES = 128

EPSILON = 1e-06
THETA = 1000000.0
NEGATIVE = -1e30

RING, PAIR, CORE, TENSOR = "ring", "pair", "core", "tensor"
FSDP = (RING, PAIR, CORE)
SWAP = [(0, 1), (1, 0)]


def low(value):
    return value.astype(jnp.bfloat16)


def wide(value):
    return value.astype(jnp.float32)


def matmul(left_side, right_side):
    return jnp.dot(left_side, right_side, preferred_element_type=jnp.float32)


def contract_rows(left_side, right_side):
    return lax.dot_general(
        left_side, right_side, (((0,), (0,)), ((), ())), preferred_element_type=jnp.float32
    )


def times_transpose(left_side, right_side):
    return lax.dot_general(
        left_side, right_side, (((1,), (1,)), ((), ())), preferred_element_type=jnp.float32
    )


def swapped(value, axis):
    return lax.ppermute(value, axis, SWAP)


def in_order(own, other, place, axis):
    first = jnp.where(place == 0, own, other)
    second = jnp.where(place == 0, other, own)
    return jnp.stack([first, second], axis=axis)


def shifted(value, steps):
    count = lax.axis_size(FSDP)
    first, last = (max(0, -steps), min(count, count - steps))
    return lax.ppermute(value, FSDP, [(source, source + steps) for source in range(first, last)])


def summed_over_fsdp(value):
    count = lax.axis_size(FSDP)
    bit = 1
    while bit < count:
        value = value + lax.ppermute(value, FSDP, [(i, i ^ bit) for i in range(count)])
        bit *= 2
    return value


def line_gather(block):
    count, here = lax.axis_size(RING), lax.axis_index(RING)
    if count > LINE:
        return lax.all_gather(block, RING, axis=0)
    right, left = [block], [block]
    for step in range(1, count):
        right.append(
            lax.ppermute(right[-1], RING, [(i, i + 1) for i in range(step - 1, count - 1)])
        )
        left.append(
            lax.ppermute(left[-1], RING, [(i, i - 1) for i in range(1, count - step + 1)])
        )
    result = jnp.zeros((count,) + block.shape, block.dtype)
    for step in range(count):
        piece = block if step == 0 else jnp.where(here >= step, right[step], left[count - step])
        result = lax.dynamic_update_slice_in_dim(
            result, piece[None], (here - step + count) % count, axis=0
        )
    return result


def line_scatter(parts):
    count, here = lax.axis_size(RING), lax.axis_index(RING)
    if count > LINE:
        return wide(lax.psum_scatter(parts, RING, scatter_dimension=0, tiled=False))

    def part(place):
        return lax.dynamic_index_in_dim(parts, place, axis=0, keepdims=False)

    right, left = None, None
    for step in range(1, count):
        to_right, to_left = part(here + count - step), part(here - count + step)
        if step > 1:
            to_right = low(wide(to_right) + wide(right))
            to_left = low(wide(to_left) + wide(left))
        right = lax.ppermute(to_right, RING, [(i, i + 1) for i in range(step)])
        left = lax.ppermute(to_left, RING, [(i, i - 1) for i in range(count - step, count)])
    return wide(part(here)) + wide(right) + wide(left)


def gather_rows(shard):
    rows = line_gather(shard)
    rows = in_order(rows, swapped(rows, PAIR), lax.axis_index(PAIR), 1)
    rows = in_order(rows, swapped(rows, CORE), lax.axis_index(CORE), 2)
    return rows.reshape((-1,) + shard.shape[1:])


def scatter_rows(total):
    pair, core = lax.axis_index(PAIR), lax.axis_index(CORE)
    parts = low(total).reshape((lax.axis_size(RING), 2, 2, -1) + total.shape[1:])

    def halved(value, axis, place, name):
        mine = lax.dynamic_index_in_dim(value, place, axis=axis, keepdims=False)
        sent = lax.dynamic_index_in_dim(value, 1 - place, axis=axis, keepdims=False)
        return low(wide(mine) + wide(swapped(sent, name)))

    parts = halved(parts, 2, core, CORE)
    parts = halved(parts, 1, pair, PAIR)
    return line_scatter(parts)


def quarter_columns(shard):
    pair, core = lax.axis_index(PAIR), lax.axis_index(CORE)
    half = shard.shape[1] // 2

    def halved(value, place, width):
        mine = lax.dynamic_slice_in_dim(value, place * width, width, axis=value.ndim - 1)
        sent = lax.dynamic_slice_in_dim(value, (1 - place) * width, width, axis=value.ndim - 1)
        return mine, sent

    mine, sent = halved(shard, pair, half)
    rows = in_order(mine, swapped(sent, PAIR), pair, 0)
    mine, sent = halved(rows, core, half // 2)
    rows = in_order(mine, swapped(sent, CORE), core, 1)
    rows = line_gather(rows.reshape(-1, half // 2))
    return rows.reshape(-1, half // 2)


def quarter_to_owner(grad):
    pair, core = lax.axis_index(PAIR), lax.axis_index(CORE)
    width = grad.shape[1]
    block = low(line_scatter(grad.reshape(lax.axis_size(RING), -1, width)))
    block = block.reshape(2, 2, -1, width)

    def halved(value, axis, place):
        mine = lax.dynamic_index_in_dim(value, place, axis=axis, keepdims=False)
        sent = lax.dynamic_index_in_dim(value, 1 - place, axis=axis, keepdims=False)
        return mine, sent

    mine, sent = halved(block, 0, pair)
    block = in_order(mine, swapped(sent, PAIR), pair, 0)
    mine, sent = halved(block, 1, core)
    block = in_order(mine, swapped(sent, CORE), core, 1)
    return jnp.concatenate([wide(block[i, j]) for i in range(2) for j in range(2)], axis=1)


def four_blocks(value):
    over = swapped(value, PAIR)
    return jnp.concatenate([value, over, swapped(value, CORE), swapped(over, CORE)], axis=0)


def four_sums(total):
    half = total.shape[0] // 2
    total = total[:half] + wide(swapped(low(total[half:]), CORE))
    total = total[: half // 2] + wide(swapped(low(total[half // 2 :]), PAIR))
    return tensor_total(total)


def tensor_total(partial_sum):
    own = lax.reduce_precision(partial_sum, 8, 7)
    return own + wide(swapped(low(own), TENSOR))


def rotation(places, width):
    half_width = width // 2
    frequency = THETA ** (-(jnp.arange(half_width, dtype=jnp.float32) * 2.0) / width)
    angles = places.astype(jnp.float32)[:, None] * frequency[None, :]
    cosine = jnp.concatenate([jnp.cos(angles), jnp.cos(angles)], axis=-1)[:, None, :]
    sine_table = jnp.concatenate([jnp.sin(angles), jnp.sin(angles)], axis=-1)[:, None, :]
    return (cosine, sine_table)


def rotate(values, cosine, sine_table):
    half_width = values.shape[-1] // 2
    turned = jnp.concatenate([-values[..., half_width:], values[..., :half_width]], axis=-1)
    return values * cosine + turned * sine_table


def rotate_back(gradient, cosine, sine_table):
    half_width = gradient.shape[-1] // 2
    moved_part = gradient * sine_table
    return gradient * cosine + jnp.concatenate(
        [moved_part[..., half_width:], -moved_part[..., :half_width]], axis=-1
    )


def root_mean_square_parts(values):
    scale_row = lax.rsqrt(jnp.mean(values * values, axis=-1, keepdims=True) + EPSILON)
    return (values * scale_row, scale_row)


def norm_back(grad_normed, normalized, scale_row, gain):
    scaled = grad_normed * gain
    return scale_row * (scaled - normalized * jnp.mean(scaled * normalized, axis=-1, keepdims=True))


def visible(seg_row, pos_row, row_start, count_rows):
    pad_rows = BACK * count_rows
    seg_padded = jnp.concatenate([jnp.full((pad_rows,), -1, jnp.int32), seg_row])
    pos_padded = jnp.concatenate([jnp.zeros((pad_rows,), jnp.int32), pos_row])
    key_seg = lax.dynamic_slice_in_dim(seg_padded, row_start, pad_rows + count_rows)
    key_pos = lax.dynamic_slice_in_dim(pos_padded, row_start, pad_rows + count_rows)
    query_seg = lax.dynamic_slice_in_dim(seg_row, row_start, count_rows)
    query_pos = lax.dynamic_slice_in_dim(pos_row, row_start, count_rows)
    return (query_seg[:, None] == key_seg[None, :]) & (key_pos[None, :] <= query_pos[:, None])


def attend(query_rows, key_rows, value_rows, allowed):
    scores = jnp.einsum("thd,sd->hts", query_rows, key_rows, preferred_element_type=jnp.float32)
    scores = scores * (1.0 / math.sqrt(query_rows.shape[-1]))
    scores = jnp.where(allowed, scores, NEGATIVE)
    row_max = jnp.max(scores, axis=-1, keepdims=True)
    log_total = row_max + jnp.log(jnp.sum(jnp.exp(scores - row_max), axis=-1, keepdims=True))
    probs_low = low(jnp.exp(scores - log_total))
    mixed = jnp.einsum("hts,sd->thd", probs_low, value_rows, preferred_element_type=jnp.float32)
    return low(mixed.reshape(query_rows.shape[0], -1)), log_total


def attend_back(grad_heads, query_rows, key_rows, value_rows, allowed, log_total):
    scale = 1.0 / math.sqrt(query_rows.shape[-1])
    scores = jnp.einsum("thd,sd->hts", query_rows, key_rows, preferred_element_type=jnp.float32)
    probs = jnp.exp(jnp.where(allowed, scores * scale, NEGATIVE) - log_total)
    grad_probs = jnp.einsum(
        "thd,sd->hts", grad_heads, value_rows, preferred_element_type=jnp.float32
    )
    row_inner = jnp.sum(probs * grad_probs, axis=-1, keepdims=True)
    grad_scores = low(probs * (grad_probs - row_inner))
    grad_query = jnp.einsum(
        "hts,sd->thd", grad_scores, key_rows, preferred_element_type=jnp.float32
    )
    grad_keys = jnp.einsum(
        "hts,thd->sd", grad_scores, query_rows, preferred_element_type=jnp.float32
    )
    grad_values = jnp.einsum(
        "hts,thd->sd", low(probs), grad_heads, preferred_element_type=jnp.float32
    )
    return grad_query * scale, grad_keys * scale, grad_values


def body(
    tokens,
    norm1_gain,
    query_weight,
    query_bias,
    key_weight,
    key_bias,
    value_weight,
    value_bias,
    output_weight,
    norm2_gain,
    gate_weight,
    up_weight,
    down_weight,
    cotangent,
    segments,
    positions,
):
    batches, count_rows, width = tokens.shape
    heads, head_size = query_bias.shape
    query_width = heads * head_size
    units = gate_weight.shape[1]
    place = lax.axis_index(FSDP)
    row_start = place * count_rows
    rows = batches * count_rows

    gains = jnp.stack([norm1_gain, norm2_gain], axis=1)
    gains = jnp.pad(gains, ((0, 0), (0, LANES - 2)))
    first_shard = jnp.concatenate([query_weight, key_weight, value_weight, gains], axis=1)
    first_all = gather_rows(first_shard)
    kv_width = query_width + 2 * head_size
    w_qkv = first_all[:, :kv_width]
    first_gain = wide(first_all[:, kv_width])
    second_gain = wide(first_all[:, kv_width + 1])
    w_out = gather_rows(output_weight.T)

    padded = -(-units // (4 * LANES)) * (4 * LANES)

    def quarter(shard):
        return quarter_columns(jnp.pad(shard, ((0, 0), (0, padded - units))))

    w_gate = quarter(gate_weight)
    w_up = quarter(up_weight)
    w_down = quarter(down_weight.T)
    grad_out = cotangent.reshape(rows, width)
    grad_out_four = four_blocks(grad_out)

    inputs = wide(tokens.reshape(rows, width))
    first_unit, first_scale = root_mean_square_parts(inputs)
    first_normed = low(first_unit * first_gain)
    biases = jnp.concatenate(
        [query_bias.reshape(-1), key_bias.reshape(-1), value_bias.reshape(-1)]
    )
    raw = matmul(first_normed, w_qkv) + wide(biases)
    own_places = lax.dynamic_slice_in_dim(positions, row_start, count_rows, axis=1)
    cosine, sine_table = rotation(own_places.reshape(-1), head_size)
    turned = rotate(
        raw[:, : query_width + head_size].reshape(rows, heads + 1, head_size), cosine, sine_table
    )
    turned = low(turned)
    query_rows = turned[:, :heads].reshape(batches, count_rows, heads, head_size)
    key_value = jnp.concatenate([turned[:, heads], low(raw[:, query_width + head_size :])], axis=1)
    key_value = key_value.reshape(batches, count_rows, 2 * head_size)
    window = jnp.concatenate(
        [shifted(key_value, back) for back in range(BACK, 0, -1)] + [key_value], axis=1
    )
    key_rows, value_rows = window[..., :head_size], window[..., head_size:]
    allowed = [
        visible(segments[b], positions[b], row_start, count_rows) for b in range(batches)
    ]
    attended = [
        attend(query_rows[b], key_rows[b], value_rows[b], allowed[b]) for b in range(batches)
    ]
    heads_out = jnp.concatenate([mixed for mixed, _ in attended], axis=0)
    residual = inputs + tensor_total(times_transpose(heads_out, w_out))

    second_unit, second_scale = root_mean_square_parts(residual)
    second_normed = four_blocks(low(second_unit * second_gain))
    gate_value = matmul(second_normed, w_gate)
    up_part = matmul(second_normed, w_up)
    sigmoid_gate = jax.nn.sigmoid(gate_value)
    silu_gate = gate_value * sigmoid_gate
    hidden = low(silu_gate * up_part)
    grad_hidden = matmul(grad_out_four, w_down)
    grad_gate = low(
        grad_hidden * up_part * sigmoid_gate * (1.0 + gate_value * (1.0 - sigmoid_gate))
    )
    grad_up = low(grad_hidden * silu_gate)
    second_back = four_sums(times_transpose(grad_gate, w_gate) + times_transpose(grad_up, w_up))
    grad_w_down = quarter_to_owner(low(contract_rows(grad_out_four, hidden)))
    grad_w_gate = quarter_to_owner(low(contract_rows(second_normed, grad_gate)))
    grad_w_up = quarter_to_owner(low(contract_rows(second_normed, grad_up)))
    output = low(residual + four_sums(times_transpose(hidden, w_down)))

    second_gain_sum = jnp.sum(second_back * second_unit, axis=0)
    grad_state = wide(grad_out) + norm_back(second_back, second_unit, second_scale, second_gain)
    grad_branch = low(grad_state)
    grad_w_out = scatter_rows(contract_rows(grad_branch, heads_out))
    grad_heads = low(matmul(grad_branch, w_out)).reshape(query_rows.shape)
    backs = [
        attend_back(
            grad_heads[b], query_rows[b], key_rows[b], value_rows[b], allowed[b], attended[b][1]
        )
        for b in range(batches)
    ]
    grad_query = jnp.stack([back[0] for back in backs]).reshape(rows, heads, head_size)
    grad_window = jnp.stack([jnp.concatenate([back[1], back[2]], axis=1) for back in backs])
    own_grad = grad_window[:, BACK * count_rows :]
    for back in range(1, BACK + 1):
        first_row = (BACK - back) * count_rows
        own_grad = own_grad + wide(
            shifted(low(grad_window[:, first_row : first_row + count_rows]), -back)
        )
    own_grad = own_grad.reshape(rows, 2, head_size)
    turned_back = rotate_back(
        jnp.concatenate([grad_query, own_grad[:, :1]], axis=1), cosine, sine_table
    )
    grad_raw = low(jnp.concatenate([turned_back, own_grad[:, 1:]], axis=1).reshape(rows, -1))
    grad_w_qkv = scatter_rows(contract_rows(first_normed, grad_raw))
    bias_sum = jnp.sum(wide(grad_raw), axis=0)
    first_back_part = times_transpose(grad_raw, w_qkv)
    first_back = tensor_total(first_back_part)
    first_gain_sum = jnp.sum(first_back * first_unit, axis=0)
    input_grad = grad_state + norm_back(first_back, first_unit, first_scale, first_gain)
    sums = summed_over_fsdp(jnp.concatenate([bias_sum, second_gain_sum, first_gain_sum]))
    bias_total = sums[:kv_width]
    gain_rows = norm1_gain.shape[0]
    second_total = lax.dynamic_slice_in_dim(sums, kv_width + place * gain_rows, gain_rows)
    first_total = lax.dynamic_slice_in_dim(sums, kv_width + width + place * gain_rows, gain_rows)

    return (
        output.reshape(tokens.shape),
        input_grad.reshape(tokens.shape),
        first_total,
        grad_w_qkv[:, :query_width],
        bias_total[:query_width].reshape(query_bias.shape),
        grad_w_qkv[:, query_width : query_width + head_size],
        bias_total[query_width : query_width + head_size].reshape(key_bias.shape),
        grad_w_qkv[:, query_width + head_size :],
        bias_total[query_width + head_size :].reshape(value_bias.shape),
        grad_w_out.T,
        second_total,
        grad_w_gate[:, :units],
        grad_w_up[:, :units],
        grad_w_down[:, :units].T,
    )


def solution(mesh):
    fsdp, tensor = mesh.shape["fsdp"], mesh.shape["tensor"]
    fine = Mesh(mesh.devices.reshape(fsdp // 4, 2, 2, tensor), (RING, PAIR, CORE, TENSOR))
    by_rows, by_columns, by_tensor = P(FSDP, TENSOR), P(TENSOR, FSDP), P(TENSOR, None)
    by_tokens, by_gain = P(None, FSDP, None), P(FSDP)
    placed = (
        by_tokens,
        by_gain,
        by_rows,
        by_tensor,
        by_rows,
        by_tensor,
        by_rows,
        by_tensor,
        by_columns,
        by_gain,
        by_rows,
        by_rows,
        by_columns,
        by_tokens,
        P(),
        P(),
    )
    return jax.shard_map(
        body,
        mesh=fine,
        in_specs=placed,
        out_specs=(
            by_tokens,
            by_tokens,
            by_gain,
            by_rows,
            by_tensor,
            by_rows,
            by_tensor,
            by_rows,
            by_tensor,
            by_columns,
            by_gain,
            by_rows,
            by_rows,
            by_columns,
        ),
        check_vma=False,
    )
```

time: 1990 us -> 844 us (0.42)
  waiting for transfers between devices: 1430 us -> 284 us
  starting transfers between devices: 74.8 us -> 305 us
  matrix products: 257 us -> 117 us
  blocking collectives: 135 us -> 0 us
  other arithmetic: 36.3 us -> 78.2 us
  local copies, waits for them, and re-layouts: 24.7 us -> 46.9 us
    reduce_scatter x7 -> x0, waiting for transfers between devices: 1000 us -> none  [the longest x1 267 us: body(): lax.psum_scatter(totals[5], 'fsdp', scatter_dimension=0, tiled=True)]
    all_gather x5 -> x0, waiting for transfers between devices: 292 us -> none  [the longest x1 106 us: fetch_weights(): lax.all_gather(w_gate, 'fsdp', axis=0, tiled=True)]
    ppermute x40 -> x108, waiting for transfers between devices: 8.86 us -> 284 us  [the longest x34 116 us: swapped(): return lax.ppermute(value, axis, SWAP)]
    ppermute x40 -> x108, starting transfers between devices: 73.4 us -> 305 us  [the longest x15 124 us: line_scatter(): right = lax.ppermute(to_right, RING, [(i, i + 1) for i in range(step)])]
    psum x3 -> x0, waiting for transfers between devices: 125 us -> none  [tensor_total(): return lax.psum(partial_sum, 'tensor')]
    unnamed x2 -> x0, blocking collectives: 97.7 us -> none
    dot_general x14 -> x5, matrix products: 109 us -> 27.6 us  [contract_rows(): lax.dot_general(left_side, right_side, (((0,), (0,)), ((), ())), preferre...]
    all_gather x2 -> x0, blocking collectives: 37.8 us -> none  [the longest x1 19.3 us: fetch_weights(): lax.all_gather(w_value, 'fsdp', axis=0, tiled=True)]
  transfers between devices with their start and end apart: 55 -> 108, of which waited for: 21 -> 35; matrix products, arithmetic and copies ran while one was open for 11% -> 19% of each run, Pallas kernels for 0% -> 0%
where the time goes in v1:
time: 844 us; the launch traced here: 836 us
  starting transfers between devices  305 us (36%)
  waiting for transfers between devices  284 us (34%)
  matrix products  117 us (14%)
  other arithmetic  78.2 us (9%)
  local copies, waits for them, and re-layouts  46.9 us (6%)
    ppermute x15, starting transfers between devices, line_scatter(): right = lax.ppermute(to_right, RING, [(i, i + 1) for i in range(step)])  124 us
    ppermute x34, waiting for transfers between devices, swapped(): return lax.ppermute(value, axis, SWAP)  116 us
    ppermute x15, waiting for transfers between devices, line_gather(): lax.ppermute(left[-1], RING, [(i, i - 1) for i in range(1, count - step +...  93.6 us
    ppermute x34, starting transfers between devices, swapped(): return lax.ppermute(value, axis, SWAP)  70.2 us
    dot_general x5, matrix products, matmul(): return jnp.dot(left_side, right_side, preferred_element_type=jnp.float32)  42.1 us
    ppermute x15, starting transfers between devices, line_gather(): lax.ppermute(right[-1], RING, [(i, i + 1) for i in range(step - 1, count...  37.2 us
    ppermute x15, waiting for transfers between devices, line_scatter(): lax.ppermute(to_left, RING, [(i, i - 1) for i in range(count - step, coun...  36.3 us
    dot_general x5, matrix products, times_transpose(): lax.dot_general(left_side, right_side, (((1,), (1,)), ((), ())), preferre...  34.5 us
  transfers between devices with their start and end apart: 108, of which 35 were waited for; matrix products, arithmetic and copies ran while one was open for 19% of the time, Pallas kernels for 0%

profile of v1, /device:TPU:0, one launch (start us, length us, event | category | flops | bytes accessed | tf_op | source)
XLA Modules:
  0.0 835.6 jit_solution(12358225796094516917)
XLA Ops:
  2.1 6.2 collective-permute-start.13
  12.1 5.2 collective-permute-start
  53.9 7.0 collective-permute-done.33
  63.3 7.8 collective-permute-done.3
  77.1 5.5 collective-permute-start.27
  82.8 11.5 %collective-permute-done.6 = bf16[4,96,1152]{2,1,0:T(8,128)(2,1)S(1)} collective-permute-done((bf16[4,96,1152]{2,1,0:T(8,128)(2,1)S(1)}, bf16[4,96,1152]{2,1,0:T(8,128)(2,1)S(1)}, u32[]{:S(2)}, u32[]{:S(2)}) %collective-permute-start.6) | collective-permute-done | bytes 884768 | tf_op jit(solution)/shard_map/ppermute | solution.py:47
  132.0 4.7 collective-permute-start.11
  142.2 7.1 collective-permute-start.35
  151.4 13.8 %collective-permute-done.29 = bf16[384,1152]{1,0:T(8,128)(2,1)S(1)} collective-permute-done((bf16[384,1152]{1,0:T(8,128)(2,1)}, bf16[384,1152]{1,0:T(8,128)(2,1)S(1)}, u32[]{:S(2)}, u32[]{:S(2)}) %collective-permute-start.29) | collective-permute-done | bytes 884768 | tf_op jit(solution)/shard_map/ppermute | solution.py:81
  179.5 4.7 collective-permute-done.37
  184.2 37.1 %collective-permute-done.30 = bf16[384,1152]{1,0:T(8,128)(2,1)S(1)} collective-permute-done((bf16[384,1152]{1,0:T(8,128)(2,1)S(1)}, bf16[384,1152]{1,0:T(8,128)(2,1)S(1)}, u32[]{:S(2)}, u32[]{:S(2)}) %collective-permute-start.30) | collective-permute-done | bytes 884768 | tf_op jit(solution)/shard_map/ppermute | solution.py:81
  222.9 5.8 collective-permute-start.43
  231.0 14.7 %collective-permute-done.38 = bf16[384,1152]{1,0:T(8,128)(2,1)S(1)} collective-permute-done((bf16[384,1152]{1,0:T(8,128)(2,1)S(1)}, bf16[384,1152]{1,0:T(8,128)(2,1)S(1)}, u32[]{:S(2)}, u32[]{:S(2)}) %collective-permute-start.38) | collective-permute-done | bytes 884768 | tf_op jit(solution)/shard_map/ppermute | solution.py:81
  252.8 10.2 %collective-permute-done.46 = bf16[384,1152]{1,0:T(8,128)(2,1)S(1)} collective-permute-done((bf16[384,1152]{1,0:T(8,128)(2,1)S(1)}, bf16[384,1152]{1,0:T(8,128)(2,1)S(1)}, u32[]{:S(2)}, u32[]{:S(2)}) %collective-permute-start.46) | collective-permute-done | bytes 884768 | tf_op jit(solution)/shard_map/ppermute | solution.py:81
  264.0 6.3 collective-permute-done.21
  280.6 20.9 %collective-permute-done.22 = bf16[384,1536]{1,0:T(8,128)(2,1)S(1)} collective-permute-done((bf16[384,1536]{1,0:T(8,128)(2,1)S(1)}, bf16[384,1536]{1,0:T(8,128)(2,1)S(1)}, u32[]{:S(2)}, u32[]{:S(2)}) %collective-permute-start.22) | collective-permute-done | bytes 1179680 | tf_op jit(solution)/shard_map/ppermute | solution.py:47
  301.9 11.5 %fusion.66 = f32[1536,1152]{1,0:T(8,128)} fusion(bf16[1536,1152]{1,0:T(8,128)(2,1)S(1)} %bitcast.533, bf16[384,1536]{1,0:T(8,128)(2,1)S(1)} %collective-permute-done.54, bf16[384,1536]{1,0:T(8,128)(2,1)S(1)} %collective-permute-done.53, bf16[384,1536]{1,0:T(8,128)(2,1)S(1)} %collective-permute-done.52, bf16[384,1536]{1,0:T(8,128)(2,1)S(1)} %bitcast.554), kind=kOutput, calls=%fused_computation.217 | convolution fusion | flops 5454692352 | bytes 15335424 | tf_op jit(solution)/shard_map/dot_general | solution.py:31
  313.4 11.4 %fusion.133 = f32[1536,1152]{1,0:T(8,128)} fusion(bf16[1536,1152]{1,0:T(8,128)(2,1)S(1)} %bitcast.537, bf16[384,1536]{1,0:T(8,128)(2,1)S(1)} %collective-permute-done.24, bf16[384,1536]{1,0:T(8,128)(2,1)S(1)} %collective-permute-done.23, bf16[384,1536]{1,0:T(8,128)(2,1)S(1)} %collective-permute-done.22, bf16[384,1536]{1,0:T(8,128)(2,1)S(1)} %multiply_convert_fusion.3), kind=kOutput, calls=%fused_computation.403 | convolution fusion | flops 5454692352 | bytes 15335424 | tf_op jit(solution)/shard_map/dot_general | solution.py:31
  324.8 16.8 %multiply_convert_fusion.1 = (bf16[1536,1152]{1,0:T(8,128)(2,1)}, bf16[1536,1152]{1,0:T(8,128)(2,1)}, bf16[1536,1152]{1,0:T(8,128)(2,1)}) fusion(f32[1536,1152]{1,0:T(8,128)} %fusion.66, f32[1536,1152]{1,0:T(8,128)} %fusion.133, bf16[1536,1152]{1,0:T(8,128)(2,1)S(1)} %bitcast.535, bf16[384,1536]{1,0:T(8,128)(2,1)} %copy-done.73, ...), kind=kOutput, calls=%fused_computation.5 | convolution fusion | flops 5481234432 | bytes 33030144 | tf_op jit(solution)/shard_map/dot_general | solution.py:31
  341.6 9.3 %convolution_convert_fusion = bf16[1536,1152]{1,0:T(8,128)(2,1)S(1)} fusion(bf16[1536,1152]{1,0:T(8,128)(2,1)} %get-tuple-element.26, bf16[384,1536]{1,0:T(8,128)(2,1)} %copy-done.68, bf16[384,1536]{1,0:T(8,128)(2,1)} %copy-done.67, bf16[384,1536]{1,0:T(8,128)(2,1)} %copy-done.66, bf16[384,1536]{1,0:T(8,128)(2,1)S(1)} %bitcast.555), kind=kOutput, calls=%fused_computation.1 | convolution fusion | flops 5456461824 | bytes 11796480 | tf_op jit(solution)/shard_map/dot_general | solution.py:35
  352.3 16.8 %collective-permute-start.100 = (bf16[384,1152]{1,0:T(8,128)(2,1)}, bf16[384,1152]{1,0:T(8,128)(2,1)S(1)}, u32[]{:S(2)}, u32[]{:S(2)}) collective-permute-start(bf16[384,1152]{1,0:T(8,128)(2,1)} %get-tuple-element.29), channel_id=1, source_target_pairs={{0,8},{1,9},{2,10},{3,11},{4,12},{5,13},{6,14},{7,15}} | collective-permute-start | bytes 2654216 | tf_op jit(solution)/shard_map/ppermute | solution.py:106
  370.7 9.1 %fusion.147 = f32[1536,1536]{1,0:T(8,128)} fusion(bf16[1536,1152]{1,0:T(8,128)(2,1)S(1)} %copy-done.76, bf16[1536,1152]{1,0:T(8,128)(2,1)S(1)} %bitcast.538), kind=kOutput, calls=%fused_computation.417 | convolution fusion | flops 5435817984 | bytes 16515072 | tf_op jit(solution)/shard_map/dot_general | solution.py:41
  379.8 6.8 convolution_convert_fusion.1
  392.0 6.8 convolution_convert_fusion.2
  402.3 11.1 %convolution_add_fusion = f32[1536,1536]{1,0:T(8,128)S(1)} fusion(f32[1536,1536]{1,0:T(8,128)} %fusion.147, bf16[1536,1152]{1,0:T(8,128)(2,1)} %get-tuple-element.24, bf16[1536,1152]{1,0:T(8,128)(2,1)} %bitcast.536), kind=kOutput, calls=%fused_computation | convolution fusion | flops 5438177280 | bytes 25952256 | tf_op jit(solution)/shard_map/dot_general | solution.py:41
  413.4 9.5 %fusion.146 = f32[1536,1536]{1,0:T(8,128)S(1)} fusion(bf16[1536,1152]{1,0:T(8,128)(2,1)} %get-tuple-element.26, bf16[1536,1152]{1,0:T(8,128)(2,1)} %bitcast.534), kind=kOutput, calls=%fused_computation.416 | convolution fusion | flops 5435817984 | bytes 16515072 | tf_op jit(solution)/shard_map/dot_general | solution.py:41
  428.6 26.5 %collective-permute-start.93 = (bf16[384,1152]{1,0:T(8,128)(2,1)S(1)}, bf16[384,1152]{1,0:T(8,128)(2,1)S(1)}, u32[]{:S(2)}, u32[]{:S(2)}) collective-permute-start(bf16[384,1152]{1,0:T(8,128)(2,1)S(1)} %fusion.40), channel_id=1, source_target_pairs={{0,8},{8,16},{1,9},{9,17},{2,10},{10,18},{3,11},{11,19},{4,12},{12... | collective-permute-start | bytes 2654216 | tf_op jit(solution)/shard_map/ppermute | solution.py:106
  457.4 16.3 %collective-permute-start.85 = (bf16[384,1152]{1,0:T(8,128)(2,1)S(1)}, bf16[384,1152]{1,0:T(8,128)(2,1)S(1)}, u32[]{:S(2)}, u32[]{:S(2)}) collective-permute-start(bf16[384,1152]{1,0:T(8,128)(2,1)S(1)} %fusion.46), channel_id=1, source_target_pairs={{0,8},{8,16},{1,9},{9,17},{2,10},{10,18},{3,11},{11,19},{4,12},{12... | collective-permute-start | bytes 2654216 | tf_op jit(solution)/shard_map/ppermute | solution.py:106
  480.1 17.6 %collective-permute-start.102 = (bf16[384,1152]{1,0:T(8,128)(2,1)}, bf16[384,1152]{1,0:T(8,128)(2,1)}, u32[]{:S(2)}, u32[]{:S(2)}) collective-permute-start(bf16[384,1152]{1,0:T(8,128)(2,1)} %get-tuple-element.27), channel_id=1, source_target_pairs={{0,8},{8,16},{16,24},{1,9},{9,17},{17,25},{2,10},{10,18},{18,26},{... | collective-permute-start | bytes 2654216 | tf_op jit(solution)/shard_map/ppermute | solution.py:106
  502.3 14.5 %collective-permute-start.94 = (bf16[384,1152]{1,0:T(8,128)(2,1)}, bf16[384,1152]{1,0:T(8,128)(2,1)}, u32[]{:S(2)}, u32[]{:S(2)}) collective-permute-start(bf16[384,1152]{1,0:T(8,128)(2,1)} %get-tuple-element.31), channel_id=1, source_target_pairs={{0,8},{8,16},{16,24},{1,9},{9,17},{17,25},{2,10},{10,18},{18,26},{... | collective-permute-start | bytes 2654216 | tf_op jit(solution)/shard_map/ppermute | solution.py:106
  526.5 4.7 collective-permute-start.86
  538.7 17.8 %collective-permute-done.105 = bf16[384,1152]{1,0:T(8,128)(2,1)S(1)} collective-permute-done((bf16[384,1152]{1,0:T(8,128)(2,1)S(1)}, bf16[384,1152]{1,0:T(8,128)(2,1)S(1)}, u32[]{:S(2)}, u32[]{:S(2)}) %collective-permute-start.105) | collective-permute-done | bytes 884768 | tf_op jit(solution)/shard_map/ppermute | solution.py:107
  562.4 13.1 %collective-permute-done.97 = bf16[384,1152]{1,0:T(8,128)(2,1)S(1)} collective-permute-done((bf16[384,1152]{1,0:T(8,128)(2,1)S(1)}, bf16[384,1152]{1,0:T(8,128)(2,1)S(1)}, u32[]{:S(2)}, u32[]{:S(2)}) %collective-permute-start.97) | collective-permute-done | bytes 884768 | tf_op jit(solution)/shard_map/ppermute | solution.py:107
  575.5 21.1 %collective-permute-start.106 = (bf16[2,96,1152]{2,1,0:T(8,128)(2,1)S(1)}, bf16[2,96,1152]{2,1,0:T(8,128)(2,1)S(1)}, u32[]{:S(2)}, u32[]{:S(2)}) collective-permute-start(bf16[2,96,1152]{2,1,0:T(8,128)(2,1)S(1)} %dynamic-slice_bitcast_fusion.8), channel_id=1, source_target_pairs={{0,4},{4,0},{1,5},{5,1},{2,6},{6,2},{3,7},{7,3},{8,12},{12,8},{9,1... | collective-permute-start | bytes 1327112 | tf_op jit(solution)/shard_map/ppermute | solution.py:47
  598.2 5.8 collective-permute-start.98
  604.4 9.9 %collective-permute-start.90 = (bf16[2,96,1152]{2,1,0:T(8,128)(2,1)S(1)}, bf16[2,96,1152]{2,1,0:T(8,128)(2,1)S(1)}, u32[]{:S(2)}, u32[]{:S(2)}) collective-permute-start(bf16[2,96,1152]{2,1,0:T(8,128)(2,1)S(1)} %dynamic-slice_bitcast_fusion.10), channel_id=1, source_target_pairs={{0,4},{4,0},{1,5},{5,1},{2,6},{6,2},{3,7},{7,3},{8,12},{12,8},{9,1... | collective-permute-start | bytes 1327112 | tf_op jit(solution)/shard_map/ppermute | solution.py:47
  617.1 4.5 collective-permute-start.57
  622.5 5.4 collective-permute-done.90
  633.0 35.4 %collective-permute-done.57 = bf16[384,1536]{1,0:T(8,128)(2,1)S(1)} collective-permute-done((bf16[384,1536]{1,0:T(8,128)(2,1)S(1)}, bf16[384,1536]{1,0:T(8,128)(2,1)S(1)}, u32[]{:S(2)}, u32[]{:S(2)}) %collective-permute-start.57) | collective-permute-done | bytes 1179680 | tf_op jit(solution)/shard_map/ppermute | solution.py:47
  694.9 4.9 collective-permute-done.59
  701.6 9.0 %collective-permute-done.61 = bf16[2,192,256]{1,2,0:T(8,128)(2,1)S(1)} collective-permute-done((bf16[2,192,256]{1,2,0:T(8,128)(2,1)S(1)}, bf16[2,192,256]{1,2,0:T(8,128)(2,1)S(1)}, u32[]{:S(2)}, u32[]{:S(2)}) %collective-permute-start.61) | collective-permute-done | bytes 196640 | tf_op jit(solution)/shard_map/ppermute | solution.py:59
  734.9 17.4 %collective-permute-done.63 = bf16[384,1536]{1,0:T(8,128)(2,1)S(1)} collective-permute-done((bf16[384,1536]{1,0:T(8,128)(2,1)S(1)}, bf16[384,1536]{1,0:T(8,128)(2,1)S(1)}, u32[]{:S(2)}, u32[]{:S(2)}) %collective-permute-start.63) | collective-permute-done | bytes 1179680 | tf_op jit(solution)/shard_map/ppermute | solution.py:47
  758.5 9.9 %collective-permute-start.66 = (f32[4096]{0:T(1024)S(1)}, f32[4096]{0:T(1024)S(1)}, u32[]{:S(2)}, u32[]{:S(2)}) collective-permute-start(f32[4096]{0:T(1024)S(1)} %add.580), channel_id=1, source_target_pairs={{0,8},{2,10},{4,12},{6,14},{8,0},{10,2},{12,4},{14,6},{16,24},{18,... | collective-permute-start | bytes 49160 | tf_op jit(solution)/shard_map/ppermute | solution.py:66
  771.9 4.4 collective-permute-start.67
  789.2 11.8 %collective-permute-done.69 = bf16[4,96,1024]{2,1,0:T(8,128)(2,1)S(1)} collective-permute-done((bf16[4,96,1024]{2,1,0:T(8,128)(2,1)S(1)}, bf16[4,96,1024]{2,1,0:T(8,128)(2,1)S(1)}, u32[]{:S(2)}, u32[]{:S(2)}) %collective-permute-start.69) | collective-permute-done | bytes 786464 | tf_op jit(solution)/shard_map/ppermute | solution.py:47
  809.1 4.4 collective-permute-start.71
  819.8 5.6 collective-permute-start.72
  828.6 5.1 collective-permute-done.75
  (552 shorter events, 288.9 us)
Async XLA Ops:
  0.7 33.1 %collective-permute-start.14 = (bf16[96,768]{1,0:T(8,128)(2,1)}, bf16[96,768]{1,0:T(8,128)(2,1)}, u32[]{:S(2)}, u32[]{:S(2)}) collective-permute-start(bf16[96,768]{1,0:T(8,128)(2,1)} %bitcast.566), channel_id=1, source_target_pairs={{8,0},{16,8},{24,16},{9,1},{17,9},{25,17},{10,2},{18,10},{26,18},{... | collective-permute-start | bytes 442376 | tf_op jit(solution)/shard_map/ppermute | solution.py:81
  2.1 36.0 %collective-permute-start.13 = (bf16[96,768]{1,0:T(8,128)(2,1)}, bf16[96,768]{1,0:T(8,128)(2,1)}, u32[]{:S(2)}, u32[]{:S(2)}) collective-permute-start(bf16[96,768]{1,0:T(8,128)(2,1)} %bitcast.567), channel_id=1, source_target_pairs={{0,8},{8,16},{16,24},{1,9},{9,17},{17,25},{2,10},{10,18},{18,26},{... | collective-permute-start | bytes 442376 | tf_op jit(solution)/shard_map/ppermute | solution.py:78
  10.8 33.8 %collective-permute-start.1 = (bf16[96,1152]{1,0:T(8,128)(2,1)}, bf16[96,1152]{1,0:T(8,128)(2,1)}, u32[]{:S(2)}, u32[]{:S(2)}) collective-permute-start(bf16[96,1152]{1,0:T(8,128)(2,1)} %fusion.129), channel_id=1, source_target_pairs={{8,0},{16,8},{24,16},{9,1},{17,9},{25,17},{10,2},{18,10},{26,18},{... | collective-permute-start | bytes 663560 | tf_op jit(solution)/shard_map/ppermute | solution.py:81
  12.1 32.8 %collective-permute-start = (bf16[96,1152]{1,0:T(8,128)(2,1)}, bf16[96,1152]{1,0:T(8,128)(2,1)}, u32[]{:S(2)}, u32[]{:S(2)}) collective-permute-start(bf16[96,1152]{1,0:T(8,128)(2,1)} %fusion.129), channel_id=1, source_target_pairs={{0,8},{8,16},{16,24},{1,9},{9,17},{17,25},{2,10},{10,18},{18,26},{... | collective-permute-start | bytes 663560 | tf_op jit(solution)/shard_map/ppermute | solution.py:78
  51.8 49.8 %collective-permute-start.19 = (bf16[4,96,768]{2,1,0:T(8,128)(2,1)S(1)}, bf16[4,96,768]{2,1,0:T(8,128)(2,1)S(1)}, u32[]{:S(2)}, u32[]{:S(2)}) collective-permute-start(bf16[4,96,768]{2,1,0:T(8,128)(2,1)S(1)} %bitcast_dynamic-update-slice_fusion.16), channel_id=1, source_target_pairs={{0,4},{4,0},{1,5},{5,1},{2,6},{6,2},{3,7},{7,3},{8,12},{12,8},{9,1... | collective-permute-start | bytes 1769480 | tf_op jit(solution)/shard_map/ppermute | solution.py:47
  62.8 33.0 %collective-permute-start.42 = (bf16[2,96,1152]{2,1,0:T(8,128)(2,1)S(1)}, bf16[2,96,1152]{2,1,0:T(8,128)(2,1)S(1)}, u32[]{:S(2)}, u32[]{:S(2)}) collective-permute-start(bf16[2,96,1152]{2,1,0:T(8,128)(2,1)S(1)} %fusion.91), channel_id=1, source_target_pairs={{0,2},{2,0},{1,3},{3,1},{4,6},{6,4},{5,7},{7,5},{8,10},{10,8},{9,1... | collective-permute-start | bytes 1327112 | tf_op jit(solution)/shard_map/ppermute | solution.py:47
  74.3 46.2 %collective-permute-start.28 = (bf16[384,1152]{1,0:T(8,128)(2,1)}, bf16[384,1152]{1,0:T(8,128)(2,1)}, u32[]{:S(2)}, u32[]{:S(2)}) collective-permute-start(bf16[384,1152]{1,0:T(8,128)(2,1)} %bitcast.58), channel_id=1, source_target_pairs={{8,0},{16,8},{24,16},{9,1},{17,9},{25,17},{10,2},{18,10},{26,18},{... | collective-permute-start | bytes 2654216 | tf_op jit(solution)/shard_map/ppermute | solution.py:81
  77.1 65.1 %collective-permute-start.27 = (bf16[384,1152]{1,0:T(8,128)(2,1)}, bf16[384,1152]{1,0:T(8,128)(2,1)}, u32[]{:S(2)}, u32[]{:S(2)}) collective-permute-start(bf16[384,1152]{1,0:T(8,128)(2,1)} %bitcast.58), channel_id=1, source_target_pairs={{0,8},{8,16},{16,24},{1,9},{9,17},{17,25},{2,10},{10,18},{18,26},{... | collective-permute-start | bytes 2654216 | tf_op jit(solution)/shard_map/ppermute | solution.py:78
  95.8 53.5 %collective-permute-start.36 = (bf16[384,1152]{1,0:T(8,128)(2,1)}, bf16[384,1152]{1,0:T(8,128)(2,1)}, u32[]{:S(2)}, u32[]{:S(2)}) collective-permute-start(bf16[384,1152]{1,0:T(8,128)(2,1)} %bitcast.68), channel_id=1, source_target_pairs={{8,0},{16,8},{24,16},{9,1},{17,9},{25,17},{10,2},{18,10},{26,18},{... | collective-permute-start | bytes 2654216 | tf_op jit(solution)/shard_map/ppermute | solution.py:81
  121.4 28.7 %collective-permute-start.44 = (bf16[384,1152]{1,0:T(8,128)(2,1)S(1)}, bf16[384,1152]{1,0:T(8,128)(2,1)S(1)}, u32[]{:S(2)}, u32[]{:S(2)}) collective-permute-start(bf16[384,1152]{1,0:T(8,128)(2,1)S(1)} %bitcast.531), channel_id=1, source_target_pairs={{8,0},{16,8},{24,16},{9,1},{17,9},{25,17},{10,2},{18,10},{26,18},{... | collective-permute-start | bytes 2654216 | tf_op jit(solution)/shard_map/ppermute | solution.py:81
  122.8 42.4 %collective-permute-start.29 = (bf16[384,1152]{1,0:T(8,128)(2,1)}, bf16[384,1152]{1,0:T(8,128)(2,1)S(1)}, u32[]{:S(2)}, u32[]{:S(2)}) collective-permute-start(bf16[384,1152]{1,0:T(8,128)(2,1)} %collective-permute-done.28), channel_id=1, source_target_pairs={{8,0},{16,8},{9,1},{17,9},{10,2},{18,10},{11,3},{19,11},{12,4},{20... | collective-permute-start | bytes 2654216 | tf_op jit(solution)/shard_map/ppermute | solution.py:81
  140.9 25.7 %collective-permute-start.12 = (bf16[2,192,256]{2,1,0:T(8,128)(2,1)S(1)}, bf16[2,192,256]{2,1,0:T(8,128)(2,1)S(1)}, u32[]{:S(2)}, u32[]{:S(2)}) collective-permute-start(bf16[2,192,256]{2,1,0:T(8,128)(2,1)S(1)} %pad_maximum_fusion.25), channel_id=1, source_target_pairs={{0,2},{2,4},{4,6},{6,8},{8,10},{10,12},{12,14},{14,16},{16,18},{18... | collective-permute-start | bytes 589832 | tf_op jit(solution)/shard_map/ppermute | solution.py:59
  142.2 80.7 %collective-permute-start.35 = (bf16[384,1152]{1,0:T(8,128)(2,1)}, bf16[384,1152]{1,0:T(8,128)(2,1)S(1)}, u32[]{:S(2)}, u32[]{:S(2)}) collective-permute-start(bf16[384,1152]{1,0:T(8,128)(2,1)} %bitcast.68), channel_id=1, source_target_pairs={{0,8},{8,16},{16,24},{1,9},{9,17},{17,25},{2,10},{10,18},{18,26},{... | collective-permute-start | bytes 2654216 | tf_op jit(solution)/shard_map/ppermute | solution.py:78
  149.4 79.4 %collective-permute-start.31 = (bf16[384,1152]{1,0:T(8,128)(2,1)}, bf16[384,1152]{1,0:T(8,128)(2,1)S(1)}, u32[]{:S(2)}, u32[]{:S(2)}) collective-permute-start(bf16[384,1152]{1,0:T(8,128)(2,1)} %collective-permute-done.27), channel_id=1, source_target_pairs={{8,16},{16,24},{9,17},{17,25},{10,18},{18,26},{11,19},{19,27},{12,... | collective-permute-start | bytes 2654216 | tf_op jit(solution)/shard_map/ppermute | solution.py:78
  150.1 34.1 %collective-permute-start.37 = (bf16[384,1152]{1,0:T(8,128)(2,1)}, bf16[384,1152]{1,0:T(8,128)(2,1)S(1)}, u32[]{:S(2)}, u32[]{:S(2)}) collective-permute-start(bf16[384,1152]{1,0:T(8,128)(2,1)} %collective-permute-done.36), channel_id=1, source_target_pairs={{8,0},{16,8},{9,1},{17,9},{10,2},{18,10},{11,3},{19,11},{12,4},{20... | collective-permute-start | bytes 2654216 | tf_op jit(solution)/shard_map/ppermute | solution.py:81
  165.2 64.2 %collective-permute-start.45 = (bf16[384,1152]{1,0:T(8,128)(2,1)S(1)}, bf16[384,1152]{1,0:T(8,128)(2,1)S(1)}, u32[]{:S(2)}, u32[]{:S(2)}) collective-permute-start(bf16[384,1152]{1,0:T(8,128)(2,1)S(1)} %collective-permute-done.44), channel_id=1, source_target_pairs={{8,0},{16,8},{9,1},{17,9},{10,2},{18,10},{11,3},{19,11},{12,4},{20... | collective-permute-start | bytes 2654216 | tf_op jit(solution)/shard_map/ppermute | solution.py:81
  166.5 54.8 %collective-permute-start.30 = (bf16[384,1152]{1,0:T(8,128)(2,1)S(1)}, bf16[384,1152]{1,0:T(8,128)(2,1)S(1)}, u32[]{:S(2)}, u32[]{:S(2)}) collective-permute-start(bf16[384,1152]{1,0:T(8,128)(2,1)S(1)} %collective-permute-done.29), channel_id=1, source_target_pairs={{8,0},{9,1},{10,2},{11,3},{12,4},{13,5},{14,6},{15,7}} | collective-permute-start | bytes 2654216 | tf_op jit(solution)/shard_map/ppermute | solution.py:81
  184.2 63.4 %collective-permute-start.52 = (bf16[384,1536]{1,0:T(8,128)(2,1)S(1)}, bf16[384,1536]{1,0:T(8,128)(2,1)S(1)}, u32[]{:S(2)}, u32[]{:S(2)}) collective-permute-start(bf16[384,1536]{1,0:T(8,128)(2,1)S(1)} %bitcast.552), channel_id=1, source_target_pairs={{0,4},{4,0},{1,5},{5,1},{2,6},{6,2},{3,7},{7,3},{8,12},{12,8},{9,1... | collective-permute-start | bytes 3538952 | tf_op jit(solution)/shard_map/ppermute | solution.py:47
  229.5 33.6 %collective-permute-start.46 = (bf16[384,1152]{1,0:T(8,128)(2,1)S(1)}, bf16[384,1152]{1,0:T(8,128)(2,1)S(1)}, u32[]{:S(2)}, u32[]{:S(2)}) collective-permute-start(bf16[384,1152]{1,0:T(8,128)(2,1)S(1)} %collective-permute-done.45), channel_id=1, source_target_pairs={{8,0},{9,1},{10,2},{11,3},{12,4},{13,5},{14,6},{15,7}} | collective-permute-start | bytes 2654216 | tf_op jit(solution)/shard_map/ppermute | solution.py:81
  247.6 54.2 %collective-permute-start.53 = (bf16[384,1536]{1,0:T(8,128)(2,1)S(1)}, bf16[384,1536]{1,0:T(8,128)(2,1)S(1)}, u32[]{:S(2)}, u32[]{:S(2)}) collective-permute-start(bf16[384,1536]{1,0:T(8,128)(2,1)S(1)} %bitcast.553), channel_id=1, source_target_pairs={{0,2},{2,0},{1,3},{3,1},{4,6},{6,4},{5,7},{7,5},{8,10},{10,8},{9,1... | collective-permute-start | bytes 3538952 | tf_op jit(solution)/shard_map/ppermute | solution.py:47
  247.7 54.1 %collective-permute-start.54 = (bf16[384,1536]{1,0:T(8,128)(2,1)S(1)}, bf16[384,1536]{1,0:T(8,128)(2,1)S(1)}, u32[]{:S(2)}, u32[]{:S(2)}) collective-permute-start(bf16[384,1536]{1,0:T(8,128)(2,1)S(1)} %collective-permute-done.52), channel_id=1, source_target_pairs={{0,2},{2,0},{1,3},{3,1},{4,6},{6,4},{5,7},{7,5},{8,10},{10,8},{9,1... | collective-permute-start | bytes 3538952 | tf_op jit(solution)/shard_map/ppermute | solution.py:47
  271.9 29.6 %collective-permute-start.22 = (bf16[384,1536]{1,0:T(8,128)(2,1)S(1)}, bf16[384,1536]{1,0:T(8,128)(2,1)S(1)}, u32[]{:S(2)}, u32[]{:S(2)}) collective-permute-start(bf16[384,1536]{1,0:T(8,128)(2,1)S(1)} %multiply_convert_fusion.3), channel_id=1, source_target_pairs={{0,4},{4,0},{1,5},{5,1},{2,6},{6,2},{3,7},{7,3},{8,12},{12,8},{9,1... | collective-permute-start | bytes 3538952 | tf_op jit(solution)/shard_map/ppermute | solution.py:47
  275.8 25.7 %collective-permute-start.48 = (bf16[384,1152]{1,0:T(8,128)(2,1)S(1)}, bf16[384,1152]{1,0:T(8,128)(2,1)S(1)}, u32[]{:S(2)}, u32[]{:S(2)}) collective-permute-start(bf16[384,1152]{1,0:T(8,128)(2,1)S(1)} %collective-permute-done.47), channel_id=1, source_target_pairs={{16,24},{17,25},{18,26},{19,27},{20,28},{21,29},{22,30},{23,31}} | collective-permute-start | bytes 2654216 | tf_op jit(solution)/shard_map/ppermute | solution.py:78
  280.5 32.9 %collective-permute-start.23 = (bf16[384,1536]{1,0:T(8,128)(2,1)S(1)}, bf16[384,1536]{1,0:T(8,128)(2,1)S(1)}, u32[]{:S(2)}, u32[]{:S(2)}) collective-permute-start(bf16[384,1536]{1,0:T(8,128)(2,1)S(1)} %multiply_convert_fusion.3), channel_id=1, source_target_pairs={{0,2},{2,0},{1,3},{3,1},{4,6},{6,4},{5,7},{7,5},{8,10},{10,8},{9,1... | collective-permute-start | bytes 3538952 | tf_op jit(solution)/shard_map/ppermute | solution.py:47
  352.3 71.3 %collective-permute-start.100 = (bf16[384,1152]{1,0:T(8,128)(2,1)}, bf16[384,1152]{1,0:T(8,128)(2,1)S(1)}, u32[]{:S(2)}, u32[]{:S(2)}) collective-permute-start(bf16[384,1152]{1,0:T(8,128)(2,1)} %get-tuple-element.29), channel_id=1, source_target_pairs={{0,8},{1,9},{2,10},{3,11},{4,12},{5,13},{6,14},{7,15}} | collective-permute-start | bytes 2654216 | tf_op jit(solution)/shard_map/ppermute | solution.py:106
  369.0 87.5 %collective-permute-start.103 = (bf16[384,1152]{1,0:T(8,128)(2,1)}, bf16[384,1152]{1,0:T(8,128)(2,1)}, u32[]{:S(2)}, u32[]{:S(2)}) collective-permute-start(bf16[384,1152]{1,0:T(8,128)(2,1)} %get-tuple-element.30), channel_id=1, source_target_pairs={{24,16},{25,17},{26,18},{27,19},{28,20},{29,21},{30,22},{31,23}} | collective-permute-start | bytes 2654216 | tf_op jit(solution)/shard_map/ppermute | solution.py:107
  388.0 36.1 %collective-permute-start.92 = (bf16[384,1152]{1,0:T(8,128)(2,1)}, bf16[384,1152]{1,0:T(8,128)(2,1)}, u32[]{:S(2)}, u32[]{:S(2)}) collective-permute-start(bf16[384,1152]{1,0:T(8,128)(2,1)} %get-tuple-element.33), channel_id=1, source_target_pairs={{0,8},{1,9},{2,10},{3,11},{4,12},{5,13},{6,14},{7,15}} | collective-permute-start | bytes 2654216 | tf_op jit(solution)/shard_map/ppermute | solution.py:106
  390.4 66.9 %collective-permute-start.95 = (bf16[384,1152]{1,0:T(8,128)(2,1)}, bf16[384,1152]{1,0:T(8,128)(2,1)}, u32[]{:S(2)}, u32[]{:S(2)}) collective-permute-start(bf16[384,1152]{1,0:T(8,128)(2,1)} %get-tuple-element.34), channel_id=1, source_target_pairs={{24,16},{25,17},{26,18},{27,19},{28,20},{29,21},{30,22},{31,23}} | collective-permute-start | bytes 2654216 | tf_op jit(solution)/shard_map/ppermute | solution.py:107
  400.1 28.6 %collective-permute-start.84 = (bf16[384,1152]{1,0:T(8,128)(2,1)}, bf16[384,1152]{1,0:T(8,128)(2,1)}, u32[]{:S(2)}, u32[]{:S(2)}) collective-permute-start(bf16[384,1152]{1,0:T(8,128)(2,1)} %get-tuple-element.37), channel_id=1, source_target_pairs={{0,8},{1,9},{2,10},{3,11},{4,12},{5,13},{6,14},{7,15}} | collective-permute-start | bytes 2654216 | tf_op jit(solution)/shard_map/ppermute | solution.py:106
  423.6 77.4 %collective-permute-start.49 = (bf16[768,1536]{1,0:T(8,128)(2,1)S(1)}, bf16[768,1536]{1,0:T(8,128)(2,1)S(1)}, u32[]{:S(2)}, u32[]{:S(2)}) collective-permute-start(bf16[768,1536]{1,0:T(8,128)(2,1)S(1)} %slice.447), channel_id=1, source_target_pairs={{0,2},{2,0},{1,3},{3,1},{4,6},{6,4},{5,7},{7,5},{8,10},{10,8},{9,1... | collective-permute-start | bytes 7077896 | tf_op jit(solution)/shard_map/ppermute | solution.py:47
  424.1 33.3 %collective-permute-start.101 = (bf16[384,1152]{1,0:T(8,128)(2,1)S(1)}, bf16[384,1152]{1,0:T(8,128)(2,1)S(1)}, u32[]{:S(2)}, u32[]{:S(2)}) collective-permute-start(bf16[384,1152]{1,0:T(8,128)(2,1)S(1)} %fusion.34), channel_id=1, source_target_pairs={{0,8},{8,16},{1,9},{9,17},{2,10},{10,18},{3,11},{11,19},{4,12},{12... | collective-permute-start | bytes 2654216 | tf_op jit(solution)/shard_map/ppermute | solution.py:106
  428.6 47.9 %collective-permute-start.93 = (bf16[384,1152]{1,0:T(8,128)(2,1)S(1)}, bf16[384,1152]{1,0:T(8,128)(2,1)S(1)}, u32[]{:S(2)}, u32[]{:S(2)}) collective-permute-start(bf16[384,1152]{1,0:T(8,128)(2,1)S(1)} %fusion.40), channel_id=1, source_target_pairs={{0,8},{8,16},{1,9},{9,17},{2,10},{10,18},{3,11},{11,19},{4,12},{12... | collective-permute-start | bytes 2654216 | tf_op jit(solution)/shard_map/ppermute | solution.py:106
  457.3 63.3 %collective-permute-start.55 = (bf16[768,1536]{1,0:T(8,128)(2,1)S(1)}, bf16[768,1536]{1,0:T(8,128)(2,1)S(1)}, u32[]{:S(2)}, u32[]{:S(2)}) collective-permute-start(bf16[768,1536]{1,0:T(8,128)(2,1)S(1)} %slice.446), channel_id=1, source_target_pairs={{0,2},{2,0},{1,3},{3,1},{4,6},{6,4},{5,7},{7,5},{8,10},{10,8},{9,1... | collective-permute-start | bytes 7077896 | tf_op jit(solution)/shard_map/ppermute | solution.py:47
  457.4 40.3 %collective-permute-start.85 = (bf16[384,1152]{1,0:T(8,128)(2,1)S(1)}, bf16[384,1152]{1,0:T(8,128)(2,1)S(1)}, u32[]{:S(2)}, u32[]{:S(2)}) collective-permute-start(bf16[384,1152]{1,0:T(8,128)(2,1)S(1)} %fusion.46), channel_id=1, source_target_pairs={{0,8},{8,16},{1,9},{9,17},{2,10},{10,18},{3,11},{11,19},{4,12},{12... | collective-permute-start | bytes 2654216 | tf_op jit(solution)/shard_map/ppermute | solution.py:106
  476.5 49.1 %collective-permute-start.104 = (bf16[384,1152]{1,0:T(8,128)(2,1)}, bf16[384,1152]{1,0:T(8,128)(2,1)S(1)}, u32[]{:S(2)}, u32[]{:S(2)}) collective-permute-start(bf16[384,1152]{1,0:T(8,128)(2,1)} %get-tuple-element.28), channel_id=1, source_target_pairs={{16,8},{24,16},{17,9},{25,17},{18,10},{26,18},{19,11},{27,19},{20,... | collective-permute-start | bytes 2654216 | tf_op jit(solution)/shard_map/ppermute | solution.py:107
  480.1 55.6 %collective-permute-start.102 = (bf16[384,1152]{1,0:T(8,128)(2,1)}, bf16[384,1152]{1,0:T(8,128)(2,1)}, u32[]{:S(2)}, u32[]{:S(2)}) collective-permute-start(bf16[384,1152]{1,0:T(8,128)(2,1)} %get-tuple-element.27), channel_id=1, source_target_pairs={{0,8},{8,16},{16,24},{1,9},{9,17},{17,25},{2,10},{10,18},{18,26},{... | collective-permute-start | bytes 2654216 | tf_op jit(solution)/shard_map/ppermute | solution.py:106
  497.7 33.8 %collective-permute-start.96 = (bf16[384,1152]{1,0:T(8,128)(2,1)}, bf16[384,1152]{1,0:T(8,128)(2,1)}, u32[]{:S(2)}, u32[]{:S(2)}) collective-permute-start(bf16[384,1152]{1,0:T(8,128)(2,1)} %get-tuple-element.32), channel_id=1, source_target_pairs={{16,8},{24,16},{17,9},{25,17},{18,10},{26,18},{19,11},{27,19},{20,... | collective-permute-start | bytes 2654216 | tf_op jit(solution)/shard_map/ppermute | solution.py:107
  502.3 57.1 %collective-permute-start.94 = (bf16[384,1152]{1,0:T(8,128)(2,1)}, bf16[384,1152]{1,0:T(8,128)(2,1)}, u32[]{:S(2)}, u32[]{:S(2)}) collective-permute-start(bf16[384,1152]{1,0:T(8,128)(2,1)} %get-tuple-element.31), channel_id=1, source_target_pairs={{0,8},{8,16},{16,24},{1,9},{9,17},{17,25},{2,10},{10,18},{18,26},{... | collective-permute-start | bytes 2654216 | tf_op jit(solution)/shard_map/ppermute | solution.py:106
  526.5 71.7 %collective-permute-start.86 = (bf16[384,1152]{1,0:T(8,128)(2,1)S(1)}, bf16[384,1152]{1,0:T(8,128)(2,1)S(1)}, u32[]{:S(2)}, u32[]{:S(2)}) collective-permute-start(bf16[384,1152]{1,0:T(8,128)(2,1)S(1)} %copy-done.48), channel_id=1, source_target_pairs={{0,8},{8,16},{16,24},{1,9},{9,17},{17,25},{2,10},{10,18},{18,26},{... | collective-permute-start | bytes 2654216 | tf_op jit(solution)/shard_map/ppermute | solution.py:106
  534.2 41.3 %collective-permute-start.97 = (bf16[384,1152]{1,0:T(8,128)(2,1)S(1)}, bf16[384,1152]{1,0:T(8,128)(2,1)S(1)}, u32[]{:S(2)}, u32[]{:S(2)}) collective-permute-start(bf16[384,1152]{1,0:T(8,128)(2,1)S(1)} %fusion.39), channel_id=1, source_target_pairs={{8,0},{16,8},{24,16},{9,1},{17,9},{25,17},{10,2},{18,10},{26,18},{... | collective-permute-start | bytes 2654216 | tf_op jit(solution)/shard_map/ppermute | solution.py:107
  535.7 78.6 %collective-permute-start.50 = (bf16[384,1536]{1,0:T(8,128)(2,1)S(1)}, bf16[384,1536]{1,0:T(8,128)(2,1)S(1)}, u32[]{:S(2)}, u32[]{:S(2)}) collective-permute-start(bf16[384,1536]{1,0:T(8,128)(2,1)S(1)} %slice.449), channel_id=1, source_target_pairs={{0,4},{4,0},{1,5},{5,1},{2,6},{6,2},{3,7},{7,3},{8,12},{12,8},{9,1... | collective-permute-start | bytes 3538952 | tf_op jit(solution)/shard_map/ppermute | solution.py:47
  556.6 47.4 %collective-permute-start.89 = (bf16[384,1152]{1,0:T(8,128)(2,1)S(1)}, bf16[384,1152]{1,0:T(8,128)(2,1)S(1)}, u32[]{:S(2)}, u32[]{:S(2)}) collective-permute-start(bf16[384,1152]{1,0:T(8,128)(2,1)S(1)} %fusion.45), channel_id=1, source_target_pairs={{8,0},{16,8},{24,16},{9,1},{17,9},{25,17},{10,2},{18,10},{26,18},{... | collective-permute-start | bytes 2654216 | tf_op jit(solution)/shard_map/ppermute | solution.py:107
  559.4 57.3 %collective-permute-start.56 = (bf16[384,1536]{1,0:T(8,128)(2,1)S(1)}, bf16[384,1536]{1,0:T(8,128)(2,1)S(1)}, u32[]{:S(2)}, u32[]{:S(2)}) collective-permute-start(bf16[384,1536]{1,0:T(8,128)(2,1)S(1)} %slice.448), channel_id=1, source_target_pairs={{0,4},{4,0},{1,5},{5,1},{2,6},{6,2},{3,7},{7,3},{8,12},{12,8},{9,1... | collective-permute-start | bytes 3538952 | tf_op jit(solution)/shard_map/ppermute | solution.py:47
  575.5 46.0 %collective-permute-start.106 = (bf16[2,96,1152]{2,1,0:T(8,128)(2,1)S(1)}, bf16[2,96,1152]{2,1,0:T(8,128)(2,1)S(1)}, u32[]{:S(2)}, u32[]{:S(2)}) collective-permute-start(bf16[2,96,1152]{2,1,0:T(8,128)(2,1)S(1)} %dynamic-slice_bitcast_fusion.8), channel_id=1, source_target_pairs={{0,4},{4,0},{1,5},{5,1},{2,6},{6,2},{3,7},{7,3},{8,12},{12,8},{9,1... | collective-permute-start | bytes 1327112 | tf_op jit(solution)/shard_map/ppermute | solution.py:47
  614.7 54.7 %collective-permute-start.51 = (bf16[384,1536]{1,0:T(8,128)(2,1)S(1)}, bf16[384,1536]{1,0:T(8,128)(2,1)S(1)}, u32[]{:S(2)}, u32[]{:S(2)}) collective-permute-start(bf16[384,1536]{1,0:T(8,128)(2,1)S(1)} %fusion.56), channel_id=1, source_target_pairs={{0,1},{1,0},{2,3},{3,2},{4,5},{5,4},{6,7},{7,6},{8,9},{9,8},{10,11... | collective-permute-start | bytes 3538952 | tf_op jit(solution)/shard_map/ppermute | solution.py:47
  617.1 51.3 %collective-permute-start.57 = (bf16[384,1536]{1,0:T(8,128)(2,1)S(1)}, bf16[384,1536]{1,0:T(8,128)(2,1)S(1)}, u32[]{:S(2)}, u32[]{:S(2)}) collective-permute-start(bf16[384,1536]{1,0:T(8,128)(2,1)S(1)} %fusion.57), channel_id=1, source_target_pairs={{0,1},{1,0},{2,3},{3,2},{4,5},{5,4},{6,7},{7,6},{8,9},{9,8},{10,11... | collective-permute-start | bytes 3538952 | tf_op jit(solution)/shard_map/ppermute | solution.py:47
  734.8 46.7 %collective-permute-start.68 = (bf16[4,2,96,1024]{3,2,0,1:T(8,128)(2,1)S(1)}, bf16[4,2,96,1024]{3,2,0,1:T(8,128)(2,1)S(1)}, u32[]{:S(2)}, u32[]{:S(2)}) collective-permute-start(bf16[4,2,96,1024]{3,2,0,1:T(8,128)(2,1)S(1)} %bitcast.551), channel_id=1, source_target_pairs={{0,2},{2,0},{1,3},{3,1},{4,6},{6,4},{5,7},{7,5},{8,10},{10,8},{9,1... | collective-permute-start | bytes 4718600 | tf_op jit(solution)/shard_map/ppermute | solution.py:47
  755.0 29.8 %collective-permute-start.77 = (bf16[4,96,768]{2,1,0:T(8,128)(2,1)S(1)}, bf16[4,96,768]{2,1,0:T(8,128)(2,1)S(1)}, u32[]{:S(2)}, u32[]{:S(2)}) collective-permute-start(bf16[4,96,768]{2,1,0:T(8,128)(2,1)S(1)} %dynamic-slice_bitcast_fusion.7), channel_id=1, source_target_pairs={{0,4},{4,0},{1,5},{5,1},{2,6},{6,2},{3,7},{7,3},{8,12},{12,8},{9,1... | collective-permute-start | bytes 1769480 | tf_op jit(solution)/shard_map/ppermute | solution.py:47
  (141 other events, 2087.6 us)

commit v2 on v1

--- a/solution.py
+++ b/solution.py
@@ -1,14 +1,18 @@
+import functools
 import math
 
 import jax
 import jax.numpy as jnp
 from jax import lax
+from jax.experimental import pallas as pl
+from jax.experimental.pallas import tpu as pltpu
 from jax.sharding import Mesh
 from jax.sharding import PartitionSpec as P
 
 BACK = 5
 LINE = 4
 LANES = 128
+VMEM_BYTES = 56 * 1024 * 1024
 
 EPSILON = 1e-06
 THETA = 1000000.0
@@ -149,7 +153,9 @@
 def quarter_to_owner(grad):
     pair, core = lax.axis_index(PAIR), lax.axis_index(CORE)
     width = grad.shape[1]
-    block = low(line_scatter(grad.reshape(lax.axis_size(RING), -1, width)))
+    block = lax.psum_scatter(
+        grad.reshape(lax.axis_size(RING), -1, width), RING, scatter_dimension=0, tiled=False
+    )
     block = block.reshape(2, 2, -1, width)
 
     def halved(value, axis, place):
@@ -236,6 +242,14 @@
     return low(mixed.reshape(query_rows.shape[0], -1)), log_total
 
 
+def log_total_of(query_rows, key_rows, allowed):
+    scores = jnp.einsum("thd,sd->hts", query_rows, key_rows, preferred_element_type=jnp.float32)
+    scores = scores * (1.0 / math.sqrt(query_rows.shape[-1]))
+    scores = jnp.where(allowed, scores, NEGATIVE)
+    row_max = jnp.max(scores, axis=-1, keepdims=True)
+    return row_max + jnp.log(jnp.sum(jnp.exp(scores - row_max), axis=-1, keepdims=True))
+
+
 def attend_back(grad_heads, query_rows, key_rows, value_rows, allowed, log_total):
     scale = 1.0 / math.sqrt(query_rows.shape[-1])
     scores = jnp.einsum("thd,sd->hts", query_rows, key_rows, preferred_element_type=jnp.float32)
@@ -255,6 +269,510 @@
         "hts,thd->sd", low(probs), grad_heads, preferred_element_type=jnp.float32
     )
     return grad_query * scale, grad_keys * scale, grad_values
+
+
+def device(**coordinates):
+    return {name: place for name, place in coordinates.items()}
+
+
+class Copies:
+    def __init__(self, send_sems, recv_sems):
+        self.send_sems, self.recv_sems = send_sems, recv_sems
+        self.used = 0
+        self.sent = []
+
+    def new(self):
+        self.used += 1
+        return self.used - 1
+
+    def _make(self, which, source, target, to):
+        return pltpu.make_async_remote_copy(
+            src_ref=source,
+            dst_ref=target,
+            send_sem=self.send_sems.at[which],
+            recv_sem=self.recv_sems.at[which],
+            device_id=to,
+            device_id_type=pl.DeviceIdType.MESH,
+        )
+
+    def send(self, which, source, target, to, cond=None):
+        only(cond, lambda: self._make(which, source, target, to).start())
+        self.sent.append((which, source, target, to, cond))
+
+    def receive(self, which, target, via):
+        self._make(which, target, target, via).wait_recv()
+
+    def finish(self):
+        for which, source, target, to, cond in self.sent:
+            only(cond, lambda: self._make(which, source, target, to).wait_send())
+        self.sent = []
+
+
+def only(cond, action):
+    if cond is None:
+        action()
+    else:
+        pl.when(cond)(action)
+
+
+class Place:
+    def __init__(self):
+        self.z, self.p = lax.axis_index(RING), lax.axis_index(PAIR)
+        self.c, self.y = lax.axis_index(CORE), lax.axis_index(TENSOR)
+        self.rank = (self.z * 2 + self.p) * 2 + self.c
+        self.pair, self.core = {PAIR: 1 - self.p}, {CORE: 1 - self.c}
+        self.cross = {PAIR: 1 - self.p, CORE: 1 - self.c}
+        self.other = {TENSOR: 1 - self.y}
+        self.right, self.left = {RING: self.z + 1}, {RING: self.z - 1}
+        self.has_right, self.has_left = self.z < LINE - 1, self.z > 0
+
+    def ranked(self, rank):
+        return {RING: rank // 4, PAIR: (rank // 2) % 2, CORE: rank % 2}
+
+    def meet(self):
+        barrier = pltpu.get_barrier_semaphore()
+
+        def greet(to, cond=None):
+            only(
+                cond,
+                lambda: pl.semaphore_signal(
+                    barrier, inc=1, device_id=to, device_id_type=pl.DeviceIdType.MESH
+                ),
+            )
+
+        for to in (self.pair, self.core, self.cross, self.other):
+            greet(to)
+        greet(self.right, self.has_right)
+        greet(self.left, self.has_left)
+        for back in range(1, BACK + 1):
+            greet(self.ranked(self.rank + back), self.rank + back < 4 * LINE)
+            greet(self.ranked(self.rank - back), self.rank >= back)
+        line = jnp.minimum(self.z, 1) + jnp.minimum(LINE - 1 - self.z, 1)
+        reach = jnp.minimum(self.rank, BACK) + jnp.minimum(4 * LINE - 1 - self.rank, BACK)
+        pl.semaphore_wait(barrier, 4 + line + reach)
+
+
+class LineFlow:
+    def __init__(self, copies, place, block):
+        self.copies, self.place, self.block = copies, place, block
+        self.ids = {(way, step): copies.new() for way in (1, -1) for step in range(1, LINE)}
+
+    def valid(self, way, step):
+        z = self.place.z
+        return z >= step if way == 1 else z + step <= LINE - 1
+
+    def origin(self, way, step):
+        return self.place.z - way * step
+
+    def onward(self, way, step, source):
+        if step == LINE - 1:
+            return
+        to = self.place.right if way == 1 else self.place.left
+        there = self.place.has_right if way == 1 else self.place.has_left
+        if step:
+            there = there & self.valid(way, step)
+        target = self.block(self.origin(way, step))
+        self.copies.send(self.ids[way, step + 1], source, target, to, there)
+
+    def start(self, source):
+        self.onward(1, 0, source)
+        self.onward(-1, 0, source)
+
+    def arrive(self, step, then=None):
+        for way in (1, -1):
+
+            def take(way=way):
+                target = self.block(self.origin(way, step))
+                via = self.place.left if way == 1 else self.place.right
+                self.copies.receive(self.ids[way, step], target, via)
+
+            pl.when(self.valid(way, step))(take)
+            if step < LINE - 1:
+                self.onward(way, step, self.block(self.origin(way, step)))
+            if then is not None:
+                then(way, step)
+
+
+class RowsFlow:
+    def __init__(self, copies, place, shard, whole):
+        self.copies, self.place, self.shard, self.whole = copies, place, shard, whole
+        self.line = LineFlow(copies, place, lambda origin: self.rows(origin, place.p, place.c))
+        items = [(0, 0)] + [(way, step) for step in range(1, LINE) for way in (1, -1)]
+        self.items = items
+        self.pair_ids = {item: copies.new() for item in items}
+        self.core_ids = {item: copies.new() for item in items}
+        self.cross_ids = {item: copies.new() for item in items}
+
+    def rows(self, origin, p, c):
+        count = self.shard.shape[0]
+        return self.whole.at[pl.ds(pl.multiple_of((origin * 4 + p * 2 + c) * count, count), count)]
+
+    def valid(self, item):
+        return None if item == (0, 0) else self.line.valid(*item)
+
+    def spread(self, way, step):
+        item, place = (way, step), self.place
+        here = self.rows(self.line.origin(way, step), place.p, place.c)
+        self.copies.send(self.pair_ids[item], here, here, place.pair, self.valid(item))
+        self.copies.send(self.core_ids[item], here, here, place.core, self.valid(item))
+
+    def start(self, own_copy):
+        self.line.start(self.shard)
+        own_copy()
+        self.spread(0, 0)
+
+    def arrive(self, step):
+        self.line.arrive(step, self.spread)
+
+    def crossing(self, step):
+        place = self.place
+        for item in self.items:
+            if item[1] != step:
+                continue
+            there = self.rows(self.line.origin(*item), 1 - place.p, place.c)
+            only(
+                self.valid(item),
+                lambda: self.copies.receive(self.pair_ids[item], there, place.pair),
+            )
+            self.copies.send(self.cross_ids[item], there, there, place.core, self.valid(item))
+
+    def end(self):
+        place = self.place
+        for item in self.items:
+            origin = self.line.origin(*item)
+
+            def take(item=item, origin=origin):
+                mine = self.rows(origin, place.p, 1 - place.c)
+                cross = self.rows(origin, 1 - place.p, 1 - place.c)
+                self.copies.receive(self.core_ids[item], mine, place.core)
+                self.copies.receive(self.cross_ids[item], cross, place.core)
+
+            only(self.valid(item), take)
+
+
+class QuarterFlow:
+    def __init__(self, copies, place, shard, whole, own_sem):
+        self.copies, self.place, self.shard, self.whole = copies, place, shard, whole
+        self.count, self.width = shard.shape[0], whole.shape[1]
+        self.own = pltpu.make_async_copy(
+            self.columns(place.p, place.c), self.rows(place.p, place.c), own_sem
+        )
+        self.near = (
+            (copies.new(), 1 - place.p, place.c, place.pair),
+            (copies.new(), place.p, 1 - place.c, place.core),
+            (copies.new(), 1 - place.p, 1 - place.c, place.cross),
+        )
+        self.line = LineFlow(copies, place, self.block)
+
+    def columns(self, p, c):
+        width = self.width
+        return self.shard.at[:, pl.ds(pl.multiple_of((p * 2 + c) * width, LANES), width)]
+
+    def rows(self, p, c):
+        count = self.count
+        start = (self.place.z * 4 + p * 2 + c) * count
+        return self.whole.at[pl.ds(pl.multiple_of(start, count), count)]
+
+    def block(self, origin):
+        count = 4 * self.count
+        return self.whole.at[pl.ds(pl.multiple_of(origin * count, count), count)]
+
+    def start(self):
+        place = self.place
+        self.own.start()
+        for which, p, c, to in self.near:
+            self.copies.send(which, self.columns(p, c), self.rows(place.p, place.c), to)
+
+    def join(self):
+        self.own.wait()
+        for which, p, c, to in self.near:
+            self.copies.receive(which, self.rows(p, c), to)
+        self.line.start(self.block(self.place.z))
+
+    def arrive(self, step):
+        self.line.arrive(step)
+
+
+class FourFlow:
+    def __init__(self, copies, place, slots, parts):
+        self.copies, self.place, self.slots = copies, place, slots
+        self.size = slots.shape[1] // parts
+        self.ids = [[copies.new() for _ in range(3)] for _ in range(parts)]
+
+    def slot(self, which, part):
+        return self.slots.at[which, pl.ds(part * self.size, self.size)]
+
+    def send(self, part, source):
+        self.copies.send(self.ids[part][0], source, self.slot(1, part), self.place.pair)
+        self.copies.send(self.ids[part][1], source, self.slot(2, part), self.place.core)
+
+    def cross(self, part):
+        got = self.slot(1, part)
+        self.copies.receive(self.ids[part][0], got, self.place.pair)
+        self.copies.send(self.ids[part][2], got, self.slot(3, part), self.place.core)
+
+    def end(self, part):
+        self.copies.receive(self.ids[part][1], self.slot(2, part), self.place.core)
+        self.copies.receive(self.ids[part][2], self.slot(3, part), self.place.core)
+
+
+PARTS = 4
+N_REMOTE = 160
+
+
+def forward_kernel(
+    heads,
+    head_size,
+    tokens,
+    first_shard,
+    out_shard,
+    gate_shard,
+    up_shard,
+    down_shard,
+    grad_out,
+    biases,
+    cosine,
+    sine,
+    allowed,
+    first_out,
+    w_out_out,
+    gate_all,
+    up_all,
+    down_all,
+    grad_out_four,
+    normed_four,
+    query_out,
+    window_out,
+    heads_out,
+    residual_out,
+    first_all,
+    w_out_all,
+    unit,
+    window,
+    keys,
+    values,
+    part_own,
+    part_other,
+    normed,
+    send_sems,
+    recv_sems,
+    local_sems,
+):
+    place = Place()
+    copies = Copies(send_sems, recv_sems)
+    rows, width = tokens.shape
+    batches = allowed.shape[0]
+    per_batch = rows // batches
+    query_width = heads * head_size
+    kv_width = query_width + 2 * head_size
+
+    window[...] = jnp.zeros_like(window)
+    place.meet()
+
+    first = RowsFlow(copies, place, first_shard, first_all)
+    outs = RowsFlow(copies, place, out_shard, w_out_all)
+    quarters = [
+        QuarterFlow(copies, place, shard, whole, local_sems.at[2 + i])
+        for i, (shard, whole) in enumerate(
+            ((gate_shard, gate_all), (up_shard, up_all), (down_shard, down_all))
+        )
+    ]
+    cot = FourFlow(copies, place, grad_out_four, 1)
+    second = FourFlow(copies, place, normed_four, PARTS)
+    part_ids = [copies.new() for _ in range(PARTS)]
+    window_ids = [copies.new() for _ in range(BACK)]
+
+    def put(flow, sem):
+        def run():
+            copy = pltpu.make_async_copy(flow.shard, flow.rows(place.z, place.p, place.c), sem)
+            copy.start()
+            copy.wait()
+
+        return run
+
+    first.start(put(first, local_sems.at[0]))
+    quarters[0].start()
+    x = wide(tokens[...])
+    scale_row = lax.rsqrt(jnp.mean(x * x, axis=-1, keepdims=True) + EPSILON)
+    unit[...] = x * scale_row
+    first.crossing(0)
+    first.arrive(1)
+    quarters[1].start()
+    first.crossing(1)
+    quarters[0].join()
+    first.arrive(2)
+    first.crossing(2)
+    first.arrive(3)
+    quarters[2].start()
+    first.crossing(3)
+    quarters[1].join()
+    first.end()
+
+    gains = wide(first_all[:, kv_width:]).T
+    first_gain, second_gain = gains[0:1], gains[1:2]
+    first_normed = low(unit[...] * first_gain)
+    sign = jnp.where(
+        lax.broadcasted_iota(jnp.int32, (1, head_size), 1) < head_size // 2, -1.0, 1.0
+    )
+    turn_sine = sine[...] * sign
+
+    def project(start, size):
+        raw = matmul(first_normed, first_all[:, start : start + size])
+        return raw + biases[:, start : start + size]
+
+    def turned(raw):
+        return low(raw * cosine[...] + pltpu.roll(raw, head_size // 2, 1) * turn_sine)
+
+    kv = project(query_width, 2 * head_size)
+    key_now, value_now = turned(kv[:, :head_size]), low(kv[:, head_size:])
+    for b in range(batches):
+        mine = slice(b * per_batch, (b + 1) * per_batch)
+        window[BACK, b, :, :head_size] = key_now[mine]
+        window[BACK, b, :, head_size:] = value_now[mine]
+    for back in range(1, BACK + 1):
+        copies.send(
+            window_ids[back - 1],
+            window.at[BACK],
+            window.at[BACK - back],
+            place.ranked(place.rank + back),
+            place.rank + back < 4 * LINE,
+        )
+    outs.start(put(outs, local_sems.at[1]))
+    quarters[2].join()
+    for h in range(0, heads, 2):
+        raw = project(h * head_size, 2 * head_size)
+        query_out[:, h * head_size : (h + 1) * head_size] = turned(raw[:, :head_size])
+        query_out[:, (h + 1) * head_size : (h + 2) * head_size] = turned(raw[:, head_size:])
+    cot_own = pltpu.make_async_copy(grad_out, grad_out_four.at[0], local_sems.at[5])
+    cot_own.start()
+    cot.send(0, grad_out)
+    outs.crossing(0)
+    outs.arrive(1)
+    outs.crossing(1)
+    quarters[0].arrive(1)
+    outs.arrive(2)
+    outs.crossing(2)
+    for back in range(1, BACK + 1):
+        only(
+            place.rank >= back,
+            lambda: copies.receive(
+                window_ids[back - 1], window.at[BACK - back], place.ranked(place.rank - back)
+            ),
+        )
+
+    root = 1.0 / math.sqrt(head_size)
+    size = rows // PARTS
+    for b in range(batches):
+        for slot in range(BACK + 1):
+            keys[slot * per_batch : (slot + 1) * per_batch] = window[slot, b, :, :head_size]
+            values[slot * per_batch : (slot + 1) * per_batch] = window[slot, b, :, head_size:]
+
+        def attend_head(h, carry, b=b):
+            columns = pl.ds(pl.multiple_of(h * head_size, head_size), head_size)
+            mine = slice(b * per_batch, (b + 1) * per_batch)
+            scores = times_transpose(query_out[mine, columns], keys[...]) * root
+            scores = jnp.where(allowed[b] > 0.0, scores, NEGATIVE)
+            weights = jnp.exp(scores - jnp.max(scores, axis=-1, keepdims=True))
+            probs = low(weights * (1.0 / jnp.sum(weights, axis=-1, keepdims=True)))
+            heads_out[mine, columns] = low(matmul(probs, values[...]))
+            return carry
+
+        lax.fori_loop(0, heads, attend_head, 0)
+        if b == 0:
+            outs.arrive(3)
+            outs.crossing(3)
+            outs.end()
+            quarters[1].arrive(1)
+        part = low(times_transpose(heads_out[b * per_batch : (b + 1) * per_batch], w_out_all[...]))
+        part_own[b * per_batch : (b + 1) * per_batch] = part
+        for i in range(b * per_batch // size, (b + 1) * per_batch // size):
+            block = pl.ds(i * size, size)
+            copies.send(part_ids[i], part_own.at[block], part_other.at[block], place.other)
+        if b == 0:
+            quarters[2].arrive(1)
+
+    for i in range(PARTS):
+        block = pl.ds(i * size, size)
+        copies.receive(part_ids[i], part_other.at[block], place.other)
+        state = wide(tokens[block]) + (wide(part_own[block]) + wide(part_other[block]))
+        residual_out[block] = state
+        scale_row = lax.rsqrt(jnp.mean(state * state, axis=-1, keepdims=True) + EPSILON)
+        normed[block] = low(state * scale_row * second_gain)
+        second.send(i, normed.at[block])
+        if i > 0:
+            second.cross(i - 1)
+    second_own = pltpu.make_async_copy(normed, normed_four.at[0], local_sems.at[6])
+    second_own.start()
+    second.cross(PARTS - 1)
+    for flow in quarters:
+        flow.arrive(2)
+    cot.cross(0)
+    first_copy = pltpu.make_async_copy(first_all, first_out, local_sems.at[0])
+    first_copy.start()
+    outs_copy = pltpu.make_async_copy(w_out_all, w_out_out, local_sems.at[1])
+    outs_copy.start()
+    window_out[...] = window[...]
+    for i in range(PARTS):
+        second.end(i)
+    cot.end(0)
+    for flow in quarters:
+        flow.arrive(3)
+    for copy in (cot_own, second_own, first_copy, outs_copy):
+        copy.wait()
+    copies.finish()
+
+
+def forward_call(heads, head_size, operands):
+    tokens, first_shard, out_shard, gate_shard = operands[:4]
+    allowed = operands[-1]
+    rows, width = tokens.shape
+    batches = allowed.shape[0]
+    per_batch = rows // batches
+    quarter = gate_shard.shape[1] // 4
+    query_width = heads * head_size
+    low_type, wide_type = jnp.bfloat16, jnp.float32
+
+    def shape(*dims, kind=low_type):
+        return jax.ShapeDtypeStruct(dims, kind)
+
+    in_vmem, anywhere = pl.BlockSpec(memory_space=pltpu.VMEM), pl.BlockSpec(memory_space=pl.ANY)
+    window_shape = (BACK + 1, batches, per_batch, 2 * head_size)
+    outs = (
+        (shape(width, first_shard.shape[1]), anywhere),
+        (shape(width, query_width), anywhere),
+        (shape(width, quarter), anywhere),
+        (shape(width, quarter), anywhere),
+        (shape(width, quarter), anywhere),
+        (shape(4, rows, width), anywhere),
+        (shape(4, rows, width), anywhere),
+        (shape(rows, query_width), in_vmem),
+        (shape(*window_shape), in_vmem),
+        (shape(rows, query_width), in_vmem),
+        (shape(rows, width, kind=wide_type), in_vmem),
+    )
+    return pl.pallas_call(
+        functools.partial(forward_kernel, heads, head_size),
+        out_shape=[out[0] for out in outs],
+        in_specs=[in_vmem] + [anywhere] * 6 + [in_vmem] * 4,
+        out_specs=[out[1] for out in outs],
+        scratch_shapes=[
+            pltpu.VMEM((width, first_shard.shape[1]), low_type),
+            pltpu.VMEM((width, query_width), low_type),
+            pltpu.VMEM((rows, width), wide_type),
+            pltpu.VMEM(window_shape, low_type),
+            pltpu.VMEM(((BACK + 1) * per_batch, head_size), low_type),
+            pltpu.VMEM(((BACK + 1) * per_batch, head_size), low_type),
+            pltpu.VMEM((rows, width), low_type),
+            pltpu.VMEM((rows, width), low_type),
+            pltpu.VMEM((rows, width), low_type),
+            pltpu.SemaphoreType.DMA((N_REMOTE,)),
+            pltpu.SemaphoreType.DMA((N_REMOTE,)),
+            pltpu.SemaphoreType.DMA((8,)),
+        ],
+        compiler_params=pltpu.CompilerParams(
+            collective_id=0, has_side_effects=True, vmem_limit_bytes=VMEM_BYTES
+        ),
+    )(*operands)
 
 
 def body(
@@ -286,55 +804,101 @@
     gains = jnp.stack([norm1_gain, norm2_gain], axis=1)
     gains = jnp.pad(gains, ((0, 0), (0, LANES - 2)))
     first_shard = jnp.concatenate([query_weight, key_weight, value_weight, gains], axis=1)
-    first_all = gather_rows(first_shard)
     kv_width = query_width + 2 * head_size
-    w_qkv = first_all[:, :kv_width]
-    first_gain = wide(first_all[:, kv_width])
-    second_gain = wide(first_all[:, kv_width + 1])
-    w_out = gather_rows(output_weight.T)
-
     padded = -(-units // (4 * LANES)) * (4 * LANES)
 
-    def quarter(shard):
-        return quarter_columns(jnp.pad(shard, ((0, 0), (0, padded - units))))
-
-    w_gate = quarter(gate_weight)
-    w_up = quarter(up_weight)
-    w_down = quarter(down_weight.T)
+    def spaced(shard):
+        return jnp.pad(shard, ((0, 0), (0, padded - units)))
+
     grad_out = cotangent.reshape(rows, width)
-    grad_out_four = four_blocks(grad_out)
-
     inputs = wide(tokens.reshape(rows, width))
-    first_unit, first_scale = root_mean_square_parts(inputs)
-    first_normed = low(first_unit * first_gain)
     biases = jnp.concatenate(
         [query_bias.reshape(-1), key_bias.reshape(-1), value_bias.reshape(-1)]
     )
-    raw = matmul(first_normed, w_qkv) + wide(biases)
     own_places = lax.dynamic_slice_in_dim(positions, row_start, count_rows, axis=1)
     cosine, sine_table = rotation(own_places.reshape(-1), head_size)
-    turned = rotate(
-        raw[:, : query_width + head_size].reshape(rows, heads + 1, head_size), cosine, sine_table
-    )
-    turned = low(turned)
-    query_rows = turned[:, :heads].reshape(batches, count_rows, heads, head_size)
-    key_value = jnp.concatenate([turned[:, heads], low(raw[:, query_width + head_size :])], axis=1)
-    key_value = key_value.reshape(batches, count_rows, 2 * head_size)
-    window = jnp.concatenate(
-        [shifted(key_value, back) for back in range(BACK, 0, -1)] + [key_value], axis=1
-    )
-    key_rows, value_rows = window[..., :head_size], window[..., head_size:]
     allowed = [
         visible(segments[b], positions[b], row_start, count_rows) for b in range(batches)
     ]
-    attended = [
-        attend(query_rows[b], key_rows[b], value_rows[b], allowed[b]) for b in range(batches)
-    ]
-    heads_out = jnp.concatenate([mixed for mixed, _ in attended], axis=0)
-    residual = inputs + tensor_total(times_transpose(heads_out, w_out))
+    if lax.axis_size(RING) == LINE:
+        (
+            first_all,
+            w_out,
+            w_gate,
+            w_up,
+            w_down,
+            grad_out_four,
+            second_normed,
+            query_rows,
+            window,
+            heads_out,
+            residual,
+        ) = forward_call(
+            heads,
+            head_size,
+            (
+                tokens.reshape(rows, width),
+                first_shard,
+                output_weight.T,
+                spaced(gate_weight),
+                spaced(up_weight),
+                spaced(down_weight.T),
+                grad_out,
+                wide(biases).reshape(1, -1),
+                cosine[:, 0],
+                sine_table[:, 0],
+                jnp.stack(allowed).astype(jnp.float32),
+            ),
+        )
+        grad_out_four = grad_out_four.reshape(-1, width)
+        second_normed = second_normed.reshape(-1, width)
+        query_rows = query_rows.reshape(batches, count_rows, heads, head_size)
+        window = window.transpose(1, 0, 2, 3).reshape(batches, -1, 2 * head_size)
+        w_qkv = first_all[:, :kv_width]
+        first_gain = wide(first_all[:, kv_width])
+        second_gain = wide(first_all[:, kv_width + 1])
+        first_unit, first_scale = root_mean_square_parts(inputs)
+        first_normed = low(first_unit * first_gain)
+        key_rows, value_rows = window[..., :head_size], window[..., head_size:]
+        log_totals = [log_total_of(query_rows[b], key_rows[b], allowed[b]) for b in range(batches)]
+    else:
+        first_all = gather_rows(first_shard)
+        w_qkv = first_all[:, :kv_width]
+        first_gain = wide(first_all[:, kv_width])
+        second_gain = wide(first_all[:, kv_width + 1])
+        w_out = gather_rows(output_weight.T)
+        w_gate = quarter_columns(spaced(gate_weight))
+        w_up = quarter_columns(spaced(up_weight))
+        w_down = quarter_columns(spaced(down_weight.T))
+        grad_out_four = four_blocks(grad_out)
+        first_unit, first_scale = root_mean_square_parts(inputs)
+        first_normed = low(first_unit * first_gain)
+        raw = matmul(first_normed, w_qkv) + wide(biases)
+        turned = rotate(
+            raw[:, : query_width + head_size].reshape(rows, heads + 1, head_size),
+            cosine,
+            sine_table,
+        )
+        turned = low(turned)
+        query_rows = turned[:, :heads].reshape(batches, count_rows, heads, head_size)
+        key_value = jnp.concatenate(
+            [turned[:, heads], low(raw[:, query_width + head_size :])], axis=1
+        )
+        key_value = key_value.reshape(batches, count_rows, 2 * head_size)
+        window = jnp.concatenate(
+            [shifted(key_value, back) for back in range(BACK, 0, -1)] + [key_value], axis=1
+        )
+        key_rows, value_rows = window[..., :head_size], window[..., head_size:]
+        attended = [
+            attend(query_rows[b], key_rows[b], value_rows[b], allowed[b]) for b in range(batches)
+        ]
+        log_totals = [log_total for _, log_total in attended]
+        heads_out = jnp.concatenate([mixed for mixed, _ in attended], axis=0)
+        residual = inputs + tensor_total(times_transpose(heads_out, w_out))
+        second_unit, second_scale = root_mean_square_parts(residual)
+        second_normed = four_blocks(low(second_unit * second_gain))
 
     second_unit, second_scale = root_mean_square_parts(residual)
-    second_normed = four_blocks(low(second_unit * second_gain))
     gate_value = matmul(second_normed, w_gate)
     up_part = matmul(second_normed, w_up)
     sigmoid_gate = jax.nn.sigmoid(gate_value)
@@ -358,7 +922,7 @@
     grad_heads = low(matmul(grad_branch, w_out)).reshape(query_rows.shape)
     backs = [
         attend_back(
-            grad_heads[b], query_rows[b], key_rows[b], value_rows[b], allowed[b], attended[b][1]
+            grad_heads[b], query_rows[b], key_rows[b], value_rows[b], allowed[b], log_totals[b]
         )
         for b in range(batches)
     ]

time: 844 us -> 684 us (0.81)
  starting transfers between devices: 305 us -> 59.2 us
  Pallas kernels: 0 us -> 235 us
  waiting for transfers between devices: 284 us -> 163 us
  other arithmetic: 78.2 us -> 59.6 us
  local copies, waits for them, and re-layouts: 46.9 us -> 35.2 us
  between operations: 3.92 us -> 15.5 us
    pallas_call x0 -> x1, Pallas kernels: none -> 235 us  [forward_call(): pl.pallas_call(functools.partial(forward_kernel, heads, head_size), out_s...]
    ppermute x15 -> x6, starting transfers between devices: 124 us -> 27.4 us  [line_scatter(): right = lax.ppermute(to_right, RING, [(i, i + 1) for i in range(step)])]
    ppermute x30 -> x0, waiting for transfers between devices: 93.6 us -> none  [the longest x15 93.6 us: line_gather(): lax.ppermute(left[-1], RING, [(i, i - 1) for i in range(1, count - step +...]
    ppermute x30 -> x0, starting transfers between devices: 57.2 us -> none  [the longest x15 37.2 us: line_gather(): lax.ppermute(right[-1], RING, [(i, i + 1) for i in range(step - 1, count...]
    ppermute x34 -> x17, starting transfers between devices: 70.2 us -> 18.2 us  [swapped(): return lax.ppermute(value, axis, SWAP)]
    ppermute x15 -> x6, waiting for transfers between devices: 36.3 us -> 4.32 us  [line_scatter(): lax.ppermute(to_left, RING, [(i, i - 1) for i in range(count - step, coun...]
    ppermute x10 -> x5, waiting for transfers between devices: 26 us -> 51.6 us  [shifted(): lax.ppermute(value, FSDP, [(source, source + steps) for source in range(f...]
    ppermute x34 -> x17, waiting for transfers between devices: 116 us -> 97.1 us  [swapped(): return lax.ppermute(value, axis, SWAP)]
  transfers between devices with their start and end apart: 108 -> 41, of which waited for: 35 -> 17; matrix products, arithmetic and copies ran while one was open for 19% -> 21% of each run, Pallas kernels for 0% -> 0%
where the time goes in v2:
time: 684 us; the launch traced here: 678 us
  Pallas kernels  235 us (34%)
  waiting for transfers between devices  163 us (24%)
  matrix products  111 us (16%)
  other arithmetic  59.6 us (9%)
  starting transfers between devices  59.2 us (9%)
  local copies, waits for them, and re-layouts  35.2 us (5%)
  between operations  15.5 us (2%)
    pallas_call x1, Pallas kernels, forward_call(): pl.pallas_call(functools.partial(forward_kernel, heads, head_size), out_s...  235 us
    ppermute x17, waiting for transfers between devices, swapped(): return lax.ppermute(value, axis, SWAP)  97.1 us
    ppermute x5, waiting for transfers between devices, shifted(): lax.ppermute(value, FSDP, [(source, source + steps) for source in range(f...  51.6 us
    dot_general x4, matrix products, times_transpose(): lax.dot_general(left_side, right_side, (((1,), (1,)), ((), ())), preferre...  33.7 us
    dot_general x4, matrix products, matmul(): return jnp.dot(left_side, right_side, preferred_element_type=jnp.float32)  33.7 us
    dot_general x5, matrix products, contract_rows(): lax.dot_general(left_side, right_side, (((0,), (0,)), ((), ())), preferre...  32.9 us
    ppermute x6, starting transfers between devices, line_scatter(): right = lax.ppermute(to_right, RING, [(i, i + 1) for i in range(step)])  27.4 us
    ppermute x17, starting transfers between devices, swapped(): return lax.ppermute(value, axis, SWAP)  18.2 us
  transfers between devices with their start and end apart: 41, of which 17 were waited for; matrix products, arithmetic and copies ran while one was open for 21% of the time, Pallas kernels for 0%

profile of v2, /device:TPU:0, one launch (start us, length us, event | category | flops | bytes accessed | tf_op | source)
XLA Modules:
  0.0 678.1 jit_solution(6836572082681821797)
XLA Ops:
  9.9 2.2 pad.19.gate_shard
  19.7 235.4 %shard_map.263 = (bf16[1536,1152]{1,0:T(8,128)(2,1)}, bf16[1536,768]{1,0:T(8,128)(2,1)}, bf16[1536,1152]{1,0:T(8,128)(2,1)}, bf16[1536,1152]{1,0:T(8,128)(2,1)},...) custom-call(bf16[384,1536]{1,0:T(8,128)(2,1)} %bitcast.345, ...), custom_call_target="tpu_custom_call" | custom-call | tf_op jit(solution)/shard_map/pallas_call | solution.py:753
  255.2 11.1 %fusion.114 = f32[1536,1152]{1,0:T(8,128)} fusion(bf16[1536,1536]{1,0:T(8,128)(2,1)} %bitcast.396, bf16[1536,1152]{1,0:T(8,128)(2,1)} %get-tuple-element.28), kind=kOutput, calls=%fused_computation.283 | convolution fusion | flops 5435817984 | bytes 15335424 | tf_op jit(solution)/shard_map/dot_general | solution.py:35
  266.3 8.2 %fusion.113 = f32[1536,1152]{1,0:T(8,128)} fusion(bf16[1536,1536]{1,0:T(8,128)(2,1)S(1)} %bitcast.398, bf16[1536,1152]{1,0:T(8,128)(2,1)S(1)} %copy-done.57), kind=kOutput, calls=%fused_computation.282 | convolution fusion | flops 5435817984 | bytes 15335424 | tf_op jit(solution)/shard_map/dot_general | solution.py:35
  274.5 13.2 %multiply_convert_fusion = (bf16[1536,1152]{1,0:T(8,128)(2,1)}, bf16[1536,1152]{1,0:T(8,128)(2,1)}, bf16[1536,1152]{1,0:T(8,128)(2,1)S(1)}) fusion(f32[1536,1152]{1,0:T(8,128)} %fusion.113, f32[1536,1152]{1,0:T(8,128)} %fusion.114, bf16[1536,1536]{1,0:T(8,128)(2,1)S(1)} %bitcast.404, bf16[1536,1152]{1,0:T(8,128)(2,1)S(1)} %copy-done.58), kind=kOutput, calls=%fused_computation.4 | convolution fusion | flops 5462360064 | bytes 33030144 | tf_op jit(solution)/shard_map/dot_general | solution.py:35
  287.8 8.2 %convolution_convert_fusion = bf16[1536,1152]{1,0:T(8,128)(2,1)} fusion(bf16[1536,1536]{1,0:T(8,128)(2,1)S(1)} %bitcast.405, bf16[1536,1152]{1,0:T(8,128)(2,1)S(1)} %get-tuple-element.46), kind=kOutput, calls=%fused_computation.1 | convolution fusion | flops 5437587456 | bytes 11796480 | tf_op jit(solution)/shard_map/dot_general | solution.py:39
  296.1 10.5 %convolution_convert_fusion.1 = bf16[1536,1152]{1,0:T(8,128)(2,1)} fusion(bf16[1536,1536]{1,0:T(8,128)(2,1)} %bitcast.397, bf16[1536,1152]{1,0:T(8,128)(2,1)} %get-tuple-element.44), kind=kOutput, calls=%fused_computation.2 | convolution fusion | flops 5437587456 | bytes 11796480 | tf_op jit(solution)/shard_map/dot_general | solution.py:39
  306.7 9.5 %fusion.115 = f32[1536,1536]{1,0:T(8,128)S(1)} fusion(bf16[1536,1152]{1,0:T(8,128)(2,1)} %copy-done.63, bf16[1536,1152]{1,0:T(8,128)(2,1)} %get-tuple-element.29), kind=kOutput, calls=%fused_computation.284 | convolution fusion | flops 5435817984 | bytes 16515072 | tf_op jit(solution)/shard_map/dot_general | solution.py:45
  316.2 3.7 copy-done.13
  321.6 4.5 collective-permute-start
  326.1 9.2 %fusion.116 = f32[1536,1536]{1,0:T(8,128)} fusion(bf16[1536,1152]{1,0:T(8,128)(2,1)S(1)} %copy-done.62, bf16[1536,1152]{1,0:T(8,128)(2,1)S(1)} %copy-done.57), kind=kOutput, calls=%fused_computation.285 | convolution fusion | flops 5435817984 | bytes 16515072 | tf_op jit(solution)/shard_map/dot_general | solution.py:45
  335.2 10.3 %convolution_add_fusion = f32[1536,1536]{1,0:T(8,128)S(1)} fusion(f32[1536,1536]{1,0:T(8,128)} %fusion.116, bf16[1536,1152]{1,0:T(8,128)(2,1)} %get-tuple-element.44, bf16[1536,1152]{1,0:T(8,128)(2,1)S(1)} %copy-done.56), kind=kOutput, calls=%fused_computation | convolution fusion | flops 5438177280 | bytes 25952256 | tf_op jit(solution)/shard_map/dot_general | solution.py:45
  345.6 1.9 slice.398
  348.5 8.0 %convolution_convert_fusion.2 = bf16[1536,1152]{1,0:T(8,128)(2,1)} fusion(bf16[1536,1536]{1,0:T(8,128)(2,1)S(1)} %bitcast.401, bf16[1536,1152]{1,0:T(8,128)(2,1)S(1)} %copy-done.62), kind=kOutput, calls=%fused_computation.3 | convolution fusion | flops 5437587456 | bytes 11796480 | tf_op jit(solution)/shard_map/dot_general | solution.py:39
  361.2 1.7 exponential_reduce_fusion.1
  365.6 5.7 slice_add_fusion
  371.6 3.8 slice_add_fusion.1
  378.5 1.7 exponential_reduce_fusion
  380.2 20.2 %collective-permute-done.4 = bf16[384,1536]{1,0:T(8,128)(2,1)S(1)} collective-permute-done((bf16[384,1536]{1,0:T(8,128)(2,1)S(1)}, bf16[384,1536]{1,0:T(8,128)(2,1)S(1)}, u32[]{:S(2)}, u32[]{:S(2)}) %collective-permute-start.4) | collective-permute-done | bytes 1179680 | tf_op jit(solution)/shard_map/ppermute | solution.py:51
  403.3 21.3 %collective-permute-done.1 = bf16[384,1536]{1,0:T(8,128)(2,1)S(1)} collective-permute-done((bf16[384,1536]{1,0:T(8,128)(2,1)S(1)}, bf16[384,1536]{1,0:T(8,128)(2,1)S(1)}, u32[]{:S(2)}, u32[]{:S(2)}) %collective-permute-start.1) | collective-permute-done | bytes 1179680 | tf_op jit(solution)/shard_map/ppermute | solution.py:51
  430.8 4.1 multiply_reduce_fusion.1
  434.9 18.6 %collective-permute-done.2 = bf16[384,1536]{1,0:T(8,128)(2,1)} collective-permute-done((bf16[384,1536]{1,0:T(8,128)(2,1)}, bf16[384,1536]{1,0:T(8,128)(2,1)}, u32[]{:S(2)}, u32[]{:S(2)}) %collective-permute-start.2) | collective-permute-done | bytes 1179680 | tf_op jit(solution)/shard_map/ppermute | solution.py:51
  453.5 5.3 multiply_add_fusion.1
  479.0 2.8 convolution_convert_fusion.4
  481.8 15.6 %collective-permute-done.10 = bf16[2,192,256]{1,2,0:T(8,128)(2,1)S(1)} collective-permute-done((bf16[2,192,256]{1,2,0:T(8,128)(2,1)S(1)}, bf16[2,192,256]{1,2,0:T(8,128)(2,1)S(1)}, u32[]{:S(2)}, u32[]{:S(2)}) %collective-permute-start.10) | collective-permute-done | bytes 196640 | tf_op jit(solution)/shard_map/ppermute | solution.py:63
  497.5 36.0 %collective-permute-done.9 = bf16[2,192,256]{1,2,0:T(8,128)(2,1)S(1)} collective-permute-done((bf16[2,192,256]{1,2,0:T(8,128)(2,1)S(1)}, bf16[2,192,256]{1,2,0:T(8,128)(2,1)S(1)}, u32[]{:S(2)}, u32[]{:S(2)}) %collective-permute-start.9) | collective-permute-done | bytes 196640 | tf_op jit(solution)/shard_map/ppermute | solution.py:63
  537.4 4.7 fusion.112
  547.9 3.3 convolution_convert_fusion.3
  552.3 18.1 %collective-permute-done.11 = bf16[384,1536]{1,0:T(8,128)(2,1)} collective-permute-done((bf16[384,1536]{1,0:T(8,128)(2,1)}, bf16[384,1536]{1,0:T(8,128)(2,1)}, u32[]{:S(2)}, u32[]{:S(2)}) %collective-permute-start.11) | collective-permute-done | bytes 1179680 | tf_op jit(solution)/shard_map/ppermute | solution.py:51
  570.4 2.2 multiply_reduce_fusion
  572.7 1.7 fusion.35
  574.7 2.1 collective-permute-start.25
  576.7 1.7 collective-permute-done.13
  579.6 2.5 collective-permute-done.14
  582.2 3.4 multiply_add_fusion
  586.8 3.8 collective-permute-done.25
  590.8 3.1 collective-permute-start.26
  596.9 4.4 collective-permute-start.27
  608.5 5.0 collective-permute-start.28
  615.5 1.8 dynamic-slice_bitcast_fusion.2
  618.1 1.8 dynamic-slice_bitcast_fusion.3
  622.2 5.7 collective-permute-done.17
  629.5 5.1 collective-permute-start.18
  638.0 4.4 collective-permute-start.19
  643.7 3.2 collective-permute-done.34
  647.1 6.2 collective-permute-done.32
  654.4 5.3 collective-permute-start.20
  665.6 4.3 collective-permute-done.23
  (336 shorter events, 95.8 us)
Async XLA Ops:
  7.2 608.3 %reduce-scatter.8.cloned.1.call-start = ((), (), s32[]{:S(2)}) async-start(), calls=%async_computation.5 | async-start | bytes 4423680 | tf_op jit(solution)/shard_map/reduce_scatter | solution.py:156
  14.3 240.8 %copy-start.44 = (s32[1,192]{1,0:T(1,128)}, s32[1,192]{1,0:T(1,128)S(1)}, u32[]{:S(2)}) copy-start(s32[1,192]{1,0:T(1,128)S(1)} %get-tuple-element.120) | copy-start | bytes 2308
  14.3 240.8 %copy-start.46 = (s32[1,192]{1,0:T(1,128)}, s32[1,192]{1,0:T(1,128)S(1)}, u32[]{:S(2)}) copy-start(s32[1,192]{1,0:T(1,128)S(1)} %get-tuple-element.121) | copy-start | bytes 2308
  14.4 240.8 %copy-start.48 = (s32[1,192]{1,0:T(1,128)}, s32[1,192]{1,0:T(1,128)S(1)}, u32[]{:S(2)}) copy-start(s32[1,192]{1,0:T(1,128)S(1)} %get-tuple-element.122) | copy-start | bytes 2308
  14.4 240.8 %copy-start.50 = (s32[1,192]{1,0:T(1,128)}, s32[1,192]{1,0:T(1,128)S(1)}, u32[]{:S(2)}) copy-start(s32[1,192]{1,0:T(1,128)S(1)} %get-tuple-element.123) | copy-start | bytes 2308
  296.0 322.1 %reduce-scatter.6.cloned.1.call-start = ((), (), s32[]{:S(2)}) async-start(), calls=%async_computation.4 | async-start | bytes 4423680 | tf_op jit(solution)/shard_map/reduce_scatter | solution.py:156
  306.6 314.5 %reduce-scatter.4.cloned.1.call-start = ((), (), s32[]{:S(2)}) async-start(), calls=%async_computation.3 | async-start | bytes 4423680 | tf_op jit(solution)/shard_map/reduce_scatter | solution.py:156
  321.6 50.0 %collective-permute-start = (bf16[768,1536]{1,0:T(8,128)(2,1)}, bf16[768,1536]{1,0:T(8,128)(2,1)}, u32[]{:S(2)}, u32[]{:S(2)}) collective-permute-start(bf16[768,1536]{1,0:T(8,128)(2,1)} %slice.399), channel_id=1, source_target_pairs={{0,2},{2,0},{1,3},{3,1},{4,6},{6,4},{5,7},{7,5},{8,10},{10,8},{9,1... | collective-permute-start | bytes 7077896 | tf_op jit(solution)/shard_map/ppermute | solution.py:51
  347.4 18.1 %collective-permute-start.3 = (bf16[768,1536]{1,0:T(8,128)(2,1)}, bf16[768,1536]{1,0:T(8,128)(2,1)}, u32[]{:S(2)}, u32[]{:S(2)}) collective-permute-start(bf16[768,1536]{1,0:T(8,128)(2,1)} %slice.398), channel_id=1, source_target_pairs={{0,2},{2,0},{1,3},{3,1},{4,6},{6,4},{5,7},{7,5},{8,10},{10,8},{9,1... | collective-permute-start | bytes 7077896 | tf_op jit(solution)/shard_map/ppermute | solution.py:51
  371.5 28.9 %collective-permute-start.4 = (bf16[384,1536]{1,0:T(8,128)(2,1)S(1)}, bf16[384,1536]{1,0:T(8,128)(2,1)S(1)}, u32[]{:S(2)}, u32[]{:S(2)}) collective-permute-start(bf16[384,1536]{1,0:T(8,128)(2,1)S(1)} %slice.400), channel_id=1, source_target_pairs={{0,4},{4,0},{1,5},{5,1},{2,6},{6,2},{3,7},{7,3},{8,12},{12,8},{9,1... | collective-permute-start | bytes 3538952 | tf_op jit(solution)/shard_map/ppermute | solution.py:51
  375.4 49.2 %copy-start.4 = (f32[768,1536]{1,0:T(8,128)}, f32[768,1536]{1,0:T(8,128)S(1)}, u32[]{:S(2)}) copy-start(f32[768,1536]{1,0:T(8,128)S(1)} %slice_add_fusion.1) | copy-start | bytes 14155780
  375.6 49.1 %collective-permute-start.1 = (bf16[384,1536]{1,0:T(8,128)(2,1)S(1)}, bf16[384,1536]{1,0:T(8,128)(2,1)S(1)}, u32[]{:S(2)}, u32[]{:S(2)}) collective-permute-start(bf16[384,1536]{1,0:T(8,128)(2,1)S(1)} %slice.401), channel_id=1, source_target_pairs={{0,4},{4,0},{1,5},{5,1},{2,6},{6,2},{3,7},{7,3},{8,12},{12,8},{9,1... | collective-permute-start | bytes 3538952 | tf_op jit(solution)/shard_map/ppermute | solution.py:51
  401.8 29.0 %collective-permute-start.5 = (bf16[384,1536]{1,0:T(8,128)(2,1)}, bf16[384,1536]{1,0:T(8,128)(2,1)}, u32[]{:S(2)}, u32[]{:S(2)}) collective-permute-start(bf16[384,1536]{1,0:T(8,128)(2,1)} %fusion.38), channel_id=1, source_target_pairs={{0,1},{1,0},{2,3},{3,2},{4,5},{5,4},{6,7},{7,6},{8,9},{9,8},{10,11... | collective-permute-start | bytes 3538952 | tf_op jit(solution)/shard_map/ppermute | solution.py:51
  426.1 27.4 %collective-permute-start.2 = (bf16[384,1536]{1,0:T(8,128)(2,1)}, bf16[384,1536]{1,0:T(8,128)(2,1)}, u32[]{:S(2)}, u32[]{:S(2)}) collective-permute-start(bf16[384,1536]{1,0:T(8,128)(2,1)} %fusion.37), channel_id=1, source_target_pairs={{0,1},{1,0},{2,3},{3,2},{4,5},{5,4},{6,7},{7,6},{8,9},{9,8},{10,11... | collective-permute-start | bytes 3538952 | tf_op jit(solution)/shard_map/ppermute | solution.py:51
  430.8 29.2 %slice-start.2 = ((s8[5308416]{0:T(1024)(128)(4,1)}), s8[4194304]{0:T(1024)(128)(4,1)S(1)}, s32[]{:S(2)}) async-start(s8[5308416]{0:T(1024)(128)(4,1)} %bitcast.343), calls=%async_computation.8 | async-start | bytes 8388608
  472.1 25.4 %collective-permute-start.10 = (bf16[2,192,256]{1,2,0:T(8,128)(2,1)S(1)}, bf16[2,192,256]{1,2,0:T(8,128)(2,1)S(1)}, u32[]{:S(2)}, u32[]{:S(2)}) collective-permute-start(bf16[2,192,256]{1,2,0:T(8,128)(2,1)S(1)} %get-tuple-element.68), channel_id=1, source_target_pairs={{10,0},{12,2},{14,4},{16,6},{18,8},{20,10},{22,12},{24,14},{26,16}... | collective-permute-start | bytes 589832 | tf_op jit(solution)/shard_map/ppermute | solution.py:63
  473.4 24.1 %collective-permute-start.6 = (bf16[2,192,256]{1,2,0:T(8,128)(2,1)S(1)}, bf16[2,192,256]{1,2,0:T(8,128)(2,1)S(1)}, u32[]{:S(2)}, u32[]{:S(2)}) collective-permute-start(bf16[2,192,256]{1,2,0:T(8,128)(2,1)S(1)} %get-tuple-element.67), channel_id=1, source_target_pairs={{2,0},{4,2},{6,4},{8,6},{10,8},{12,10},{14,12},{16,14},{18,16},{20... | collective-permute-start | bytes 589832 | tf_op jit(solution)/shard_map/ppermute | solution.py:63
  474.7 22.8 %collective-permute-start.7 = (bf16[2,192,256]{1,2,0:T(8,128)(2,1)S(1)}, bf16[2,192,256]{1,2,0:T(8,128)(2,1)S(1)}, u32[]{:S(2)}, u32[]{:S(2)}) collective-permute-start(bf16[2,192,256]{1,2,0:T(8,128)(2,1)S(1)} %get-tuple-element.71), channel_id=1, source_target_pairs={{4,0},{6,2},{8,4},{10,6},{12,8},{14,10},{16,12},{18,14},{20,16},{2... | collective-permute-start | bytes 589832 | tf_op jit(solution)/shard_map/ppermute | solution.py:63
  476.0 21.5 %collective-permute-start.8 = (bf16[2,192,256]{1,2,0:T(8,128)(2,1)S(1)}, bf16[2,192,256]{1,2,0:T(8,128)(2,1)S(1)}, u32[]{:S(2)}, u32[]{:S(2)}) collective-permute-start(bf16[2,192,256]{1,2,0:T(8,128)(2,1)S(1)} %get-tuple-element.70), channel_id=1, source_target_pairs={{6,0},{8,2},{10,4},{12,6},{14,8},{16,10},{18,12},{20,14},{22,16},{... | collective-permute-start | bytes 589832 | tf_op jit(solution)/shard_map/ppermute | solution.py:63
  477.3 56.1 %collective-permute-start.9 = (bf16[2,192,256]{1,2,0:T(8,128)(2,1)S(1)}, bf16[2,192,256]{1,2,0:T(8,128)(2,1)S(1)}, u32[]{:S(2)}, u32[]{:S(2)}) collective-permute-start(bf16[2,192,256]{1,2,0:T(8,128)(2,1)S(1)} %get-tuple-element.69), channel_id=1, source_target_pairs={{8,0},{10,2},{12,4},{14,6},{16,8},{18,10},{20,12},{22,14},{24,16},... | collective-permute-start | bytes 589832 | tf_op jit(solution)/shard_map/ppermute | solution.py:63
  481.8 52.6 %copy-start.23 = (f32[384,128]{1,0:T(8,128)S(1)}, f32[384,128]{1,0:T(8,128)}, u32[]{:S(2)}) copy-start(f32[384,128]{1,0:T(8,128)} %get-tuple-element.125.sine) | copy-start | bytes 589828
  542.1 28.3 %collective-permute-start.11 = (bf16[384,1536]{1,0:T(8,128)(2,1)}, bf16[384,1536]{1,0:T(8,128)(2,1)}, u32[]{:S(2)}, u32[]{:S(2)}) collective-permute-start(bf16[384,1536]{1,0:T(8,128)(2,1)} %get-tuple-element.118), channel_id=1, source_target_pairs={{0,1},{1,0},{2,3},{3,2},{4,5},{5,4},{6,7},{7,6},{8,9},{9,8},{10,11... | collective-permute-start | bytes 3538952 | tf_op jit(solution)/shard_map/ppermute | solution.py:51
  545.8 26.9 %collective-permute-start.24 = (bf16[4,2,96,768]{3,2,0,1:T(8,128)(2,1)}, bf16[4,2,96,768]{3,2,0,1:T(8,128)(2,1)}, u32[]{:S(2)}, u32[]{:S(2)}) collective-permute-start(bf16[4,2,96,768]{3,2,0,1:T(8,128)(2,1)} %bitcast.339), channel_id=1, source_target_pairs={{0,2},{2,0},{1,3},{3,1},{4,6},{6,4},{5,7},{7,5},{8,10},{10,8},{9,1... | collective-permute-start | bytes 3538952 | tf_op jit(solution)/shard_map/ppermute | solution.py:51
  551.7 53.8 %collective-permute-start.16 = (bf16[4,2,96,1024]{3,2,0,1:T(8,128)(2,1)S(1)}, bf16[4,2,96,1024]{3,2,0,1:T(8,128)(2,1)S(1)}, u32[]{:S(2)}, u32[]{:S(2)}) collective-permute-start(bf16[4,2,96,1024]{3,2,0,1:T(8,128)(2,1)S(1)} %bitcast.365), channel_id=1, source_target_pairs={{0,2},{2,0},{1,3},{3,1},{4,6},{6,4},{5,7},{7,5},{8,10},{10,8},{9,1... | collective-permute-start | bytes 4718600 | tf_op jit(solution)/shard_map/ppermute | solution.py:51
  572.6 1.9 collective-permute-start.12
  574.5 3.9 collective-permute-start.13
  574.7 16.0 %collective-permute-start.25 = (bf16[4,96,768]{2,1,0:T(8,128)(2,1)S(1)}, bf16[4,96,768]{2,1,0:T(8,128)(2,1)S(1)}, u32[]{:S(2)}, u32[]{:S(2)}) collective-permute-start(bf16[4,96,768]{2,1,0:T(8,128)(2,1)S(1)} %dynamic-slice_bitcast_fusion.1), channel_id=1, source_target_pairs={{0,4},{4,0},{1,5},{5,1},{2,6},{6,2},{3,7},{7,3},{8,12},{12,8},{9,1... | collective-permute-start | bytes 1769480 | tf_op jit(solution)/shard_map/ppermute | solution.py:51
  578.4 3.7 collective-permute-start.14
  582.2 4.6 collective-permute-start.15
  590.8 6.1 collective-permute-start.26
  594.5 7.9 %collective-permute-start.29 = (bf16[96,768]{1,0:T(8,128)(2,1)S(1)}, bf16[96,768]{1,0:T(8,128)(2,1)S(1)}, u32[]{:S(2)}, u32[]{:S(2)}) collective-permute-start(bf16[96,768]{1,0:T(8,128)(2,1)S(1)} %get-tuple-element.79), channel_id=1, source_target_pairs={{24,16},{25,17},{26,18},{27,19},{28,20},{29,21},{30,22},{31,23}} | collective-permute-start | bytes 442376 | tf_op jit(solution)/shard_map/ppermute | solution.py:111
  596.9 7.1 %collective-permute-start.27 = (bf16[96,768]{1,0:T(8,128)(2,1)S(1)}, bf16[96,768]{1,0:T(8,128)(2,1)S(1)}, u32[]{:S(2)}, u32[]{:S(2)}) collective-permute-start(bf16[96,768]{1,0:T(8,128)(2,1)S(1)} %fusion.89), channel_id=1, source_target_pairs={{0,8},{8,16},{1,9},{9,17},{2,10},{10,18},{3,11},{11,19},{4,12},{12... | collective-permute-start | bytes 442376 | tf_op jit(solution)/shard_map/ppermute | solution.py:110
  604.7 8.7 %collective-permute-start.30 = (bf16[96,768]{1,0:T(8,128)(2,1)S(1)}, bf16[96,768]{1,0:T(8,128)(2,1)S(1)}, u32[]{:S(2)}, u32[]{:S(2)}) collective-permute-start(bf16[96,768]{1,0:T(8,128)(2,1)S(1)} %get-tuple-element.77), channel_id=1, source_target_pairs={{16,8},{24,16},{17,9},{25,17},{18,10},{26,18},{19,11},{27,19},{20,... | collective-permute-start | bytes 442376 | tf_op jit(solution)/shard_map/ppermute | solution.py:111
  607.2 20.7 %collective-permute-start.17 = (bf16[4,96,1024]{2,1,0:T(8,128)(2,1)}, bf16[4,96,1024]{2,1,0:T(8,128)(2,1)S(1)}, u32[]{:S(2)}, u32[]{:S(2)}) collective-permute-start(bf16[4,96,1024]{2,1,0:T(8,128)(2,1)} %dynamic-slice_bitcast_fusion), channel_id=1, source_target_pairs={{0,4},{4,0},{1,5},{5,1},{2,6},{6,2},{3,7},{7,3},{8,12},{12,8},{9,1... | collective-permute-start | bytes 2359304 | tf_op jit(solution)/shard_map/ppermute | solution.py:51
  608.5 21.1 %collective-permute-start.28 = (bf16[96,768]{1,0:T(8,128)(2,1)}, bf16[96,768]{1,0:T(8,128)(2,1)S(1)}, u32[]{:S(2)}, u32[]{:S(2)}) collective-permute-start(bf16[96,768]{1,0:T(8,128)(2,1)} %get-tuple-element.76), channel_id=1, source_target_pairs={{0,8},{8,16},{16,24},{1,9},{9,17},{17,25},{2,10},{10,18},{18,26},{... | collective-permute-start | bytes 442376 | tf_op jit(solution)/shard_map/ppermute | solution.py:110
  614.2 20.5 %collective-permute-start.31 = (bf16[96,768]{1,0:T(8,128)(2,1)}, bf16[96,768]{1,0:T(8,128)(2,1)}, u32[]{:S(2)}, u32[]{:S(2)}) collective-permute-start(bf16[96,768]{1,0:T(8,128)(2,1)} %fusion.88), channel_id=1, source_target_pairs={{8,0},{16,8},{24,16},{9,1},{17,9},{25,17},{10,2},{18,10},{26,18},{... | collective-permute-start | bytes 442376 | tf_op jit(solution)/shard_map/ppermute | solution.py:111
  617.3 25.1 %collective-permute-start.36 = (bf16[2,96,1152]{2,1,0:T(8,128)(2,1)}, bf16[2,96,1152]{2,1,0:T(8,128)(2,1)}, u32[]{:S(2)}, u32[]{:S(2)}) collective-permute-start(bf16[2,96,1152]{2,1,0:T(8,128)(2,1)} %dynamic-slice_bitcast_fusion.2), channel_id=1, source_target_pairs={{0,4},{4,0},{1,5},{5,1},{2,6},{6,2},{3,7},{7,3},{8,12},{12,8},{9,1... | collective-permute-start | bytes 1327112 | tf_op jit(solution)/shard_map/ppermute | solution.py:51
  619.9 27.0 %collective-permute-start.34 = (bf16[2,96,1152]{2,1,0:T(8,128)(2,1)}, bf16[2,96,1152]{2,1,0:T(8,128)(2,1)S(1)}, u32[]{:S(2)}, u32[]{:S(2)}) collective-permute-start(bf16[2,96,1152]{2,1,0:T(8,128)(2,1)} %dynamic-slice_bitcast_fusion.3), channel_id=1, source_target_pairs={{0,4},{4,0},{1,5},{5,1},{2,6},{6,2},{3,7},{7,3},{8,12},{12,8},{9,1... | collective-permute-start | bytes 1327112 | tf_op jit(solution)/shard_map/ppermute | solution.py:51
  627.9 25.3 %collective-permute-start.32 = (bf16[2,96,1152]{2,1,0:T(8,128)(2,1)S(1)}, bf16[2,96,1152]{2,1,0:T(8,128)(2,1)S(1)}, u32[]{:S(2)}, u32[]{:S(2)}) collective-permute-start(bf16[2,96,1152]{2,1,0:T(8,128)(2,1)S(1)} %dynamic-slice_bitcast_fusion.4), channel_id=1, source_target_pairs={{0,4},{4,0},{1,5},{5,1},{2,6},{6,2},{3,7},{7,3},{8,12},{12,8},{9,1... | collective-permute-start | bytes 1327112 | tf_op jit(solution)/shard_map/ppermute | solution.py:51
  629.5 8.4 %collective-permute-start.18 = (bf16[96,1024]{1,0:T(8,128)(2,1)S(1)}, bf16[96,1024]{1,0:T(8,128)(2,1)S(1)}, u32[]{:S(2)}, u32[]{:S(2)}) collective-permute-start(bf16[96,1024]{1,0:T(8,128)(2,1)S(1)} %get-tuple-element.74), channel_id=1, source_target_pairs={{0,8},{1,9},{2,10},{3,11},{4,12},{5,13},{6,14},{7,15}} | collective-permute-start | bytes 589832 | tf_op jit(solution)/shard_map/ppermute | solution.py:110
  636.3 17.0 %collective-permute-start.21 = (bf16[96,1024]{1,0:T(8,128)(2,1)S(1)}, bf16[96,1024]{1,0:T(8,128)(2,1)S(1)}, u32[]{:S(2)}, u32[]{:S(2)}) collective-permute-start(bf16[96,1024]{1,0:T(8,128)(2,1)S(1)} %get-tuple-element.75), channel_id=1, source_target_pairs={{24,16},{25,17},{26,18},{27,19},{28,20},{29,21},{30,22},{31,23}} | collective-permute-start | bytes 589832 | tf_op jit(solution)/shard_map/ppermute | solution.py:111
  638.0 15.4 %collective-permute-start.19 = (bf16[96,1024]{1,0:T(8,128)(2,1)S(1)}, bf16[96,1024]{1,0:T(8,128)(2,1)S(1)}, u32[]{:S(2)}, u32[]{:S(2)}) collective-permute-start(bf16[96,1024]{1,0:T(8,128)(2,1)S(1)} %fusion.74), channel_id=1, source_target_pairs={{0,8},{8,16},{1,9},{9,17},{2,10},{10,18},{3,11},{11,19},{4,12},{12... | collective-permute-start | bytes 589832 | tf_op jit(solution)/shard_map/ppermute | solution.py:110
  643.6 17.5 %collective-permute-start.37 = (bf16[2,96,1152]{2,1,0:T(8,128)(2,1)S(1)}, bf16[2,96,1152]{2,1,0:T(8,128)(2,1)S(1)}, u32[]{:S(2)}, u32[]{:S(2)}) collective-permute-start(bf16[2,96,1152]{2,1,0:T(8,128)(2,1)S(1)} %fusion.54), channel_id=1, source_target_pairs={{0,2},{2,0},{1,3},{3,1},{4,6},{6,4},{5,7},{7,5},{8,10},{10,8},{9,1... | collective-permute-start | bytes 1327112 | tf_op jit(solution)/shard_map/ppermute | solution.py:51
  647.1 14.2 %collective-permute-start.35 = (bf16[2,96,1152]{2,1,0:T(8,128)(2,1)S(1)}, bf16[2,96,1152]{2,1,0:T(8,128)(2,1)S(1)}, u32[]{:S(2)}, u32[]{:S(2)}) collective-permute-start(bf16[2,96,1152]{2,1,0:T(8,128)(2,1)S(1)} %fusion.58), channel_id=1, source_target_pairs={{0,2},{2,0},{1,3},{3,1},{4,6},{6,4},{5,7},{7,5},{8,10},{10,8},{9,1... | collective-permute-start | bytes 1327112 | tf_op jit(solution)/shard_map/ppermute | solution.py:51
  653.5 6.2 collective-permute-start.22
  654.3 7.2 %collective-permute-start.33 = (bf16[2,96,1152]{2,1,0:T(8,128)(2,1)S(1)}, bf16[2,96,1152]{2,1,0:T(8,128)(2,1)S(1)}, u32[]{:S(2)}, u32[]{:S(2)}) collective-permute-start(bf16[2,96,1152]{2,1,0:T(8,128)(2,1)S(1)} %fusion.62), channel_id=1, source_target_pairs={{0,2},{2,0},{1,3},{3,1},{4,6},{6,4},{5,7},{7,5},{8,10},{10,8},{9,1... | collective-permute-start | bytes 1327112 | tf_op jit(solution)/shard_map/ppermute | solution.py:51
  654.4 11.3 %collective-permute-start.20 = (bf16[96,1024]{1,0:T(8,128)(2,1)S(1)}, bf16[96,1024]{1,0:T(8,128)(2,1)S(1)}, u32[]{:S(2)}, u32[]{:S(2)}) collective-permute-start(bf16[96,1024]{1,0:T(8,128)(2,1)S(1)} %get-tuple-element.72), channel_id=1, source_target_pairs={{0,8},{8,16},{16,24},{1,9},{9,17},{17,25},{2,10},{10,18},{18,26},{... | collective-permute-start | bytes 589832 | tf_op jit(solution)/shard_map/ppermute | solution.py:110
  659.8 10.2 %collective-permute-start.23 = (bf16[96,1024]{1,0:T(8,128)(2,1)S(1)}, bf16[96,1024]{1,0:T(8,128)(2,1)S(1)}, u32[]{:S(2)}, u32[]{:S(2)}) collective-permute-start(bf16[96,1024]{1,0:T(8,128)(2,1)S(1)} %fusion.73), channel_id=1, source_target_pairs={{8,0},{16,8},{24,16},{9,1},{17,9},{25,17},{10,2},{18,10},{26,18},{... | collective-permute-start | bytes 589832 | tf_op jit(solution)/shard_map/ppermute | solution.py:111
  (68 other events, 519.5 us)
Sparse Core Ops, SparseCore 0:
  296.2 75.4 reduce-scatter.7
  374.0 66.6 reduce-scatter.5
  443.0 90.2 reduce-scatter.3

commit v3 on v2

--- a/solution.py
+++ b/solution.py
@@ -12,7 +12,7 @@
 BACK = 5
 LINE = 4
 LANES = 128
-VMEM_BYTES = 56 * 1024 * 1024
+VMEM_BYTES = 62 * 1024 * 1024
 
 EPSILON = 1e-06
 THETA = 1000000.0
@@ -302,10 +302,23 @@
     def receive(self, which, target, via):
         self._make(which, target, target, via).wait_recv()
 
-    def finish(self):
-        for which, source, target, to, cond in self.sent:
-            only(cond, lambda: self._make(which, source, target, to).wait_send())
-        self.sent = []
+    def settle(self, until=None):
+        until = len(self.sent) if until is None else until
+        for i in range(until):
+            if self.sent[i] is not None:
+                which, source, target, to, cond = self.sent[i]
+                only(cond, lambda: self._make(which, source, target, to).wait_send())
+                self.sent[i] = None
+
+    def left(self, which):
+        for i, entry in enumerate(self.sent):
+            if entry is not None and entry[0] == which:
+                _, source, target, to, cond = entry
+                only(cond, lambda: self._make(which, source, target, to).wait_send())
+                self.sent[i] = None
+
+    def mark(self):
+        return len(self.sent)
 
 
 def only(cond, action):
@@ -323,6 +336,8 @@
         self.pair, self.core = {PAIR: 1 - self.p}, {CORE: 1 - self.c}
         self.cross = {PAIR: 1 - self.p, CORE: 1 - self.c}
         self.other = {TENSOR: 1 - self.y}
+        self.near = {RING: self.z + 1 - 2 * (self.z % 2)}
+        self.far = {RING: self.z + 2 - 4 * (self.z // 2)}
         self.right, self.left = {RING: self.z + 1}, {RING: self.z - 1}
         self.has_right, self.has_left = self.z < LINE - 1, self.z > 0
 
@@ -342,6 +357,7 @@
 
         for to in (self.pair, self.core, self.cross, self.other):
             greet(to)
+        greet(self.far)
         greet(self.right, self.has_right)
         greet(self.left, self.has_left)
         for back in range(1, BACK + 1):
@@ -349,7 +365,7 @@
             greet(self.ranked(self.rank - back), self.rank >= back)
         line = jnp.minimum(self.z, 1) + jnp.minimum(LINE - 1 - self.z, 1)
         reach = jnp.minimum(self.rank, BACK) + jnp.minimum(4 * LINE - 1 - self.rank, BACK)
-        pl.semaphore_wait(barrier, 4 + line + reach)
+        pl.semaphore_wait(barrier, 5 + line + reach)
 
 
 class LineFlow:
@@ -496,11 +512,12 @@
 class FourFlow:
     def __init__(self, copies, place, slots, parts):
         self.copies, self.place, self.slots = copies, place, slots
-        self.size = slots.shape[1] // parts
+        self.rows = slots.shape[0] // 4
+        self.size = self.rows // parts
         self.ids = [[copies.new() for _ in range(3)] for _ in range(parts)]
 
     def slot(self, which, part):
-        return self.slots.at[which, pl.ds(part * self.size, self.size)]
+        return self.slots.at[pl.ds(which * self.rows + part * self.size, self.size)]
 
     def send(self, part, source):
         self.copies.send(self.ids[part][0], source, self.slot(1, part), self.place.pair)
@@ -516,11 +533,186 @@
         self.copies.receive(self.ids[part][2], self.slot(3, part), self.place.core)
 
 
+def fetch(source, target, sem):
+    copy = pltpu.make_async_copy(source, target, sem)
+    copy.start()
+    copy.wait()
+
+
+def add_to(target, source):
+    target[...] = low(wide(target[...]) + wide(source[...]))
+
+
+class LineScatter:
+    def __init__(self, copies, place, block, arrived, stage, sem):
+        self.copies, self.place, self.block = copies, place, block
+        self.arrived, self.stage, self.sem = arrived, stage, sem
+        self.ids = {(way, step): copies.new() for way in (1, -1) for step in range(1, LINE)}
+
+    def landing(self, way, step):
+        return self.arrived.at[(1 - way) // 2, step - 1]
+
+    def target(self, way, step):
+        return self.block(self.place.z + way * (LINE - step))
+
+    def takes(self, way, step):
+        z = self.place.z
+        if way == 1:
+            return (z >= 1) & (z <= step)
+        return (z <= LINE - 2) & (z >= LINE - 1 - step)
+
+    def send(self, way, step, cond):
+        to = self.place.right if way == 1 else self.place.left
+        self.copies.send(
+            self.ids[way, step], self.target(way, step), self.landing(way, step), to, cond
+        )
+
+    def start(self):
+        for step in range(1, LINE):
+            self.send(1, step, self.place.z == 0)
+            self.send(-1, step, self.place.z == LINE - 1)
+
+    def take(self, way, step):
+        via = self.place.left if way == 1 else self.place.right
+        self.copies.receive(self.ids[way, step], self.landing(way, step), via)
+        fetch(self.landing(way, step), self.stage, self.sem)
+
+    def step(self, step):
+        for way in (1, -1):
+            there = self.takes(way, step - 1)
+
+            def add(way=way):
+                self.take(way, step - 1)
+                add_to(self.target(way, step), self.stage)
+
+            pl.when(there)(add)
+            self.send(way, step, there)
+
+    def finish(self, add):
+        for way in (1, -1):
+
+            def last(way=way):
+                self.take(way, LINE - 1)
+                add()
+
+            pl.when(self.takes(way, LINE - 1))(last)
+
+
+class QuarterScatter:
+    def __init__(self, copies, place, grad, owner, arrived, stage, sem):
+        self.copies, self.place, self.grad, self.owner, self.sem = copies, place, grad, owner, sem
+        self.stage = stage
+        self.count, self.width = owner.shape[0], grad.shape[1]
+        self.line = LineScatter(copies, place, self.block, arrived, stage, sem)
+        self.near = (
+            (copies.new(), 1 - place.p, place.c, place.pair),
+            (copies.new(), place.p, 1 - place.c, place.core),
+            (copies.new(), 1 - place.p, 1 - place.c, place.cross),
+        )
+
+    def block(self, origin):
+        count = 4 * self.count
+        return self.grad.at[pl.ds(pl.multiple_of(origin * count, count), count)]
+
+    def rows(self, p, c):
+        count = self.count
+        start = (self.place.z * 4 + p * 2 + c) * count
+        return self.grad.at[pl.ds(pl.multiple_of(start, count), count)]
+
+    def columns(self, p, c):
+        width = self.width
+        return self.owner.at[:, pl.ds(pl.multiple_of((p * 2 + c) * width, LANES), width)]
+
+    def finish(self):
+        place = self.place
+        self.line.finish(lambda: add_to(self.block(place.z), self.stage))
+        for which, p, c, to in self.near:
+            self.copies.send(which, self.rows(p, c), self.columns(place.p, place.c), to)
+        fetch(self.rows(place.p, place.c), self.columns(place.p, place.c), self.sem)
+
+    def end(self):
+        for which, p, c, to in self.near:
+            self.copies.receive(which, self.columns(p, c), to)
+
+
+class RowsScatter:
+    def __init__(self, copies, place, whole, from_core, from_pair, arrived, stage, sem):
+        self.copies, self.place, self.whole, self.sem = copies, place, whole, sem
+        self.from_core, self.from_pair = from_core, from_pair
+        self.count, self.columns = from_pair.shape[1], from_pair.shape[2]
+        self.stage = stage
+        self.core_id = copies.new()
+        self.pair_ids = [copies.new() for _ in range(LINE)]
+        self.line = LineScatter(
+            copies, place, lambda d: self.part(place.c, place.p, d), arrived, self.small(1), sem
+        )
+
+    def small(self, blocks):
+        return self.stage.at[pl.ds(0, blocks * self.count), pl.ds(0, self.columns)]
+
+    def part(self, c, p, origin, blocks=1):
+        start = ((c * 2 + p) * LINE + origin) * self.count
+        return self.whole.at[
+            pl.ds(pl.multiple_of(start, self.count), blocks * self.count), pl.ds(0, self.columns)
+        ]
+
+    def fill(self, origin, value):
+        for p in range(2):
+            for c in range(2):
+                start = (p * 2 + c) * self.count
+                self.part(c, p, origin)[...] = value[start : start + self.count]
+
+    def start(self):
+        place = self.place
+        self.copies.send(
+            self.core_id, self.part(1 - place.c, 0, 0, 2 * LINE), self.from_core, place.core
+        )
+
+    def halve(self):
+        place = self.place
+        self.copies.receive(self.core_id, self.from_core, place.core)
+        size = LINE * self.count
+        for p in (1 - place.p, place.p):
+            start = pl.multiple_of(p * size, size)
+            fetch(self.from_core.at[pl.ds(start, size)], self.small(LINE), self.sem)
+            add_to(self.part(place.c, p, 0, LINE), self.small(LINE))
+            if p is place.p:
+                continue
+            for origin in (3, 0, 2, 1):
+                self.copies.send(
+                    self.pair_ids[origin],
+                    self.part(place.c, p, origin),
+                    self.from_pair.at[origin],
+                    place.pair,
+                )
+
+    def quarter(self):
+        place = self.place
+        for origin in (3, 0, 2, 1):
+            self.copies.receive(self.pair_ids[origin], self.from_pair.at[origin], place.pair)
+            fetch(self.from_pair.at[origin], self.small(1), self.sem)
+            add_to(self.part(place.c, place.p, origin), self.small(1))
+        self.line.start()
+
+    def finish(self, out):
+        out[...] = wide(self.part(self.place.c, self.place.p, self.place.z)[...])
+
+        def add():
+            out[...] += wide(self.small(1)[...])
+
+        self.line.finish(add)
+
+
 PARTS = 4
-N_REMOTE = 160
-
-
-def forward_kernel(
+N_REMOTE = 200
+SUM_ROWS = 32
+
+
+def eight_rows(value):
+    return jnp.sum(value.reshape(-1, 8, value.shape[-1]), axis=0)
+
+
+def layer_kernel(
     heads,
     head_size,
     tokens,
@@ -533,27 +725,59 @@
     biases,
     cosine,
     sine,
-    allowed,
-    first_out,
-    w_out_out,
+    own_segments,
+    own_positions,
+    key_segments,
+    key_positions,
+    output,
+    input_grad,
+    grad_first,
+    grad_w_out,
+    grad_w_down,
+    grad_w_gate,
+    grad_w_up,
+    sums_out,
+    first_kept,
+    line_landing,
+    out_core_landing,
+    out_pair_landing,
+    out_other_landing,
+    first_core_landing,
+    first_pair_landing,
+    first_line_landing,
+    wo_core_landing,
+    wo_pair_landing,
+    wo_line_landing,
+    first_all,
+    w_out_all,
+    state,
+    window,
+    keys,
+    values,
+    mail,
+    first_normed,
+    query,
+    heads_out,
     gate_all,
     up_all,
     down_all,
-    grad_out_four,
     normed_four,
-    query_out,
-    window_out,
-    heads_out,
-    residual_out,
-    first_all,
-    w_out_all,
-    unit,
-    window,
-    keys,
-    values,
-    part_own,
-    part_other,
-    normed,
+    grad_four,
+    hidden,
+    grad_gate,
+    grad_up,
+    pair_landing,
+    other_landing,
+    stage,
+    grad_keys,
+    grad_values,
+    own_grad,
+    window_landing,
+    first_scale,
+    second_scale,
+    totals,
+    sums,
+    sums_landing,
     send_sems,
     recv_sems,
     local_sems,
@@ -561,67 +785,69 @@
     place = Place()
     copies = Copies(send_sems, recv_sems)
     rows, width = tokens.shape
-    batches = allowed.shape[0]
+    batches = own_segments.shape[0]
     per_batch = rows // batches
     query_width = heads * head_size
     kv_width = query_width + 2 * head_size
+    size = rows // PARTS
+    root = 1.0 / math.sqrt(head_size)
+    sem = local_sems.at[0]
 
     window[...] = jnp.zeros_like(window)
     place.meet()
 
     first = RowsFlow(copies, place, first_shard, first_all)
     outs = RowsFlow(copies, place, out_shard, w_out_all)
-    quarters = [
+    gates, ups, downs = [
         QuarterFlow(copies, place, shard, whole, local_sems.at[2 + i])
         for i, (shard, whole) in enumerate(
             ((gate_shard, gate_all), (up_shard, up_all), (down_shard, down_all))
         )
     ]
-    cot = FourFlow(copies, place, grad_out_four, 1)
+    cot = FourFlow(copies, place, grad_four, 1)
     second = FourFlow(copies, place, normed_four, PARTS)
     part_ids = [copies.new() for _ in range(PARTS)]
     window_ids = [copies.new() for _ in range(BACK)]
 
     def put(flow, sem):
-        def run():
-            copy = pltpu.make_async_copy(flow.shard, flow.rows(place.z, place.p, place.c), sem)
-            copy.start()
-            copy.wait()
-
-        return run
-
-    first.start(put(first, local_sems.at[0]))
-    quarters[0].start()
+        return lambda: fetch(flow.shard, flow.rows(place.z, place.p, place.c), sem)
+
+    first.start(put(first, sem))
+    gates.start()
     x = wide(tokens[...])
-    scale_row = lax.rsqrt(jnp.mean(x * x, axis=-1, keepdims=True) + EPSILON)
-    unit[...] = x * scale_row
+    first_scale[...] = lax.rsqrt(jnp.mean(x * x, axis=-1, keepdims=True) + EPSILON)
+    state[...] = x * first_scale[...]
     first.crossing(0)
     first.arrive(1)
-    quarters[1].start()
+    ups.start()
     first.crossing(1)
-    quarters[0].join()
+    gates.join()
     first.arrive(2)
     first.crossing(2)
     first.arrive(3)
-    quarters[2].start()
+    downs.start()
     first.crossing(3)
-    quarters[1].join()
+    ups.join()
     first.end()
 
     gains = wide(first_all[:, kv_width:]).T
     first_gain, second_gain = gains[0:1], gains[1:2]
-    first_normed = low(unit[...] * first_gain)
+    first_normed[...] = low(state[...] * first_gain)
     sign = jnp.where(
         lax.broadcasted_iota(jnp.int32, (1, head_size), 1) < head_size // 2, -1.0, 1.0
     )
-    turn_sine = sine[...] * sign
 
     def project(start, size):
-        raw = matmul(first_normed, first_all[:, start : start + size])
+        raw = matmul(first_normed[...], first_all[:, start : start + size])
         return raw + biases[:, start : start + size]
 
     def turned(raw):
-        return low(raw * cosine[...] + pltpu.roll(raw, head_size // 2, 1) * turn_sine)
+        half_turn = pltpu.roll(raw, head_size // 2, 1)
+        return low(raw * cosine[...] + half_turn * (sine[...] * sign))
+
+    def turned_back(gradient, mine):
+        half_turn = pltpu.roll(gradient * sine[mine], head_size // 2, 1)
+        return low(gradient * cosine[mine] - half_turn * sign)
 
     kv = project(query_width, 2 * head_size)
     key_now, value_now = turned(kv[:, :head_size]), low(kv[:, head_size:])
@@ -637,19 +863,20 @@
             place.ranked(place.rank + back),
             place.rank + back < 4 * LINE,
         )
-    outs.start(put(outs, local_sems.at[1]))
-    quarters[2].join()
+    outs.start(put(outs, sem))
     for h in range(0, heads, 2):
         raw = project(h * head_size, 2 * head_size)
-        query_out[:, h * head_size : (h + 1) * head_size] = turned(raw[:, :head_size])
-        query_out[:, (h + 1) * head_size : (h + 2) * head_size] = turned(raw[:, head_size:])
-    cot_own = pltpu.make_async_copy(grad_out, grad_out_four.at[0], local_sems.at[5])
+        query[:, h * head_size : (h + 1) * head_size] = turned(raw[:, :head_size])
+        query[:, (h + 1) * head_size : (h + 2) * head_size] = turned(raw[:, head_size:])
+    keep_first = pltpu.make_async_copy(first_all, first_kept, local_sems.at[1])
+    keep_first.start()
+    cot_own = pltpu.make_async_copy(grad_out, cot.slot(0, 0), local_sems.at[5])
     cot_own.start()
     cot.send(0, grad_out)
     outs.crossing(0)
     outs.arrive(1)
     outs.crossing(1)
-    quarters[0].arrive(1)
+    gates.arrive(1)
     outs.arrive(2)
     outs.crossing(2)
     for back in range(1, BACK + 1):
@@ -660,20 +887,26 @@
             ),
         )
 
-    root = 1.0 / math.sqrt(head_size)
-    size = rows // PARTS
-    for b in range(batches):
+    def take_window(b):
         for slot in range(BACK + 1):
             keys[slot * per_batch : (slot + 1) * per_batch] = window[slot, b, :, :head_size]
             values[slot * per_batch : (slot + 1) * per_batch] = window[slot, b, :, head_size:]
 
-        def attend_head(h, carry, b=b):
+    def probabilities(b, mine, columns):
+        scores = times_transpose(query[mine, columns], keys[...]) * root
+        allowed = (own_segments[b] == key_segments[b]) & (key_positions[b] <= own_positions[b])
+        scores = jnp.where(allowed, scores, NEGATIVE)
+        weights = jnp.exp(scores - jnp.max(scores, axis=-1, keepdims=True))
+        return weights * (1.0 / jnp.sum(weights, axis=-1, keepdims=True))
+
+    part_own, part_other = mail.at[pl.ds(0, rows)], mail.at[pl.ds(rows, rows)]
+    for b in range(batches):
+        take_window(b)
+        mine = slice(b * per_batch, (b + 1) * per_batch)
+
+        def attend_head(h, carry, b=b, mine=mine):
             columns = pl.ds(pl.multiple_of(h * head_size, head_size), head_size)
-            mine = slice(b * per_batch, (b + 1) * per_batch)
-            scores = times_transpose(query_out[mine, columns], keys[...]) * root
-            scores = jnp.where(allowed[b] > 0.0, scores, NEGATIVE)
-            weights = jnp.exp(scores - jnp.max(scores, axis=-1, keepdims=True))
-            probs = low(weights * (1.0 / jnp.sum(weights, axis=-1, keepdims=True)))
+            probs = low(probabilities(b, mine, columns))
             heads_out[mine, columns] = low(matmul(probs, values[...]))
             return carry
 
@@ -682,97 +915,430 @@
             outs.arrive(3)
             outs.crossing(3)
             outs.end()
-            quarters[1].arrive(1)
-        part = low(times_transpose(heads_out[b * per_batch : (b + 1) * per_batch], w_out_all[...]))
-        part_own[b * per_batch : (b + 1) * per_batch] = part
+            ups.arrive(1)
+        part = low(times_transpose(heads_out[mine], w_out_all[...]))
+        part_own[mine] = part
         for i in range(b * per_batch // size, (b + 1) * per_batch // size):
             block = pl.ds(i * size, size)
             copies.send(part_ids[i], part_own.at[block], part_other.at[block], place.other)
-        if b == 0:
-            quarters[2].arrive(1)
+    early = copies.mark()
+    gates.arrive(2)
 
     for i in range(PARTS):
         block = pl.ds(i * size, size)
         copies.receive(part_ids[i], part_other.at[block], place.other)
-        state = wide(tokens[block]) + (wide(part_own[block]) + wide(part_other[block]))
-        residual_out[block] = state
-        scale_row = lax.rsqrt(jnp.mean(state * state, axis=-1, keepdims=True) + EPSILON)
-        normed[block] = low(state * scale_row * second_gain)
-        second.send(i, normed.at[block])
+        copies.left(part_ids[i])
+        row_sum = wide(tokens[block]) + (wide(part_own[block]) + wide(part_other[block]))
+        state[block] = row_sum
+        scale_row = lax.rsqrt(jnp.mean(row_sum * row_sum, axis=-1, keepdims=True) + EPSILON)
+        second_scale[block] = scale_row
+        second.slot(0, i)[...] = low(row_sum * scale_row * second_gain)
+        second.send(i, second.slot(0, i))
         if i > 0:
             second.cross(i - 1)
-    second_own = pltpu.make_async_copy(normed, normed_four.at[0], local_sems.at[6])
-    second_own.start()
+    ups.arrive(2)
     second.cross(PARTS - 1)
-    for flow in quarters:
-        flow.arrive(2)
+    downs.join()
     cot.cross(0)
-    first_copy = pltpu.make_async_copy(first_all, first_out, local_sems.at[0])
-    first_copy.start()
-    outs_copy = pltpu.make_async_copy(w_out_all, w_out_out, local_sems.at[1])
-    outs_copy.start()
-    window_out[...] = window[...]
+    keep_first.wait()
     for i in range(PARTS):
         second.end(i)
+    cot_own.wait()
+    gates.arrive(3)
+    ups.arrive(3)
+
+    tile = 256
+
+    def forward_tile(t, carry):
+        block = pl.ds(pl.multiple_of(t * tile, tile), tile)
+        gate = matmul(normed_four[block], gate_all[...])
+        up = matmul(normed_four[block], up_all[...])
+        sigmoid = 1.0 / (1.0 + jnp.exp(-gate))
+        silu = gate * sigmoid
+        hidden[block] = low(silu * up)
+        grad_up[block] = low(silu)
+        grad_gate[block] = low(up * sigmoid * (1.0 + gate * (1.0 - sigmoid)))
+        return carry
+
+    lax.fori_loop(0, 4 * rows // tile, forward_tile, 0)
     cot.end(0)
-    for flow in quarters:
-        flow.arrive(3)
-    for copy in (cot_own, second_own, first_copy, outs_copy):
-        copy.wait()
-    copies.finish()
-
-
-def forward_call(heads, head_size, operands):
+    downs.arrive(1)
+    copies.settle(early)
+    grad_down = first_all
+
+    def columns_of(d):
+        return pl.ds(pl.multiple_of(d * rows, rows), rows)
+
+    def weight_grad(target, left_side, right_side):
+        def block(d, carry):
+            part = contract_rows(left_side[:, columns_of(d)], right_side[...])
+            target[columns_of(d)] = low(part)
+            return carry
+
+        lax.fori_loop(0, LINE, block, 0)
+
+    scatters = [
+        QuarterScatter(copies, place, grad, owner, line_landing.at[i], stage, sem)
+        for i, (grad, owner) in enumerate(
+            ((grad_down, grad_w_down), (up_all, grad_w_up), (gate_all, grad_w_gate))
+        )
+    ]
+    down_back, up_back, gate_back = scatters
+    weight_grad(grad_down, grad_four, hidden)
+    late = copies.mark()
+    down_back.line.start()
+    downs.arrive(2)
+    downs.arrive(3)
+
+    def backward_tile(t, carry):
+        block = pl.ds(pl.multiple_of(t * tile, tile), tile)
+        back = matmul(grad_four[block], down_all[...])
+        grad_gate[block] = low(back * wide(grad_gate[block]))
+        grad_up[block] = low(back * wide(grad_up[block]))
+        return carry
+
+    lax.fori_loop(0, 4 * rows // tile, backward_tile, 0)
+    copies.settle(late)
+
+    normed_grad = grad_four
+    core_ids = [copies.new() for _ in range(2)]
+    pair_ids = [copies.new() for _ in range(PARTS)]
+    other_ids = [copies.new() for _ in range(PARTS)]
+
+    def slot(which, part=0, parts=1):
+        return pl.ds(which * rows + part * (rows // parts), rows // parts)
+
+    def normed_tile(t, carry):
+        block = columns_of(3 - t)
+        normed_grad[block] = low(
+            times_transpose(grad_gate[block], gate_all[...])
+            + times_transpose(grad_up[block], up_all[...])
+        )
+        return carry
+
+    lax.fori_loop(0, 2, normed_tile, 0)
+    for i in (1, 0):
+        copies.send(
+            core_ids[i],
+            normed_grad.at[slot(2 + i)],
+            mail.at[pl.ds(i * rows, rows)],
+            place.core,
+        )
+    lax.fori_loop(2, 4, normed_tile, 0)
+    copies.receive(core_ids[1], mail.at[pl.ds(rows, rows)], place.core)
+    for i in range(PARTS):
+        block = slot(1, i, PARTS)
+        add_to(normed_grad.at[block], mail.at[pl.ds(rows + i * size, size)])
+        copies.send(
+            pair_ids[i],
+            normed_grad.at[block],
+            pair_landing.at[pl.ds(i * size, size)],
+            place.pair,
+        )
+    copies.receive(core_ids[0], mail.at[pl.ds(0, rows)], place.core)
+    add_to(normed_grad.at[slot(0)], mail.at[pl.ds(0, rows)])
+    weight_grad(up_all, normed_four, grad_up)
+    up_back.line.start()
+    down_back.line.step(2)
+    out_sum = normed_four
+    out_core_id, out_pair_id, out_other_id = copies.new(), copies.new(), copies.new()
+    first_weights = hidden
+    first_fetch = pltpu.make_async_copy(first_kept, first_weights, local_sems.at[6])
+
+    def out_tile(t, carry):
+        block = columns_of(t)
+        out_sum[block] = low(times_transpose(hidden[block], down_all[...]))
+        return carry
+
+    for i in range(PARTS):
+        block = pl.ds(i * size, size)
+        copies.receive(pair_ids[i], pair_landing.at[block], place.pair)
+        add_to(normed_grad.at[block], pair_landing.at[block])
+        copies.send(other_ids[i], normed_grad.at[block], other_landing.at[block], place.other)
+        if i == 0:
+            weight_grad(gate_all, normed_four, grad_gate)
+            gate_back.line.start()
+        if i == 1:
+            lax.fori_loop(0, 4, out_tile, 0)
+            copies.send(
+                out_core_id, out_sum.at[pl.ds(2 * rows, 2 * rows)], out_core_landing, place.core
+            )
+            first_fetch.start()
+    down_back.line.step(3)
+    grad_own = mail.at[pl.ds(rows, rows)]
+    grad_branch = mail.at[pl.ds(0, rows)]
+    fetch(grad_out, grad_own, sem)
+    second_sum = totals.at[:, pl.ds(kv_width, width)]
+    second_sum[...] = jnp.zeros_like(second_sum)
+    for i in range(PARTS):
+        block = pl.ds(i * size, size)
+        copies.receive(other_ids[i], other_landing.at[block], place.other)
+        back = wide(normed_grad[block]) + wide(other_landing[block])
+        scale_row = second_scale[block]
+        unit = state[block] * scale_row
+        second_sum[...] += eight_rows(back * unit)
+        grad_state = wide(grad_own[block]) + norm_back(back, unit, scale_row, second_gain)
+        input_grad[block] = grad_state
+        grad_branch[block] = low(grad_state)
+
+    grad_heads = grad_up.at[pl.ds(0, rows), pl.ds(0, query_width)]
+    grad_raw = grad_up.at[pl.ds(rows, rows), pl.ds(0, kv_width)]
+    grad_heads[...] = low(matmul(grad_branch[...], w_out_all[...]))
+    wo_back = RowsScatter(
+        copies, place, w_out_all, wo_core_landing, wo_pair_landing, wo_line_landing, stage, sem
+    )
+    for origin in range(LINE):
+        branch = grad_branch[:, origin * rows : (origin + 1) * rows]
+        wo_back.fill(origin, low(contract_rows(branch, heads_out[...])))
+    wo_back.start()
+    down_back.finish()
+    back_ids = [[copies.new() for _ in range(batches)] for _ in range(BACK)]
+    for b in range(batches):
+        take_window(b)
+        mine = slice(b * per_batch, (b + 1) * per_batch)
+        grad_keys[...] = jnp.zeros_like(grad_keys)
+        grad_values[...] = jnp.zeros_like(grad_values)
+
+        def attend_back_head(h, carry, b=b, mine=mine):
+            columns = pl.ds(pl.multiple_of(h * head_size, head_size), head_size)
+            probs = probabilities(b, mine, columns)
+            grad_head = grad_heads[mine, columns]
+            grad_probs = times_transpose(grad_head, values[...])
+            row_inner = jnp.sum(probs * grad_probs, axis=-1, keepdims=True)
+            grad_scores = low(probs * (grad_probs - row_inner))
+            grad_raw[mine, columns] = turned_back(matmul(grad_scores, keys[...]) * root, mine)
+            grad_keys[...] += contract_rows(grad_scores, query[mine, columns])
+            grad_values[...] += contract_rows(low(probs), grad_head)
+            return carry
+
+        lax.fori_loop(0, heads, attend_back_head, 0)
+        for s in range(BACK):
+            there = slice(s * per_batch, (s + 1) * per_batch)
+            window[s, b, :, :head_size] = low(grad_keys[there] * root)
+            window[s, b, :, head_size:] = low(grad_values[there])
+        there = slice(BACK * per_batch, (BACK + 1) * per_batch)
+        own_grad[mine, :head_size] = grad_keys[there] * root
+        own_grad[mine, head_size:] = grad_values[there]
+        for back in range(1, BACK + 1):
+            copies.send(
+                back_ids[back - 1][b],
+                window.at[BACK - back, b],
+                window_landing.at[back - 1, b],
+                place.ranked(place.rank - back),
+                place.rank >= back,
+            )
+        if b == 0:
+            wo_back.halve()
+            up_back.line.step(2)
+    wo_back.quarter()
+    for back in range(1, BACK + 1):
+        for b in range(batches):
+            mine = slice(b * per_batch, (b + 1) * per_batch)
+
+            def take(back=back, b=b, mine=mine):
+                landing = window_landing.at[back - 1, b]
+                copies.receive(back_ids[back - 1][b], landing, place.ranked(place.rank + back))
+                own_grad[mine] += wide(landing[...])
+
+            pl.when(place.rank + back < 4 * LINE)(take)
+    every = slice(0, rows)
+    grad_raw[:, query_width : query_width + head_size] = turned_back(
+        own_grad[:, :head_size], every
+    )
+    grad_raw[:, query_width + head_size :] = low(own_grad[:, head_size:])
+    first_back = RowsScatter(
+        copies,
+        place,
+        grad_gate,
+        first_core_landing,
+        first_pair_landing,
+        first_line_landing,
+        stage,
+        sem,
+    )
+    for origin in range(LINE):
+        normed = first_normed[:, origin * rows : (origin + 1) * rows]
+        first_back.fill(origin, low(contract_rows(normed, grad_raw[...])))
+    first_back.start()
+
+    first_ids = [copies.new() for _ in range(PARTS)]
+    sum_ids = [copies.new() for _ in range(5)]
+    first_at = kv_width + width
+    first_own, first_other = mail.at[pl.ds(0, rows)], pair_landing
+    first_fetch.wait()
+
+    def first_tile(t, carry):
+        block = pl.ds(pl.multiple_of(t * tile, tile), tile)
+        part = times_transpose(grad_raw[...], first_weights[block, :kv_width])
+        first_own[:, block] = low(part)
+        unit = wide(tokens[:, block]) * first_scale[...]
+        at = pl.ds(pl.multiple_of(first_at + t * tile, tile), tile)
+        totals[:, at] = eight_rows(part * unit)
+        return carry
+
+    lax.fori_loop(0, width // tile, first_tile, 0)
+    for i in range(PARTS):
+        block = pl.ds(i * size, size)
+        copies.send(first_ids[i], first_own.at[block], first_other.at[block], place.other)
+    totals[:, :kv_width] = eight_rows(wide(grad_raw[...]))
+
+    def sum_row(t, carry):
+        columns = pl.ds(pl.multiple_of(t * LANES, LANES), LANES)
+        sums[0, pl.ds(t, 1)] = jnp.sum(totals[:, columns], axis=0, keepdims=True)
+        return carry
+
+    lax.fori_loop(0, sums.shape[1], sum_row, 0)
+    shared = first_at // LANES
+
+    def sum_step(i, to):
+        copies.send(sum_ids[i], sums.at[i], sums_landing.at[i], to)
+
+    def sum_take(i, to):
+        copies.receive(sum_ids[i], sums_landing.at[i], to)
+        if i < 4:
+            sums[i + 1] = sums[i] + sums_landing[i]
+
+    sum_step(0, place.core)
+    first_back.halve()
+    sum_take(0, place.core)
+    sum_step(1, place.pair)
+    up_back.line.step(3)
+    sum_take(1, place.pair)
+    sum_step(2, place.near)
+
+    spare = mail.at[pl.ds(rows, rows)]
+    copies.receive(out_core_id, out_core_landing, place.core)
+    fetch(out_core_landing.at[pl.ds(rows, rows)], spare, sem)
+    add_to(out_sum.at[slot(1)], spare)
+    copies.send(out_pair_id, out_sum.at[slot(1)], out_pair_landing, place.pair)
+    fetch(out_core_landing.at[pl.ds(0, rows)], spare, sem)
+    add_to(out_sum.at[slot(0)], spare)
+    first_back.quarter()
+    sum_take(2, place.near)
+    sum_step(3, place.far)
+    for i in range(PARTS):
+        block = pl.ds(i * size, size)
+        copies.receive(first_ids[i], first_other.at[block], place.other)
+        unit = wide(tokens[block]) * first_scale[block]
+        back = wide(first_own[block]) + wide(first_other[block])
+        input_grad[block] += norm_back(back, unit, first_scale[block], first_gain)
+    sum_take(3, place.far)
+    sum_step(4, place.other)
+    copies.receive(out_pair_id, out_pair_landing, place.pair)
+    fetch(out_pair_landing, spare, sem)
+    add_to(out_sum.at[slot(0)], spare)
+    copies.send(out_other_id, out_sum.at[slot(0)], out_other_landing, place.other)
+    up_back.finish()
+    wo_back.line.step(2)
+    first_back.line.step(2)
+    wo_back.line.step(3)
+    first_back.line.step(3)
+    gate_back.line.step(2)
+    sum_take(4, place.other)
+    sums_out[...] = sums[4]
+    sums_out[shared:] += sums_landing[4, shared:]
+    copies.receive(out_other_id, out_other_landing, place.other)
+    fetch(out_other_landing, spare, sem)
+    spare[...] = low(state[...] + (wide(out_sum[slot(0)]) + wide(spare[...])))
+    fetch(spare, output, sem)
+    wo_back.finish(grad_w_out)
+    first_back.finish(grad_first)
+    gate_back.line.step(3)
+    gate_back.finish()
+    for scatter in scatters:
+        scatter.end()
+    copies.settle()
+
+
+def layer_call(heads, head_size, operands):
     tokens, first_shard, out_shard, gate_shard = operands[:4]
-    allowed = operands[-1]
+    own_segments = operands[10]
     rows, width = tokens.shape
-    batches = allowed.shape[0]
+    batches = own_segments.shape[0]
     per_batch = rows // batches
-    quarter = gate_shard.shape[1] // 4
+    count, padded = gate_shard.shape
+    quarter = padded // 4
     query_width = heads * head_size
+    kv_width = query_width + 2 * head_size
     low_type, wide_type = jnp.bfloat16, jnp.float32
+    in_vmem, anywhere = pl.BlockSpec(memory_space=pltpu.VMEM), pl.BlockSpec(memory_space=pl.ANY)
 
     def shape(*dims, kind=low_type):
         return jax.ShapeDtypeStruct(dims, kind)
 
-    in_vmem, anywhere = pl.BlockSpec(memory_space=pltpu.VMEM), pl.BlockSpec(memory_space=pl.ANY)
-    window_shape = (BACK + 1, batches, per_batch, 2 * head_size)
+    def vmem(*dims, kind=low_type):
+        return pltpu.VMEM(dims, kind)
+
+    sum_rows = (kv_width + 2 * width) // LANES
     outs = (
-        (shape(width, first_shard.shape[1]), anywhere),
-        (shape(width, query_width), anywhere),
-        (shape(width, quarter), anywhere),
-        (shape(width, quarter), anywhere),
-        (shape(width, quarter), anywhere),
-        (shape(4, rows, width), anywhere),
-        (shape(4, rows, width), anywhere),
-        (shape(rows, query_width), in_vmem),
-        (shape(*window_shape), in_vmem),
-        (shape(rows, query_width), in_vmem),
+        (shape(rows, width), anywhere),
         (shape(rows, width, kind=wide_type), in_vmem),
-    )
-    return pl.pallas_call(
-        functools.partial(forward_kernel, heads, head_size),
-        out_shape=[out[0] for out in outs],
-        in_specs=[in_vmem] + [anywhere] * 6 + [in_vmem] * 4,
-        out_specs=[out[1] for out in outs],
-        scratch_shapes=[
-            pltpu.VMEM((width, first_shard.shape[1]), low_type),
-            pltpu.VMEM((width, query_width), low_type),
-            pltpu.VMEM((rows, width), wide_type),
-            pltpu.VMEM(window_shape, low_type),
-            pltpu.VMEM(((BACK + 1) * per_batch, head_size), low_type),
-            pltpu.VMEM(((BACK + 1) * per_batch, head_size), low_type),
-            pltpu.VMEM((rows, width), low_type),
-            pltpu.VMEM((rows, width), low_type),
-            pltpu.VMEM((rows, width), low_type),
-            pltpu.SemaphoreType.DMA((N_REMOTE,)),
-            pltpu.SemaphoreType.DMA((N_REMOTE,)),
-            pltpu.SemaphoreType.DMA((8,)),
-        ],
+        (shape(count, kv_width, kind=wide_type), in_vmem),
+        (shape(count, query_width, kind=wide_type), in_vmem),
+        (shape(count, padded), anywhere),
+        (shape(count, padded), anywhere),
+        (shape(count, padded), anywhere),
+        (shape(sum_rows, LANES, kind=wide_type), in_vmem),
+    )
+    kept = (
+        shape(width, first_shard.shape[1]),
+        shape(3, 2, LINE - 1, 4 * count, quarter),
+        shape(2 * rows, width),
+        shape(rows, width),
+        shape(rows, width),
+        shape(2 * LINE * count, kv_width),
+        shape(LINE, count, kv_width),
+        shape(2, LINE - 1, count, kv_width),
+        shape(2 * LINE * count, query_width),
+        shape(LINE, count, query_width),
+        shape(2, LINE - 1, count, query_width),
+    )
+    scratch = (
+        vmem(width, first_shard.shape[1]),
+        vmem(width, query_width),
+        vmem(rows, width, kind=wide_type),
+        vmem(BACK + 1, batches, per_batch, 2 * head_size),
+        vmem((BACK + 1) * per_batch, head_size),
+        vmem((BACK + 1) * per_batch, head_size),
+        vmem(2 * rows, width),
+        vmem(rows, width),
+        vmem(rows, query_width),
+        vmem(rows, query_width),
+        vmem(width, quarter),
+        vmem(width, quarter),
+        vmem(width, quarter),
+        vmem(4 * rows, width),
+        vmem(4 * rows, width),
+        vmem(4 * rows, quarter),
+        vmem(4 * rows, quarter),
+        vmem(4 * rows, quarter),
+        vmem(rows, width),
+        vmem(rows, width),
+        vmem(4 * count, quarter),
+        vmem((BACK + 1) * per_batch, head_size, kind=wide_type),
+        vmem((BACK + 1) * per_batch, head_size, kind=wide_type),
+        vmem(rows, 2 * head_size, kind=wide_type),
+        vmem(BACK, batches, per_batch, 2 * head_size),
+        vmem(rows, 1, kind=wide_type),
+        vmem(rows, 1, kind=wide_type),
+        vmem(8, sum_rows * LANES, kind=wide_type),
+        vmem(6, sum_rows, LANES, kind=wide_type),
+        vmem(5, sum_rows, LANES, kind=wide_type),
+        pltpu.SemaphoreType.DMA((N_REMOTE,)),
+        pltpu.SemaphoreType.DMA((N_REMOTE,)),
+        pltpu.SemaphoreType.DMA((8,)),
+    )
+    results = pl.pallas_call(
+        functools.partial(layer_kernel, heads, head_size),
+        out_shape=[out[0] for out in outs] + list(kept),
+        in_specs=[in_vmem] + [anywhere] * 6 + [in_vmem] * 7,
+        out_specs=[out[1] for out in outs] + [anywhere] * len(kept),
+        scratch_shapes=scratch,
         compiler_params=pltpu.CompilerParams(
             collective_id=0, has_side_effects=True, vmem_limit_bytes=VMEM_BYTES
         ),
     )(*operands)
+    return results[: len(outs)]
 
 
 def body(
@@ -817,23 +1383,26 @@
     )
     own_places = lax.dynamic_slice_in_dim(positions, row_start, count_rows, axis=1)
     cosine, sine_table = rotation(own_places.reshape(-1), head_size)
-    allowed = [
-        visible(segments[b], positions[b], row_start, count_rows) for b in range(batches)
-    ]
     if lax.axis_size(RING) == LINE:
+        key_segments, key_positions = [], []
+        for b in range(batches):
+            padding = jnp.full((BACK * count_rows,), -1, jnp.int32)
+            for rows_of, padded_rows in ((key_segments, segments), (key_positions, positions)):
+                padded_rows = jnp.concatenate([padding, padded_rows[b]])
+                rows_of.append(
+                    lax.dynamic_slice_in_dim(padded_rows, row_start, (BACK + 1) * count_rows)
+                )
+        own_segments = lax.dynamic_slice_in_dim(segments, row_start, count_rows, axis=1)
         (
-            first_all,
-            w_out,
-            w_gate,
-            w_up,
-            w_down,
-            grad_out_four,
-            second_normed,
-            query_rows,
-            window,
-            heads_out,
-            residual,
-        ) = forward_call(
+            output,
+            input_grad,
+            grad_w_qkv,
+            grad_w_out,
+            grad_w_down,
+            grad_w_gate,
+            grad_w_up,
+            sums,
+        ) = layer_call(
             heads,
             head_size,
             (
@@ -847,21 +1416,18 @@
                 wide(biases).reshape(1, -1),
                 cosine[:, 0],
                 sine_table[:, 0],
-                jnp.stack(allowed).astype(jnp.float32),
+                own_segments[..., None],
+                own_places[..., None],
+                jnp.stack(key_segments)[:, None],
+                jnp.stack(key_positions)[:, None],
             ),
         )
-        grad_out_four = grad_out_four.reshape(-1, width)
-        second_normed = second_normed.reshape(-1, width)
-        query_rows = query_rows.reshape(batches, count_rows, heads, head_size)
-        window = window.transpose(1, 0, 2, 3).reshape(batches, -1, 2 * head_size)
-        w_qkv = first_all[:, :kv_width]
-        first_gain = wide(first_all[:, kv_width])
-        second_gain = wide(first_all[:, kv_width + 1])
-        first_unit, first_scale = root_mean_square_parts(inputs)
-        first_normed = low(first_unit * first_gain)
-        key_rows, value_rows = window[..., :head_size], window[..., head_size:]
-        log_totals = [log_total_of(query_rows[b], key_rows[b], allowed[b]) for b in range(batches)]
+        sums = sums.reshape(-1)
+        grad_w_down, grad_w_gate, grad_w_up = map(wide, (grad_w_down, grad_w_gate, grad_w_up))
     else:
+        allowed = [
+            visible(segments[b], positions[b], row_start, count_rows) for b in range(batches)
+        ]
         first_all = gather_rows(first_shard)
         w_qkv = first_all[:, :kv_width]
         first_gain = wide(first_all[:, kv_width])
@@ -898,54 +1464,54 @@
         second_unit, second_scale = root_mean_square_parts(residual)
         second_normed = four_blocks(low(second_unit * second_gain))
 
-    second_unit, second_scale = root_mean_square_parts(residual)
-    gate_value = matmul(second_normed, w_gate)
-    up_part = matmul(second_normed, w_up)
-    sigmoid_gate = jax.nn.sigmoid(gate_value)
-    silu_gate = gate_value * sigmoid_gate
-    hidden = low(silu_gate * up_part)
-    grad_hidden = matmul(grad_out_four, w_down)
-    grad_gate = low(
-        grad_hidden * up_part * sigmoid_gate * (1.0 + gate_value * (1.0 - sigmoid_gate))
-    )
-    grad_up = low(grad_hidden * silu_gate)
-    second_back = four_sums(times_transpose(grad_gate, w_gate) + times_transpose(grad_up, w_up))
-    grad_w_down = quarter_to_owner(low(contract_rows(grad_out_four, hidden)))
-    grad_w_gate = quarter_to_owner(low(contract_rows(second_normed, grad_gate)))
-    grad_w_up = quarter_to_owner(low(contract_rows(second_normed, grad_up)))
-    output = low(residual + four_sums(times_transpose(hidden, w_down)))
-
-    second_gain_sum = jnp.sum(second_back * second_unit, axis=0)
-    grad_state = wide(grad_out) + norm_back(second_back, second_unit, second_scale, second_gain)
-    grad_branch = low(grad_state)
-    grad_w_out = scatter_rows(contract_rows(grad_branch, heads_out))
-    grad_heads = low(matmul(grad_branch, w_out)).reshape(query_rows.shape)
-    backs = [
-        attend_back(
-            grad_heads[b], query_rows[b], key_rows[b], value_rows[b], allowed[b], log_totals[b]
-        )
-        for b in range(batches)
-    ]
-    grad_query = jnp.stack([back[0] for back in backs]).reshape(rows, heads, head_size)
-    grad_window = jnp.stack([jnp.concatenate([back[1], back[2]], axis=1) for back in backs])
-    own_grad = grad_window[:, BACK * count_rows :]
-    for back in range(1, BACK + 1):
-        first_row = (BACK - back) * count_rows
-        own_grad = own_grad + wide(
-            shifted(low(grad_window[:, first_row : first_row + count_rows]), -back)
-        )
-    own_grad = own_grad.reshape(rows, 2, head_size)
-    turned_back = rotate_back(
-        jnp.concatenate([grad_query, own_grad[:, :1]], axis=1), cosine, sine_table
-    )
-    grad_raw = low(jnp.concatenate([turned_back, own_grad[:, 1:]], axis=1).reshape(rows, -1))
-    grad_w_qkv = scatter_rows(contract_rows(first_normed, grad_raw))
-    bias_sum = jnp.sum(wide(grad_raw), axis=0)
-    first_back_part = times_transpose(grad_raw, w_qkv)
-    first_back = tensor_total(first_back_part)
-    first_gain_sum = jnp.sum(first_back * first_unit, axis=0)
-    input_grad = grad_state + norm_back(first_back, first_unit, first_scale, first_gain)
-    sums = summed_over_fsdp(jnp.concatenate([bias_sum, second_gain_sum, first_gain_sum]))
+        second_unit, second_scale = root_mean_square_parts(residual)
+        gate_value = matmul(second_normed, w_gate)
+        up_part = matmul(second_normed, w_up)
+        sigmoid_gate = jax.nn.sigmoid(gate_value)
+        silu_gate = gate_value * sigmoid_gate
+        hidden = low(silu_gate * up_part)
+        grad_hidden = matmul(grad_out_four, w_down)
+        grad_gate = low(
+            grad_hidden * up_part * sigmoid_gate * (1.0 + gate_value * (1.0 - sigmoid_gate))
+        )
+        grad_up = low(grad_hidden * silu_gate)
+        second_back = four_sums(times_transpose(grad_gate, w_gate) + times_transpose(grad_up, w_up))
+        grad_w_down = quarter_to_owner(low(contract_rows(grad_out_four, hidden)))
+        grad_w_gate = quarter_to_owner(low(contract_rows(second_normed, grad_gate)))
+        grad_w_up = quarter_to_owner(low(contract_rows(second_normed, grad_up)))
+        output = low(residual + four_sums(times_transpose(hidden, w_down)))
+
+        second_gain_sum = jnp.sum(second_back * second_unit, axis=0)
+        grad_state = wide(grad_out) + norm_back(second_back, second_unit, second_scale, second_gain)
+        grad_branch = low(grad_state)
+        grad_w_out = scatter_rows(contract_rows(grad_branch, heads_out))
+        grad_heads = low(matmul(grad_branch, w_out)).reshape(query_rows.shape)
+        backs = [
+            attend_back(
+                grad_heads[b], query_rows[b], key_rows[b], value_rows[b], allowed[b], log_totals[b]
+            )
+            for b in range(batches)
+        ]
+        grad_query = jnp.stack([back[0] for back in backs]).reshape(rows, heads, head_size)
+        grad_window = jnp.stack([jnp.concatenate([back[1], back[2]], axis=1) for back in backs])
+        own_grad = grad_window[:, BACK * count_rows :]
+        for back in range(1, BACK + 1):
+            first_row = (BACK - back) * count_rows
+            own_grad = own_grad + wide(
+                shifted(low(grad_window[:, first_row : first_row + count_rows]), -back)
+            )
+        own_grad = own_grad.reshape(rows, 2, head_size)
+        turned_back = rotate_back(
+            jnp.concatenate([grad_query, own_grad[:, :1]], axis=1), cosine, sine_table
+        )
+        grad_raw = low(jnp.concatenate([turned_back, own_grad[:, 1:]], axis=1).reshape(rows, -1))
+        grad_w_qkv = scatter_rows(contract_rows(first_normed, grad_raw))
+        bias_sum = jnp.sum(wide(grad_raw), axis=0)
+        first_back_part = times_transpose(grad_raw, w_qkv)
+        first_back = tensor_total(first_back_part)
+        first_gain_sum = jnp.sum(first_back * first_unit, axis=0)
+        input_grad = grad_state + norm_back(first_back, first_unit, first_scale, first_gain)
+        sums = summed_over_fsdp(jnp.concatenate([bias_sum, second_gain_sum, first_gain_sum]))
     bias_total = sums[:kv_width]
     gain_rows = norm1_gain.shape[0]
     second_total = lax.dynamic_slice_in_dim(sums, kv_width + place * gain_rows, gain_rows)

time: 684 us -> 570 us (0.83)
  Pallas kernels: 235 us -> 537 us
  waiting for transfers between devices: 163 us -> 0 us
  matrix products: 111 us -> 0 us
  starting transfers between devices: 59.2 us -> 0 us
  other arithmetic: 59.6 us -> 8.93 us
  local copies, waits for them, and re-layouts: 35.2 us -> 17.3 us
  between operations: 15.5 us -> 1.26 us
    pallas_call x1, Pallas kernels: 235 us -> 537 us  [layer_call(): pl.pallas_call(functools.partial(layer_kernel, heads, head_size), out_sha...]
    ppermute x38 -> x0, waiting for transfers between devices: 163 us -> none  [the longest x17 97.1 us: swapped(): return lax.ppermute(value, axis, SWAP)]
    dot_general x23 -> x0, matrix products: 111 us -> none  [the longest x4 33.7 us: times_transpose(): lax.dot_general(left_side, right_side, (((1,), (1,)), ((), ())), preferre...]
    ppermute x38 -> x0, starting transfers between devices: 59.1 us -> none  [the longest x6 27.4 us: line_scatter(): right = lax.ppermute(to_right, RING, [(i, i + 1) for i in range(step)])]
    add x13 -> x0, other arithmetic: 20.6 us -> none  [the longest x2 9.55 us: four_sums(): total = total[:half] + wide(swapped(low(total[half:]), CORE))]
    convert_element_type x17 -> x0, other arithmetic: 13.3 us -> none  [the longest x15 11.2 us: low(): return value.astype(jnp.bfloat16)]
    reduce_sum x7 -> x0, other arithmetic: 10.5 us -> none  [the longest x1 4.14 us: body(): second_gain_sum = jnp.sum(second_back * second_unit, axis=0)]
    unnamed x153 -> x38, local copies, waits for them, and re-layouts: 10.3 us -> 3.4 us
  transfers between devices with their start and end apart: 41 -> 0, of which waited for: 17 -> 0; matrix products, arithmetic and copies ran while one was open for 21% -> 0% of each run, Pallas kernels for 0% -> 0%
where the time goes in v3:
time: 570 us; the launch traced here: 565 us
  Pallas kernels  537 us (94%)
  local copies, waits for them, and re-layouts  17.3 us (3%)
  other arithmetic  8.93 us (2%)
    pallas_call x1, Pallas kernels, layer_call(): pl.pallas_call(functools.partial(layer_kernel, heads, head_size), out_sha...  537 us

profile of v3, /device:TPU:0, one launch (start us, length us, event | category | flops | bytes accessed | tf_op | source)
XLA Modules:
  0.0 564.8 jit_solution(14654841898052665630)
XLA Ops:
  0.6 0.0 copy-start.2
  0.7 0.9 fusion.4
  1.5 0.1 pad_dynamic-slice_fusion.2
  1.6 0.6 broadcast_in_dim.16.key_segments
  2.2 0.8 fusion.3
  3.1 0.1 pad_dynamic-slice_fusion
  3.2 0.6 broadcast_in_dim.17.key_positions
  3.8 0.8 dynamic-slice_bitcast_fusion.1
  4.6 0.1 convert_element_type.31
  4.7 0.8 multiply_sine_fusion
  5.4 0.9 pad_maximum_fusion
  6.4 0.8 copy.38.own_positions
  7.2 0.8 dynamic-slice_bitcast_fusion
  8.0 0.8 copy.37.own_segments
  8.8 0.0 copy-done.2
  8.8 1.0 pad.19.gate_shard
  9.8 0.0 copy-done.3
  9.8 0.0 copy-start.10
  9.8 0.0 copy-start.11
  9.8 0.0 copy-start.12
  9.8 0.0 copy-start.13
  9.8 0.0 copy-start.14
  9.8 1.0 pad.20.up_shard
  10.8 0.0 copy-done.4
  10.8 1.0 pad.21.down_shard
  11.8 0.0 copy-done.15
  11.8 0.0 copy-done.16
  11.8 0.1 copy.36
  11.9 0.0 copy-done.9
  11.9 0.7 fusion.1.first_shard
  12.7 0.6 maximum_convert_fusion.biases
  13.3 537.3 %shard_map.263 = (bf16[384,1536]{1,0:T(8,128)(2,1)}, f32[384,1536]{1,0:T(8,128)}, f32[96,1024]{1,0:T(8,128)}, f32[96,768]{1,0:T(8,128)}, bf16[96,4608]{1,0:T(8,1...) custom-call(bf16[384,1536]{1,0:T(8,128)(2,1)} %bitcast.26, ...), custom_call_target="tpu_custom_call" | custom-call | tf_op jit(solution)/shard_map/pallas_call | solution.py:1331
  550.6 0.0 copy-start.6
  550.6 2.5 convert_bitcast_fusion
  553.1 1.3 slice_convert_fusion
  554.4 0.2 copy-done.5
  554.6 1.3 slice_convert_fusion.1
  555.9 0.0 copy-done.7
  555.9 0.7 slice.58
  556.7 0.6 fusion.2
  557.3 1.4 fusion.5
  558.7 1.3 slice.59
  559.9 1.3 fusion.6
  561.2 0.0 copy-done.1
  561.2 1.0 copy.45
  562.2 1.4 copy.46
  563.6 0.0 copy-done.8
  563.6 0.7 copy.47
  (26 shorter events, 0.1 us)
Async XLA Ops:
  0.6 8.1 %copy-start.2 = (bf16[96,4480]{1,0:T(8,128)(2,1)S(1)}, bf16[96,4480]{1,0:T(8,128)(2,1)}, u32[]{:S(2)}) copy-start(bf16[96,4480]{1,0:T(8,128)(2,1)} %param.26) | copy-start | bytes 2580484
  3.2 6.6 %copy-start.3 = (bf16[96,4480]{1,0:T(8,128)(2,1)S(1)}, bf16[96,4480]{1,0:T(8,128)(2,1)}, u32[]{:S(2)}) copy-start(bf16[96,4480]{1,0:T(8,128)(2,1)} %param.27) | copy-start | bytes 2580484
  8.8 2.0 copy-start.4
  9.8 2.0 copy-start.15
  9.8 2.0 copy-start.16
  9.8 2.2 copy-start.9
  9.8 2.2 copy-start.10
  9.8 2.2 copy-start.11
  9.8 2.9 copy-start.12
  9.8 2.9 copy-start.13
  9.8 2.8 copy-start.14
  550.6 2.6 copy-start.6
  553.1 1.5 copy-start.5
  554.4 1.5 copy-start.7
  554.4 6.8 %copy-start.1 = (bf16[384,1536]{1,0:T(8,128)(2,1)S(1)}, bf16[384,1536]{1,0:T(8,128)(2,1)}, u32[]{:S(2)}) copy-start(bf16[384,1536]{1,0:T(8,128)(2,1)} %get-tuple-element.22) | copy-start | bytes 3538948
  555.9 6.3 %copy-start = (f32[384,1536]{1,0:T(8,128)S(1)}, f32[384,1536]{1,0:T(8,128)}, u32[]{:S(2)}) copy-start(f32[384,1536]{1,0:T(8,128)} %get-tuple-element.23) | copy-start | bytes 7077892
  562.2 1.4 copy-start.8
